TPU v7x, 256 devices: a whole 4x4x8 slice. The times are simulated.
256 devices in a mesh: outer: 16 (over x, y), inner: 16 (over z, core).
Axes of the slice: x: 4, y: 4, z: 8, core: 2. Of those that a mesh axis runs over, the one named last changes fastest.
Arguments:
- queries: bfloat16 [32768, 1024], P(('outer', 'inner')), may hold values from -6 to 6
- keys: bfloat16 [32768, 1024], P(('outer', 'inner')), may hold values from -6 to 6
- values: bfloat16 [32768, 1024], P(('outer', 'inner')), may hold values from -6 to 6
- saved_out: bfloat16 [32768, 1024], P(('outer', 'inner')), may hold values from -6 to 6
- out_grad: bfloat16 [32768, 1024], P(('outer', 'inner')), may hold values from -6 to 6
- offsets: int32 [16], replicated, may hold values from 0 to 15
Outputs:
- queries_grad: bfloat16 [32768, 1024], P(('outer', 'inner'))
- keys_grad: bfloat16 [32768, 1024], P(('outer', 'inner'))
- values_grad: bfloat16 [32768, 1024], P(('outer', 'inner'))
All inputs are finite; a program needn't handle non-finite values.
Results may differ from a plain program's by a relative error of at most 0.007.
Values may be sent and summed in bfloat16 or wider, within the bound.
No kernel may reach another device: no remote copies, remote signals or barrier semaphores. Data moves between devices by JAX's collectives and lax.ppermute only.
A program may use at most 128 MiB of HBM per device.

v0:
```python
import jax
import jax.numpy as jnp
from jax import lax
from jax.sharding import PartitionSpec as P

HEADS = 16
HD = 64
BLOCK = 128


def pick_rows(array, offset, groups):
    shaped = array.reshape((-1, groups, BLOCK) + array.shape[1:])
    chosen = lax.dynamic_index_in_dim(shaped, offset, 1, keepdims=False)
    return chosen.reshape((-1,) + array.shape[1:])


def place_rows(rows_in, offset, groups):
    shaped = rows_in.reshape((-1, 1, BLOCK) + rows_in.shape[1:])
    select = (jnp.arange(groups) == offset).reshape((1, groups, 1) + (1,) * (rows_in.ndim - 1))
    placed = jnp.where(select, shaped, jnp.zeros((), rows_in.dtype))
    return placed.reshape((-1,) + rows_in.shape[1:])


def on_device(queries, keys, values, saved_out, out_grad, offsets):
    groups = lax.axis_size("outer")
    inner_count = lax.axis_size("inner")
    local_count = HEADS // inner_count
    scale = HD ** (-0.5)
    seg_q, seg_k, seg_v, seg_o, seg_g = (
        lax.all_to_all(queries, "inner", split_axis=1, concat_axis=0, tiled=True),
        lax.all_to_all(keys, "inner", split_axis=1, concat_axis=0, tiled=True),
        lax.all_to_all(values, "inner", split_axis=1, concat_axis=0, tiled=True),
        lax.all_to_all(saved_out, "inner", split_axis=1, concat_axis=0, tiled=True),
        lax.all_to_all(out_grad, "inner", split_axis=1, concat_axis=0, tiled=True),
    )
    products = seg_g.astype(jnp.float32) * seg_o.astype(jnp.float32)
    row_terms = jnp.sum(products.reshape(products.shape[0], local_count, HD), axis=2)
    seg_rows = seg_q.shape[0]
    first_head = lax.axis_index("inner") * local_count
    head_offsets = lax.dynamic_slice_in_dim(offsets, first_head, local_count)
    picked_keys = pick_rows(seg_k, head_offsets[0], groups)
    picked_values = pick_rows(seg_v, head_offsets[0], groups)
    far_keys, far_values = (
        lax.all_gather(picked_keys, "outer", axis=0, tiled=True),
        lax.all_gather(picked_values, "outer", axis=0, tiled=True),
    )
    block_ids = jnp.arange(seg_rows) // BLOCK % groups
    query_list, key_near_list, value_near_list = ([], [], [])
    key_far_list, value_far_list = ([], [])
    local_head = 0
    offset = head_offsets[local_head]
    flags = block_ids == offset
    head_term = row_terms[:, local_head]
    picked_q = pick_rows(seg_q, offset, groups)
    picked_g = pick_rows(seg_g, offset, groups)
    picked_term = pick_rows(head_term, offset, groups)
    near = jnp.dot(seg_q, seg_k.T, preferred_element_type=jnp.float32) * scale
    far = jnp.dot(picked_q, far_keys.T, preferred_element_type=jnp.float32) * scale
    top_near = jnp.max(near, axis=1)
    top = jnp.where(
        flags, jnp.maximum(top_near, place_rows(jnp.max(far, axis=1), offset, groups)), top_near
    )
    near_sum = jnp.sum(jnp.exp(near - top[:, None]), axis=1)
    picked_top = pick_rows(top, offset, groups)
    far_sum = jnp.sum(jnp.exp(far - picked_top[:, None]), axis=1)
    lse = top + jnp.log(near_sum + place_rows(far_sum, offset, groups))
    picked_lse = pick_rows(lse, offset, groups)
    prob_near = jnp.exp(near - lse[:, None])
    prob_far = jnp.exp(far - picked_lse[:, None])
    dprob_near = jnp.dot(seg_g, seg_v.T, preferred_element_type=jnp.float32)
    dprob_far = jnp.dot(picked_g, far_values.T, preferred_element_type=jnp.float32)
    dscore_near = (prob_near * (dprob_near - head_term[:, None])).astype(jnp.bfloat16)
    dscore_far = (prob_far * (dprob_far - picked_term[:, None])).astype(jnp.bfloat16)
    far_part = jnp.dot(dscore_far, far_keys, preferred_element_type=jnp.float32)
    query_grad = (
        jnp.dot(dscore_near, seg_k, preferred_element_type=jnp.float32)
        + place_rows(far_part, offset, groups)
    ) * scale
    query_list.append(query_grad)
    key_near_list.append(jnp.dot(dscore_near.T, seg_q, preferred_element_type=jnp.float32) * scale)
    value_near_list.append(
        jnp.dot(prob_near.astype(jnp.bfloat16).T, seg_g, preferred_element_type=jnp.float32)
    )
    key_far_list.append(jnp.dot(dscore_far.T, picked_q, preferred_element_type=jnp.float32) * scale)
    value_far_list.append(
        jnp.dot(prob_far.astype(jnp.bfloat16).T, picked_g, preferred_element_type=jnp.float32)
    )
    own_keys, own_values = (
        lax.psum_scatter(
            key_far_list[0].astype(jnp.bfloat16), "outer", scatter_dimension=0, tiled=True
        ).astype(jnp.float32),
        lax.psum_scatter(
            value_far_list[0].astype(jnp.bfloat16), "outer", scatter_dimension=0, tiled=True
        ).astype(jnp.float32),
    )
    own_key_list = [own_keys]
    own_value_list = [own_values]
    key_grads, value_grads = ([], [])
    local_head = 0
    offset = head_offsets[local_head]
    key_grads.append(
        (key_near_list[local_head] + place_rows(own_key_list[local_head], offset, groups)).astype(
            jnp.bfloat16
        )
    )
    value_grads.append(
        (
            value_near_list[local_head] + place_rows(own_value_list[local_head], offset, groups)
        ).astype(jnp.bfloat16)
    )
    query_block = jnp.concatenate([grad.astype(jnp.bfloat16) for grad in query_list], axis=1)
    key_block = key_grads[0]
    value_block = value_grads[0]
    queries_grad, keys_grad, values_grad = (
        lax.all_to_all(query_block, "inner", split_axis=0, concat_axis=1, tiled=True),
        lax.all_to_all(key_block, "inner", split_axis=0, concat_axis=1, tiled=True),
        lax.all_to_all(value_block, "inner", split_axis=0, concat_axis=1, tiled=True),
    )
    return (queries_grad, keys_grad, values_grad)


def solution(mesh):
    return jax.shard_map(
        on_device,
        mesh=mesh,
        in_specs=(
            P(("outer", "inner"), None),
            P(("outer", "inner"), None),
            P(("outer", "inner"), None),
            P(("outer", "inner"), None),
            P(("outer", "inner"), None),
            P(),
        ),
        out_specs=(
            P(("outer", "inner"), None),
            P(("outer", "inner"), None),
            P(("outer", "inner"), None),
        ),
        check_vma=False,
    )
```

profile of v0, /device:TPU:1, one launch (start us, length us, event | category | flops | bytes accessed | tf_op | source)
XLA Modules:
  0.0 334.9 jit_solution(13747821435145924800)
XLA Ops:
  7.2 1.8 copy.31
  9.0 10.0 %all-to-all-start.1 = ((bf16[128,16,64]{0,2,1:T(8,128)(2,1)}), bf16[128,16,64]{0,2,1:T(8,128)(2,1)S(1)}, u32[]{:S(2)}, u32[]{:S(2)}) async-start(bf16[128,16,64]{0,2,1:T(8,128)(2,1)} %bitcast.2), calls=%async_computation.1 | async-start | bytes 524288 | tf_op jit(solution)/shard_map/all_to_all | solution.py:31
  18.9 1.8 copy.35
  20.7 9.9 %all-to-all-done.1 = bf16[128,16,64]{0,2,1:T(8,128)(2,1)S(1)} async-done(((bf16[128,16,64]{0,2,1:T(8,128)(2,1)}), bf16[128,16,64]{0,2,1:T(8,128)(2,1)S(1)}, u32[]{:S(2)}, u32[]{:S(2)}) %all-to-all-start.1) | async-done | bytes 262176 | tf_op jit(solution)/shard_map/all_to_all | solution.py:31
  30.6 3.4 %all-to-all-start.3 = ((bf16[128,16,64]{0,2,1:T(8,128)(2,1)}), bf16[128,16,64]{0,2,1:T(8,128)(2,1)S(1)}, u32[]{:S(2)}, u32[]{:S(2)}) async-start(bf16[128,16,64]{0,2,1:T(8,128)(2,1)} %bitcast.14), calls=%async_computation.3 | async-start | bytes 524288 | tf_op jit(solution)/shard_map/all_to_all | solution.py:32
  34.1 1.3 dynamic_slice.16
  36.6 1.8 copy.29
  38.4 1.8 copy.37
  40.2 1.8 copy.33
  42.6 0.6 iota_compare_fusion
  43.2 0.7 dynamic-slice.24
  43.8 1.4 all-to-all-done.3
  45.2 5.4 %all-to-all-start = ((bf16[128,16,64]{0,2,1:T(8,128)(2,1)}), bf16[128,16,64]{0,2,1:T(8,128)(2,1)S(1)}, u32[]{:S(2)}, u32[]{:S(2)}) async-start(bf16[128,16,64]{0,2,1:T(8,128)(2,1)} %bitcast), calls=%async_computation | async-start | bytes 524288 | tf_op jit(solution)/shard_map/all_to_all | solution.py:30
  50.6 19.7 %all-gather = bf16[2048,1,64]{0,2,1:T(8,128)(2,1)S(1)} all-gather(bf16[128,1,64]{0,2,1:T(8,128)(2,1)S(1)} %constant_dynamic-slice_fusion.4), channel_id=2, replica_groups=mesh['outer'=16,'inner'=16] {'outer'}, dimensions={0}, use_global_device_ids=true | all-gather | bytes 278528 | tf_op jit(solution)/shard_map/all_gather | solution.py:44
  70.4 11.8 %all-to-all-start.4 = ((bf16[128,16,64]{0,2,1:T(8,128)(2,1)}), bf16[128,16,64]{0,2,1:T(8,128)(2,1)S(1)}, u32[]{:S(2)}, u32[]{:S(2)}) async-start(bf16[128,16,64]{0,2,1:T(8,128)(2,1)} %bitcast.16), calls=%async_computation.4 | async-start | bytes 524288 | tf_op jit(solution)/shard_map/all_to_all | solution.py:33
  82.2 0.4 fusion.76
  82.6 8.1 %multiply_reduce_fusion = (f32[2048]{0:T(1024)S(1)}, f32[2048,2048]{0,1:T(8,128)}) fusion(bf16[128,16,64]{0,2,1:T(8,128)(2,1)S(1)} %all-to-all-done.1, bf16[128,16,64]{0,2,1:T(8,128)(2,1)S(1)} %all-to-all-done), kind=kOutput, calls=%fused_computation.4 | convolution fusion | flops 545257472 | bytes 17309696 | tf_op jit(solution)/shard_map/dot_general | solution.py:57
  90.7 3.2 all-to-all-done.4
  93.9 4.0 %all-to-all-start.2 = ((bf16[128,16,64]{0,2,1:T(8,128)(2,1)}), bf16[128,16,64]{0,2,1:T(8,128)(2,1)S(1)}, u32[]{:S(2)}, u32[]{:S(2)}) async-start(bf16[128,16,64]{0,2,1:T(8,128)(2,1)} %bitcast.12), calls=%async_computation.2 | async-start | bytes 524288 | tf_op jit(solution)/shard_map/all_to_all | solution.py:34
  98.0 19.2 %all-gather.1 = bf16[2048,1,64]{0,2,1:T(8,128)(2,1)S(1)} all-gather(bf16[128,1,64]{0,2,1:T(8,128)(2,1)S(1)} %constant_dynamic-slice_fusion.1), channel_id=3, replica_groups=mesh['outer'=16,'inner'=16] {'outer'}, dimensions={0}, use_global_device_ids=true | all-gather | bytes 278528 | tf_op jit(solution)/shard_map/all_gather | solution.py:45
  117.2 0.7 maximum_select_fusion.1
  117.9 0.7 maximum_select_fusion
  119.0 8.6 %exponential_reduce_fusion = f32[2048]{0:T(1024)S(1)} fusion(f32[2048,2048]{0,1:T(8,128)} %get-tuple-element.10, f32[2048]{0:T(1024)S(1)} %maximum_select_fusion.1), kind=kLoop, calls=%fused_computation.2 | loop fusion | flops 12580864 | bytes 16793600 | tf_op jit(solution)/shard_map/reduce_sum | solution.py:63
  127.6 0.7 fusion.73
  129.3 1.1 copy.46
  130.3 0.4 convolution_convert_fusion
  130.7 1.0 copy.48
  131.8 7.9 %multiply_convert_fusion = bf16[2048,2048]{0,1:T(8,128)(2,1)S(1)} fusion(f32[2048,2048]{0,1:T(8,128)} %get-tuple-element.10, f32[2048]{0:T(1024)S(1)} %bitcast.168, f32[2048]{0:T(1024)S(1)} %fusion.54, bf16[128,16,64]{0,2,1:T(8,128)(2,1)S(1)} %all-to-all-done.3, bf16[128,16,64]{0,2,1:T(8,128)(2,1)S(1)} %all-to-all-done.2), kind=kOutput, calls=%fused_computation | convolution fusion | flops 557842432 | bytes 25706496 | tf_op jit(solution)/shard_map/dot_general | solution.py:70
  139.7 3.2 copy-done
  142.9 1.7 fusion.16
  144.6 0.8 copy.100
  145.4 11.4 %all-to-all-start.5 = ((bf16[16,128,64]{1,2,0:T(8,128)(2,1)}), bf16[16,128,64]{1,2,0:T(8,128)(2,1)S(1)}, u32[]{:S(2)}, u32[]{:S(2)}) async-start(bf16[16,128,64]{1,2,0:T(8,128)(2,1)} %bitcast.161), calls=%async_computation.5 | async-start | bytes 524288 | tf_op jit(solution)/shard_map/all_to_all | solution.py:115
  156.8 0.7 reduce-scatter.7.cloned.1.call-update
  157.5 52.6 %reduce-scatter.9.cloned.1.call-done = bf16[128,64]{1,0:T(8,128)(2,1)} async-done(((bf16[2048,64]{1,0:T(8,128)(2,1)}), bf16[128,64]{1,0:T(8,128)(2,1)}) %reduce-scatter.9.cloned.1.call-update) | async-done | bytes 16400
  210.1 0.8 copy.49
  211.0 7.6 %fusion.18 = bf16[8,16,8,128]{3,2,1,0:T(8,128)(2,1)S(1)} fusion(f32[2048,2048]{0,1:T(8,128)} %get-tuple-element.10, f32[2048]{0:T(1024)S(1)} %fusion.54, f32[8,8,16,128]{3,2,1,0:T(8,128)S(1)} %bitcast.162, pred[2048]{0:T(1024)(128)(4,1)S(1)} %broadcast_bitcast_fusion, bf16[128,16,64]{0,2,1:T(8,128)(2,1)S(1)} %all-to-all-done.2), kind=kOutput, calls=%fused_computation.23 | convolution fusion | flops 549847040 | bytes 17836032 | tf_op jit(solution)/shard_map/dot_general | solution.py:82
  218.6 0.8 copy.98
  219.4 71.4 %reduce-scatter.7.cloned.1.call-done = bf16[128,64]{1,0:T(8,128)(2,1)} async-done(((bf16[2048,64]{1,0:T(8,128)(2,1)}), bf16[128,64]{1,0:T(8,128)(2,1)}) %reduce-scatter.7.cloned.1.call-update) | async-done | bytes 16400
  290.8 0.8 copy.47
  291.6 9.3 %all-to-all-start.7 = ((bf16[16,128,64]{1,2,0:T(8,128)(2,1)}), bf16[16,128,64]{1,2,0:T(8,128)(2,1)S(1)}, u32[]{:S(2)}, u32[]{:S(2)}) async-start(bf16[16,128,64]{1,2,0:T(8,128)(2,1)} %bitcast.159), calls=%async_computation.7 | async-start | bytes 524288 | tf_op jit(solution)/shard_map/all_to_all | solution.py:117
  301.0 6.1 %fusion.17 = bf16[8,16,8,128]{3,2,1,0:T(8,128)(2,1)S(1)} fusion(bf16[2048,2048]{0,1:T(8,128)(2,1)} %copy-done, f32[8,8,16,128]{3,2,1,0:T(8,128)S(1)} %bitcast.163, pred[2048]{0:T(1024)(128)(4,1)S(1)} %broadcast_bitcast_fusion, bf16[128,16,64]{0,2,1:T(8,128)(2,1)S(1)} %all-to-all-done), kind=kOutput, calls=%fused_computation.22 | convolution fusion | flops 537395200 | bytes 9439232 | tf_op jit(solution)/shard_map/dot_general | solution.py:80
  307.0 0.8 copy.99
  307.8 4.8 %all-to-all-done.7 = bf16[16,128,64]{1,2,0:T(8,128)(2,1)S(1)} async-done(((bf16[16,128,64]{1,2,0:T(8,128)(2,1)}), bf16[16,128,64]{1,2,0:T(8,128)(2,1)S(1)}, u32[]{:S(2)}, u32[]{:S(2)}) %all-to-all-start.7) | async-done | bytes 262176 | tf_op jit(solution)/shard_map/all_to_all | solution.py:117
  312.6 3.4 %all-to-all-start.6 = ((bf16[16,128,64]{1,2,0:T(8,128)(2,1)}), bf16[16,128,64]{1,2,0:T(8,128)(2,1)S(1)}, u32[]{:S(2)}, u32[]{:S(2)}) async-start(bf16[16,128,64]{1,2,0:T(8,128)(2,1)} %bitcast.160), calls=%async_computation.6 | async-start | bytes 524288 | tf_op jit(solution)/shard_map/all_to_all | solution.py:116
  316.1 0.9 copy.42
  316.9 0.8 copy.44
  317.8 9.4 %all-to-all-done.6 = bf16[16,128,64]{1,2,0:T(8,128)(2,1)S(1)} async-done(((bf16[16,128,64]{1,2,0:T(8,128)(2,1)}), bf16[16,128,64]{1,2,0:T(8,128)(2,1)S(1)}, u32[]{:S(2)}, u32[]{:S(2)}) %all-to-all-start.6) | async-done | bytes 262176 | tf_op jit(solution)/shard_map/all_to_all | solution.py:116
  327.2 0.8 copy.43
  (21 shorter events, 1.7 us)
Async XLA Ops:
  9.0 21.7 %all-to-all-start.1 = ((bf16[128,16,64]{0,2,1:T(8,128)(2,1)}), bf16[128,16,64]{0,2,1:T(8,128)(2,1)S(1)}, u32[]{:S(2)}, u32[]{:S(2)}) async-start(bf16[128,16,64]{0,2,1:T(8,128)(2,1)} %bitcast.2), calls=%async_computation.1 | async-start | bytes 524288 | tf_op jit(solution)/shard_map/all_to_all | solution.py:31
  30.6 14.6 %all-to-all-start.3 = ((bf16[128,16,64]{0,2,1:T(8,128)(2,1)}), bf16[128,16,64]{0,2,1:T(8,128)(2,1)S(1)}, u32[]{:S(2)}, u32[]{:S(2)}) async-start(bf16[128,16,64]{0,2,1:T(8,128)(2,1)} %bitcast.14), calls=%async_computation.3 | async-start | bytes 524288 | tf_op jit(solution)/shard_map/all_to_all | solution.py:32
  45.2 25.1 %all-to-all-start = ((bf16[128,16,64]{0,2,1:T(8,128)(2,1)}), bf16[128,16,64]{0,2,1:T(8,128)(2,1)S(1)}, u32[]{:S(2)}, u32[]{:S(2)}) async-start(bf16[128,16,64]{0,2,1:T(8,128)(2,1)} %bitcast), calls=%async_computation | async-start | bytes 524288 | tf_op jit(solution)/shard_map/all_to_all | solution.py:30
  70.4 23.5 %all-to-all-start.4 = ((bf16[128,16,64]{0,2,1:T(8,128)(2,1)}), bf16[128,16,64]{0,2,1:T(8,128)(2,1)S(1)}, u32[]{:S(2)}, u32[]{:S(2)}) async-start(bf16[128,16,64]{0,2,1:T(8,128)(2,1)} %bitcast.16), calls=%async_computation.4 | async-start | bytes 524288 | tf_op jit(solution)/shard_map/all_to_all | solution.py:33
  93.9 24.7 %all-to-all-start.2 = ((bf16[128,16,64]{0,2,1:T(8,128)(2,1)}), bf16[128,16,64]{0,2,1:T(8,128)(2,1)S(1)}, u32[]{:S(2)}, u32[]{:S(2)}) async-start(bf16[128,16,64]{0,2,1:T(8,128)(2,1)} %bitcast.12), calls=%async_computation.2 | async-start | bytes 524288 | tf_op jit(solution)/shard_map/all_to_all | solution.py:34
  98.0 112.2 %reduce-scatter.9.cloned.1.call-start = ((), (), s32[]{:S(2)}) async-start(), calls=%async_computation.11 | async-start | bytes 557056
  139.7 3.2 copy-start
  145.4 146.3 %all-to-all-start.5 = ((bf16[16,128,64]{1,2,0:T(8,128)(2,1)}), bf16[16,128,64]{1,2,0:T(8,128)(2,1)S(1)}, u32[]{:S(2)}, u32[]{:S(2)}) async-start(bf16[16,128,64]{1,2,0:T(8,128)(2,1)} %bitcast.161), calls=%async_computation.5 | async-start | bytes 524288 | tf_op jit(solution)/shard_map/all_to_all | solution.py:115
  156.8 134.0 %reduce-scatter.7.cloned.1.call-start = ((), (), s32[]{:S(2)}) async-start(), calls=%async_computation.10 | async-start | bytes 557056
  291.6 21.0 %all-to-all-start.7 = ((bf16[16,128,64]{1,2,0:T(8,128)(2,1)}), bf16[16,128,64]{1,2,0:T(8,128)(2,1)S(1)}, u32[]{:S(2)}, u32[]{:S(2)}) async-start(bf16[16,128,64]{1,2,0:T(8,128)(2,1)} %bitcast.159), calls=%async_computation.7 | async-start | bytes 524288 | tf_op jit(solution)/shard_map/all_to_all | solution.py:117
  312.6 14.6 %all-to-all-start.6 = ((bf16[16,128,64]{1,2,0:T(8,128)(2,1)}), bf16[16,128,64]{1,2,0:T(8,128)(2,1)S(1)}, u32[]{:S(2)}, u32[]{:S(2)}) async-start(bf16[16,128,64]{1,2,0:T(8,128)(2,1)} %bitcast.160), calls=%async_computation.6 | async-start | bytes 524288 | tf_op jit(solution)/shard_map/all_to_all | solution.py:116
Sparse Core Ops, SparseCore 0:
  131.9 78.1 reduce-scatter.8
  214.0 76.7 reduce-scatter.6
where the time goes:
time: 336 us; the launch traced here: 335 us
  waiting for transfers between devices  153 us (46%)
  starting transfers between devices  58.9 us (18%)
  blocking collectives  38.9 us (12%)
  matrix products  33 us (10%)
  local copies, waits for them, and re-layouts  22.9 us (7%)
  between operations  16 us (5%)
  other arithmetic  11.7 us (3%)
    unnamed x4, waiting for transfers between devices  125 us
    all_gather x1, blocking collectives, on_device(): lax.all_gather(picked_keys, 'outer', axis=0, tiled=True)  19.7 us
    all_gather x1, blocking collectives, on_device(): lax.all_gather(picked_values, 'outer', axis=0, tiled=True)  19.2 us
    unnamed x14, local copies, waits for them, and re-layouts  18.4 us
    all_to_all x1, starting transfers between devices, on_device(): lax.all_to_all(saved_out, 'inner', split_axis=1, concat_axis=0, tiled=True)  11.8 us
    all_to_all x1, starting transfers between devices, on_device(): lax.all_to_all(query_block, 'inner', split_axis=0, concat_axis=1, tiled=T...  11.4 us
    all_to_all x1, starting transfers between devices, on_device(): lax.all_to_all(keys, 'inner', split_axis=1, concat_axis=0, tiled=True)  9.98 us
    all_to_all x1, waiting for transfers between devices, on_device(): lax.all_to_all(keys, 'inner', split_axis=1, concat_axis=0, tiled=True)  9.93 us
  transfers between devices with their start and end apart: 10, of which 7 were waited for; matrix products, arithmetic and copies ran while one was open for 15% of the time, Pallas kernels for 0%

commit v1 on v0

v1 whole, which is shorter than its diff:
```python
import jax
import jax.numpy as jnp
from jax import lax
from jax.experimental import pallas as pl
from jax.experimental.pallas import tpu as pltpu
from jax.sharding import PartitionSpec as P

HEADS = 16
HD = 64
BLOCK = 128
NB = 16
SEG = NB * BLOCK
CHUNK = 256
BF = jnp.bfloat16
F32 = jnp.float32
VMEM = pl.BlockSpec(memory_space=pltpu.VMEM)
SMEM = pl.BlockSpec(memory_space=pltpu.SMEM)
QG_ROWS = BLOCK + 16
OUT_ROWS = BLOCK + HD


def params(mib):
    return pltpu.CompilerParams(vmem_limit_bytes=mib * 1024 * 1024)


def cost(flops, nbytes, exps=0):
    return pl.CostEstimate(flops=flops, bytes_accessed=nbytes, transcendentals=exps)


def dot(a, b):
    return jnp.dot(a, b, preferred_element_type=F32)


def dot_nt(a, b):
    return lax.dot_general(a, b, (((1,), (1,)), ((), ())), preferred_element_type=F32)


def split3(x):
    high = x.astype(BF)
    rest = x - high.astype(F32)
    mid = rest.astype(BF)
    low = (rest - mid.astype(F32)).astype(BF)
    return high, mid, low


def pack_kernel(q_ref, k_ref, v_ref, o_ref, g_ref, kv_ref, qg_ref):
    head_of = lax.broadcasted_iota(jnp.int32, (HEADS, HEADS * HD), 1) // HD
    mine = head_of == lax.broadcasted_iota(jnp.int32, (HEADS, HEADS * HD), 0)
    ones = jnp.where(mine, 1.0, 0.0).astype(BF)
    product = g_ref[...].astype(F32) * o_ref[...].astype(F32)
    high = product.astype(BF)
    low = (product - high.astype(F32)).astype(BF)
    terms = dot_nt(ones, high) + dot_nt(ones, low)
    parts = [part.astype(F32) for part in split3(terms)]
    row = lax.broadcasted_iota(jnp.int32, (16, BLOCK), 0)
    for pair in range(HEADS // 2):
        cols = slice(pair * 2 * HD, (pair + 1) * 2 * HD)
        q, k, v, g = (
            (q_ref[:, cols].astype(F32) * (HD**-0.5)).astype(BF),
            k_ref[:, cols],
            v_ref[:, cols],
            g_ref[:, cols],
        )
        for sub in range(2):
            head = 2 * pair + sub
            half = slice(sub * HD, (sub + 1) * HD)
            kv_ref[head] = jnp.concatenate([k[:, half], v[:, half]], axis=1)
            qg_ref[head, :BLOCK, :] = jnp.concatenate([q[:, half], g[:, half]], axis=1)
            tail = jnp.zeros((16, BLOCK), F32)
            for n, part in enumerate(parts):
                tail = jnp.where(row == n, part[head : head + 1, :], tail)
            qg_ref[head, BLOCK:, :] = tail.astype(BF)


def pack(queries, keys, values, saved_out, out_grad):
    return pl.pallas_call(
        pack_kernel,
        out_shape=(
            jax.ShapeDtypeStruct((HEADS, BLOCK, 2 * HD), BF),
            jax.ShapeDtypeStruct((HEADS, QG_ROWS, 2 * HD), BF),
        ),
        in_specs=[VMEM] * 5,
        out_specs=(VMEM, VMEM),
        compiler_params=params(32),
        cost_estimate=cost(10**7, 2 * 10**6),
        name="pack_heads",
    )(queries, keys, values, saved_out, out_grad)


def block_terms(tail):
    tail = tail.astype(F32)
    return tail[0:1, :] + tail[1:2, :] + tail[2:3, :]


def score_weights(qg):
    turned = qg.T
    top_half = lax.broadcasted_iota(jnp.int32, turned.shape, 0) < HD
    zero = jnp.zeros_like(turned)
    return jnp.concatenate(
        [jnp.where(top_half, turned, zero), jnp.where(top_half, zero, turned)], axis=1
    )


def grad_weights(qg, factor):
    scaled = (qg.T.astype(F32) * factor).T
    left = lax.broadcasted_iota(jnp.int32, scaled.shape, 1) < HD
    return jnp.concatenate(
        [jnp.where(left, 0.0, scaled), jnp.where(left, scaled, 0.0)], axis=0
    ).astype(BF)


def fold(x, op):
    return op(x.reshape(-1, 8, x.shape[1]), axis=0)


def far_kernel(offs_ref, kv_ref, qg_ref, far_ref, part_ref, stat_ref, near_s, far_s, ed):
    offset = offs_ref[lax.axis_index("inner")]
    qg = qg_ref[offset, :BLOCK, :]
    terms = block_terms(qg_ref[offset, BLOCK:, :])
    weights = score_weights(qg)
    top8 = jnp.full((8, BLOCK), -jnp.inf, F32)
    for c in range(SEG // CHUNK):
        rows = slice(c * CHUNK, (c + 1) * CHUNK)
        blocks = slice(c * CHUNK // BLOCK, (c + 1) * CHUNK // BLOCK)
        near = dot(kv_ref[blocks].reshape(CHUNK, 2 * HD), weights[:, :BLOCK])
        near_s[rows, :] = near
        far = dot(far_ref[blocks].reshape(CHUNK, 2 * HD), weights)
        far_s[rows, :] = far
        top8 = jnp.maximum(top8, jnp.maximum(fold(near, jnp.max), fold(far[:, :BLOCK], jnp.max)))
    top = jnp.max(top8, axis=0, keepdims=True)
    sum8 = jnp.zeros((8, BLOCK), F32)
    for c in range(SEG // CHUNK):
        rows = slice(c * CHUNK, (c + 1) * CHUNK)
        sum8 += fold(jnp.exp(near_s[rows, :] - top), jnp.sum)
        prob = jnp.exp(far_s[rows, :BLOCK] - top)
        sum8 += fold(prob, jnp.sum)
        ed[rows, :BLOCK] = prob.astype(BF)
        ed[rows, BLOCK:] = (prob * (far_s[rows, BLOCK:] - terms)).astype(BF)
    factor = 1.0 / jnp.sum(sum8, axis=0, keepdims=True)
    second = grad_weights(qg, factor)
    query_grad = jnp.zeros((HD, BLOCK), F32)
    for c in range(SEG // CHUNK):
        rows = slice(c * CHUNK, (c + 1) * CHUNK)
        blocks = slice(c * CHUNK // BLOCK, (c + 1) * CHUNK // BLOCK)
        both = ed[rows, :]
        part_ref[blocks] = dot(both, second).astype(BF).reshape(-1, BLOCK, 2 * HD)
        keys = far_ref[blocks].reshape(CHUNK, 2 * HD).T[:HD, :]
        query_grad += dot(keys, both[:, BLOCK:])
    stat_ref[0:1, :] = top
    stat_ref[1:2, :] = factor
    stat_ref[8:, :] = query_grad * factor * (HD**-0.5)


def far_part(offsets, kv, qg, far):
    return pl.pallas_call(
        far_kernel,
        out_shape=(
            jax.ShapeDtypeStruct((NB, BLOCK, 2 * HD), BF),
            jax.ShapeDtypeStruct((8 + HD, BLOCK), F32),
        ),
        in_specs=[SMEM, VMEM, VMEM, VMEM],
        out_specs=(VMEM, VMEM),
        scratch_shapes=[
            pltpu.VMEM((SEG, BLOCK), F32),
            pltpu.VMEM((SEG, 2 * BLOCK), F32),
            pltpu.VMEM((SEG, 2 * BLOCK), BF),
        ],
        compiler_params=params(32),
        cost_estimate=cost(2 * 10**9, 2 * 10**6),
        name="far_part",
    )(offsets, kv, qg, far)


def near_kernel(
    offs_ref, kv_ref, qg_ref, stat_ref, out_ref, pick_ref, keys_t, s0, s1, e0, e1, acc, st0, st1
):
    offset = offs_ref[lax.axis_index("inner")]
    score_refs, grad_refs, stats = (s0, s1), (e0, e1), (st0, st1)
    acc[...] = jnp.zeros_like(acc)
    for b in range(NB):
        keys_t[:, b * BLOCK : (b + 1) * BLOCK] = kv_ref[b].T[:HD, :]

    def step(j, slot, first, second, third):
        s_now, s_old = score_refs[slot], score_refs[1 - slot]
        e_now, e_old = grad_refs[1 - slot], grad_refs[slot]
        st_now, st_old = stats[slot], stats[1 - slot]
        if first:
            weights = score_weights(qg_ref[j, :BLOCK, :])
            top8 = jnp.full((8, BLOCK), -jnp.inf, F32)
        if second:
            picked1 = (j - 1) == offset
            terms = block_terms(qg_ref[j - 1, BLOCK:, :])
            top = st_old[0:1, :]
            sum8 = jnp.zeros((8, BLOCK), F32)
        if third:
            picked2 = (j - 2) == offset
            factor = st_now[1:2, :]
            gweights = grad_weights(qg_ref[j - 2, :BLOCK, :], factor)
            query_grad = jnp.zeros((HD, BLOCK), F32)
        for c in range(SEG // CHUNK):
            rows = slice(c * CHUNK, (c + 1) * CHUNK)
            blocks = slice(c * CHUNK // BLOCK, (c + 1) * CHUNK // BLOCK)
            if third:
                both = e_old[rows, :]
                acc[rows, :] += dot(both, gweights)
                query_grad += dot(keys_t[:, rows], both[:, BLOCK:])
            if first:
                score = dot(kv_ref[blocks].reshape(CHUNK, 2 * HD), weights)
                s_now[rows, :] = score
                top8 = jnp.maximum(top8, fold(score[:, :BLOCK], jnp.max))
            if second:
                prob = jnp.exp(s_old[rows, :BLOCK] - top)
                sum8 += fold(prob, jnp.sum)
                e_now[rows, :BLOCK] = prob.astype(BF)
                e_now[rows, BLOCK:] = (prob * (s_old[rows, BLOCK:] - terms)).astype(BF)
        if third:
            query_grad = query_grad * (factor * (HD**-0.5))
            query_grad += jnp.where(picked2, stat_ref[8:, :], 0.0)
            out_ref[j - 2, BLOCK:, :] = query_grad.astype(BF)
        if first:
            top = jnp.max(top8, axis=0, keepdims=True)
            st_now[0:1, :] = jnp.where(j == offset, stat_ref[0:1, :], top)
        if second:
            total = jnp.sum(sum8, axis=0, keepdims=True)
            st_old[1:2, :] = jnp.where(picked1, stat_ref[1:2, :], 1.0 / total)

    step(0, 0, True, False, False)
    step(1, 1, True, True, False)

    def pair(i, carry):
        step(2 * i, 0, True, True, True)
        step(2 * i + 1, 1, True, True, True)
        return carry

    lax.fori_loop(1, NB // 2, pair, 0)
    step(NB, 0, False, True, True)
    step(NB + 1, 1, False, False, True)
    for b in range(NB):
        out_ref[b, :BLOCK, :] = acc[b * BLOCK : (b + 1) * BLOCK, :].astype(BF)
    pick_ref[...] = acc[pl.ds(pl.multiple_of(offset * BLOCK, BLOCK), BLOCK), :]


def near_part(offsets, kv, qg, stat):
    return pl.pallas_call(
        near_kernel,
        out_shape=(
            jax.ShapeDtypeStruct((NB, OUT_ROWS, BLOCK), BF),
            jax.ShapeDtypeStruct((BLOCK, 2 * HD), F32),
        ),
        in_specs=[SMEM, VMEM, VMEM, VMEM],
        out_specs=(VMEM, VMEM),
        scratch_shapes=[
            pltpu.VMEM((HD, SEG), BF),
            pltpu.VMEM((SEG, 2 * BLOCK), F32),
            pltpu.VMEM((SEG, 2 * BLOCK), F32),
            pltpu.VMEM((SEG, 2 * BLOCK), BF),
            pltpu.VMEM((SEG, 2 * BLOCK), BF),
            pltpu.VMEM((SEG, 2 * HD), F32),
            pltpu.VMEM((8, BLOCK), F32),
            pltpu.VMEM((8, BLOCK), F32),
        ],
        compiler_params=params(40),
        cost_estimate=cost(15 * 10**9, 4 * 10**6, SEG * SEG),
        name="near_part",
    )(offsets, kv, qg, stat)


def finish_kernel(offs_ref, pick_ref, parts_ref, whole_ref, out_ref):
    del offs_ref, whole_ref
    total = pick_ref[...]
    for n in range(NB):
        total += parts_ref[n].astype(F32)
    out_ref[0] = total.astype(BF)


def finish(head_offset, pick, parts, whole):
    return pl.pallas_call(
        finish_kernel,
        out_shape=jax.ShapeDtypeStruct((NB, OUT_ROWS, BLOCK), BF),
        grid_spec=pltpu.PrefetchScalarGridSpec(
            num_scalar_prefetch=1,
            grid=(1,),
            in_specs=[
                pl.BlockSpec((BLOCK, 2 * HD), lambda i, off: (0, 0)),
                pl.BlockSpec((NB, BLOCK, 2 * HD), lambda i, off: (0, 0, 0)),
                pl.BlockSpec(memory_space=pl.ANY),
            ],
            out_specs=pl.BlockSpec((1, BLOCK, 2 * HD), lambda i, off: (off[0], 0, 0)),
        ),
        input_output_aliases={3: 0},
        cost_estimate=cost(10**6, 10**6),
        name="finish_picked",
    )(head_offset, pick, parts, whole)


def unpack_kernel(in_ref, q_ref, k_ref, v_ref):
    for pair in range(HEADS // 2):
        cols = slice(pair * 2 * HD, (pair + 1) * 2 * HD)
        one, two = in_ref[2 * pair, :BLOCK, :], in_ref[2 * pair + 1, :BLOCK, :]
        k_ref[:, cols] = jnp.concatenate([one[:, :HD], two[:, :HD]], axis=1)
        v_ref[:, cols] = jnp.concatenate([one[:, HD:], two[:, HD:]], axis=1)
        turned = jnp.concatenate(
            [in_ref[2 * pair, BLOCK:, :], in_ref[2 * pair + 1, BLOCK:, :]], axis=0
        )
        q_ref[:, cols] = turned.T


def unpack(block):
    shape = jax.ShapeDtypeStruct((BLOCK, HEADS * HD), BF)
    return pl.pallas_call(
        unpack_kernel,
        out_shape=(shape, shape, shape),
        in_specs=[VMEM],
        out_specs=(VMEM, VMEM, VMEM),
        compiler_params=params(32),
        cost_estimate=cost(10**6, 2 * 10**6),
        name="unpack_heads",
    )(block)


def exchange(array, axis):
    return lax.all_to_all(array, axis, split_axis=0, concat_axis=0, tiled=True)


def on_device(queries, keys, values, saved_out, out_grad, offsets):
    head_offset = lax.dynamic_slice_in_dim(offsets, lax.axis_index("inner"), 1)
    kv, qg = pack(queries, keys, values, saved_out, out_grad)
    kv = exchange(kv, "inner")
    picked = lax.dynamic_index_in_dim(kv, head_offset[0], 0, keepdims=True)
    far = exchange(jnp.broadcast_to(picked, kv.shape), "outer")
    qg = exchange(qg, "inner")
    parts, stat = far_part(offsets, kv, qg, far)
    parts = exchange(parts, "outer")
    whole, pick = near_part(offsets, kv, qg, stat)
    whole = finish(head_offset, pick, parts, whole)
    return unpack(exchange(whole, "inner"))


def solution(mesh):
    rows = P(("outer", "inner"), None)
    return jax.shard_map(
        on_device,
        mesh=mesh,
        in_specs=(rows, rows, rows, rows, rows, P()),
        out_specs=(rows, rows, rows),
        check_vma=False,
    )
```

time: 336 us -> 130 us (0.39)
  waiting for transfers between devices: 153 us -> 14.9 us
  starting transfers between devices: 58.9 us -> 7.05 us
  matrix products: 33 us -> 0 us
  blocking collectives: 38.9 us -> 71.8 us
  Pallas kernels: 0 us -> 24.4 us
  local copies, waits for them, and re-layouts: 22.9 us -> 8.42 us
  between operations: 16 us -> 2.65 us
  other arithmetic: 11.7 us -> 0 us
    unnamed x4 -> x0, waiting for transfers between devices: 125 us -> none
    all_to_all x0 -> x3, blocking collectives: none -> 71.8 us  [exchange(): return lax.all_to_all(array, axis, split_axis=0, concat_axis=0, tiled=True)]
    all_to_all x8 -> x2, starting transfers between devices: 58.8 us -> 7.05 us  [exchange(): return lax.all_to_all(array, axis, split_axis=0, concat_axis=0, tiled=True)]
    all_gather x2 -> x0, blocking collectives: 38.9 us -> none  [the longest x1 19.7 us: on_device(): lax.all_gather(picked_keys, 'outer', axis=0, tiled=True)]
    dot_general x10 -> x0, matrix products: 33 us -> none  [the longest x1 8.11 us: on_device(): near = jnp.dot(seg_q, seg_k.T, preferred_element_type=jnp.float32) * scale]
    pallas_call x0 -> x5, Pallas kernels: none -> 24.4 us  [the longest x1 16.5 us: near_part(): pl.pallas_call(near_kernel, out_shape=(jax.ShapeDtypeStruct((NB, OUT_ROWS...]
    all_to_all x8 -> x2, waiting for transfers between devices: 28.8 us -> 14.9 us  [exchange(): return lax.all_to_all(array, axis, split_axis=0, concat_axis=0, tiled=True)]
    unnamed x14 -> x18, local copies, waits for them, and re-layouts: 18.4 us -> 7.74 us
  transfers between devices with their start and end apart: 10 -> 2, of which waited for: 7 -> 1; matrix products, arithmetic and copies ran while one was open for 15% -> 0% of each run, Pallas kernels for 0% -> 13%
where the time goes in v1:
time: 130 us; the launch traced here: 129 us
  blocking collectives  71.8 us (55%)
  Pallas kernels  24.4 us (19%)
  waiting for transfers between devices  14.9 us (11%)
  local copies, waits for them, and re-layouts  8.42 us (6%)
  starting transfers between devices  7.05 us (5%)
  between operations  2.65 us (2%)
    all_to_all x3, blocking collectives, exchange(): return lax.all_to_all(array, axis, split_axis=0, concat_axis=0, tiled=True)  71.8 us
    pallas_call x1, Pallas kernels, near_part(): pl.pallas_call(near_kernel, out_shape=(jax.ShapeDtypeStruct((NB, OUT_ROWS...  16.5 us
    all_to_all x2, waiting for transfers between devices, exchange(): return lax.all_to_all(array, axis, split_axis=0, concat_axis=0, tiled=True)  14.9 us
    unnamed x18, local copies, waits for them, and re-layouts  7.74 us
    all_to_all x2, starting transfers between devices, exchange(): return lax.all_to_all(array, axis, split_axis=0, concat_axis=0, tiled=True)  7.05 us
    pallas_call x1, Pallas kernels, far_part(): pl.pallas_call(far_kernel, out_shape=(jax.ShapeDtypeStruct((NB, BLOCK, 2...  3.15 us
  transfers between devices with their start and end apart: 2, of which 1 were waited for; matrix products, arithmetic and copies ran while one was open for 0% of the time, Pallas kernels for 13%

profile of v1, /device:TPU:1, one launch (start us, length us, event | category | flops | bytes accessed | tf_op | source)
XLA Modules:
  0.0 129.2 jit_solution(5687506479420171437)
XLA Ops:
  0.6 0.0 copy-start.1
  0.6 0.9 copy-done.1
  1.6 0.0 copy-start.2
  1.6 0.9 copy-done.2
  2.5 0.0 copy-start.3
  2.5 0.9 copy-done.3
  3.5 0.0 copy-start.4
  3.5 0.9 copy-done.4
  4.4 0.0 copy-start.5
  4.4 0.9 copy-done.5
  5.4 1.2 pack_heads.1
  6.6 27.1 %all_to_all.25.kv_ref = bf16[16,128,128]{2,1,0:T(8,128)(2,1)S(1)} all-to-all(bf16[16,128,128]{2,1,0:T(8,128)(2,1)S(1)} %get-tuple-element.9), channel_id=1, replica_groups=mesh['outer'=16,'inner'=16] {'inner'}, dimensions={0} | all-to-all | bytes 1048576 | tf_op jit(solution)/shard_map/all_to_all | solution.py:322
  33.7 3.5 %all-to-all-start.1 = ((bf16[16,144,128]{2,1,0:T(8,128)(2,1)}), bf16[16,144,128]{2,1,0:T(8,128)(2,1)S(1)}, u32[]{:S(2)}, u32[]{:S(2)}) async-start(bf16[16,144,128]{2,1,0:T(8,128)(2,1)} %get-tuple-element.10), calls=%async_computation.1 | async-start | bytes 1179648 | tf_op jit(solution)/shard_map/all_to_all | solution.py:322
  37.2 0.0 copy-start.7
  37.2 0.6 copy-done.7
  37.8 0.6 dynamic_slice.7.offs_ref
  40.4 14.9 %all-to-all-done.1.qg_ref = bf16[16,144,128]{2,1,0:T(8,128)(2,1)S(1)} async-done(((bf16[16,144,128]{2,1,0:T(8,128)(2,1)}), bf16[16,144,128]{2,1,0:T(8,128)(2,1)S(1)}, u32[]{:S(2)}, u32[]{:S(2)}) %all-to-all-start.1) | async-done | bytes 589856 | tf_op jit(solution)/shard_map/all_to_all | solution.py:322
  55.2 0.1 broadcast_in_dim.8
  55.3 17.8 %all_to_all.26.far_ref = bf16[16,128,128]{2,1,0:T(8,128)(2,1)S(1)} all-to-all(bf16[16,128,128]{2,1,0:T(8,128)(2,1)S(1)} %broadcast_in_dim.8), channel_id=1, replica_groups=mesh['outer'=16,'inner'=16] {'outer'}, dimensions={0} | all-to-all | bytes 1048576 | tf_op jit(solution)/shard_map/all_to_all | solution.py:322
  73.2 3.1 %far_part.1 = (bf16[16,128,128]{2,1,0:T(8,128)(2,1)}, f32[72,128]{1,0:T(8,128)S(1)}) custom-call(s32[16]{0:T(128)S(1)} %copy-done.7, bf16[16,128,128]{2,1,0:T(8,128)(2,1)S(1)} %all_to_all.25.kv_ref, bf16[16,144,128]{2,1,0:T(8,128)(2,1)S(1)} %all-to-all-done.1.qg_ref, bf16[16,128,128]{2,1,0:T(8,128)(2,1)S(1)} %all_to_all.26.far_ref), custom_call_target="tpu_custom_call" | custom-call | flops 2000000000 | bytes 2000000 | tf_op jit(solution)/shard_map/far_part/pallas_call | solution.py:155
  76.3 3.6 %all-to-all-start.3 = ((bf16[16,128,128]{2,1,0:T(8,128)(2,1)}), bf16[16,128,128]{2,1,0:T(8,128)(2,1)S(1)}, u32[]{:S(2)}, u32[]{:S(2)}) async-start(bf16[16,128,128]{2,1,0:T(8,128)(2,1)} %get-tuple-element.13), calls=%async_computation.3 | async-start | bytes 1048576 | tf_op jit(solution)/shard_map/all_to_all | solution.py:322
  79.9 16.5 %near_part.1 = (bf16[16,192,128]{2,1,0:T(8,128)(2,1)S(1)}, f32[128,128]{1,0:T(8,128)S(1)}) custom-call(s32[16]{0:T(128)S(1)} %copy-done.7, bf16[16,128,128]{2,1,0:T(8,128)(2,1)S(1)} %all_to_all.25.kv_ref, bf16[16,144,128]{2,1,0:T(8,128)(2,1)S(1)} %all-to-all-done.1.qg_ref, f32[72,128]{1,0:T(8,128)S(1)} %get-tuple-element.11.stat_ref), custom_call_target="tpu_custom_call" | custom-call | flops 15000000512 | bytes 4000000 | tf_op jit(solution)/shard_map/near_part/pallas_call | solution.py:244
  96.4 0.0 copy-start
  96.4 0.9 copy-done
  97.3 0.0 copy-start.6
  97.3 0.6 copy-done.6
  97.9 0.0 all-to-all-done.3.parts_ref
  97.9 0.0 copy-start.8
  97.9 0.8 copy-done.8
  98.8 2.4 %finish_picked.1 = bf16[16,192,128]{2,1,0:T(8,128)(2,1)} custom-call(s32[1]{0:T(128)} %dynamic_slice.7.offs_ref, f32[128,128]{1,0:T(8,128)} %copy-done.6, bf16[16,128,128]{2,1,0:T(8,128)(2,1)} %copy-done.8, bf16[16,192,128]{2,1,0:T(8,128)(2,1)} %copy-done), custom_call_target="tpu_custom_call", output_to_operand_aliasing={{}: (3, {})} | custom-call | flops 1000000 | bytes 1000000 | tf_op jit(solution)/shard_map/finish_picked/pallas_call | solution.py:277
  101.2 26.9 %all_to_all.27.in_ref = bf16[16,192,128]{2,1,0:T(8,128)(2,1)S(1)} all-to-all(bf16[16,192,128]{2,1,0:T(8,128)(2,1)} %finish_picked.1), channel_id=1, replica_groups=mesh['outer'=16,'inner'=16] {'inner'}, dimensions={0} | all-to-all | bytes 1572864 | tf_op jit(solution)/shard_map/all_to_all | solution.py:322
  128.0 1.1 unpack_heads.1
  (1 shorter events, 0.0 us)
Async XLA Ops:
  0.6 1.0 copy-start.1
  1.6 0.9 copy-start.2
  2.5 0.9 copy-start.3
  3.5 0.9 copy-start.4
  4.4 0.9 copy-start.5
  33.7 21.6 %all-to-all-start.1 = ((bf16[16,144,128]{2,1,0:T(8,128)(2,1)}), bf16[16,144,128]{2,1,0:T(8,128)(2,1)S(1)}, u32[]{:S(2)}, u32[]{:S(2)}) async-start(bf16[16,144,128]{2,1,0:T(8,128)(2,1)} %get-tuple-element.10), calls=%async_computation.1 | async-start | bytes 1179648 | tf_op jit(solution)/shard_map/all_to_all | solution.py:322
  37.2 0.7 copy-start.7
  76.3 21.6 %all-to-all-start.3 = ((bf16[16,128,128]{2,1,0:T(8,128)(2,1)}), bf16[16,128,128]{2,1,0:T(8,128)(2,1)S(1)}, u32[]{:S(2)}, u32[]{:S(2)}) async-start(bf16[16,128,128]{2,1,0:T(8,128)(2,1)} %get-tuple-element.13), calls=%async_computation.3 | async-start | bytes 1048576 | tf_op jit(solution)/shard_map/all_to_all | solution.py:322
  96.4 0.9 copy-start
  97.3 0.6 copy-start.6
  97.9 0.8 copy-start.8

commit v2 on v1

--- a/solution.py
+++ b/solution.py
@@ -9,6 +9,7 @@
 HD = 64
 BLOCK = 128
 NB = 16
+RING = 4
 SEG = NB * BLOCK
 CHUNK = 256
 BF = jnp.bfloat16
@@ -43,7 +44,17 @@
     return high, mid, low
 
 
-def pack_kernel(q_ref, k_ref, v_ref, o_ref, g_ref, kv_ref, qg_ref):
+def pack_kernel(q_in, k_in, v_in, o_in, g_in, kv_ref, qg_ref, q_ref, k_ref, v_ref, o_ref, g_ref, sems):
+    copies = [
+        pltpu.make_async_copy(source, target, sems.at[n])
+        for n, (source, target) in enumerate(
+            ((g_in, g_ref), (o_in, o_ref), (q_in, q_ref), (k_in, k_ref), (v_in, v_ref))
+        )
+    ]
+    for copy in copies:
+        copy.start()
+    copies[0].wait()
+    copies[1].wait()
     head_of = lax.broadcasted_iota(jnp.int32, (HEADS, HEADS * HD), 1) // HD
     mine = head_of == lax.broadcasted_iota(jnp.int32, (HEADS, HEADS * HD), 0)
     ones = jnp.where(mine, 1.0, 0.0).astype(BF)
@@ -53,6 +64,8 @@
     terms = dot_nt(ones, high) + dot_nt(ones, low)
     parts = [part.astype(F32) for part in split3(terms)]
     row = lax.broadcasted_iota(jnp.int32, (16, BLOCK), 0)
+    for copy in copies[2:]:
+        copy.wait()
     for pair in range(HEADS // 2):
         cols = slice(pair * 2 * HD, (pair + 1) * 2 * HD)
         q, k, v, g = (
@@ -79,12 +92,29 @@
             jax.ShapeDtypeStruct((HEADS, BLOCK, 2 * HD), BF),
             jax.ShapeDtypeStruct((HEADS, QG_ROWS, 2 * HD), BF),
         ),
-        in_specs=[VMEM] * 5,
+        in_specs=[pl.BlockSpec(memory_space=pl.ANY)] * 5,
         out_specs=(VMEM, VMEM),
-        compiler_params=params(32),
+        scratch_shapes=[pltpu.VMEM((BLOCK, HEADS * HD), BF)] * 5 + [pltpu.SemaphoreType.DMA((5,))],
+        compiler_params=params(60),
         cost_estimate=cost(10**7, 2 * 10**6),
         name="pack_heads",
     )(queries, keys, values, saved_out, out_grad)
+
+
+def pick_kernel(offs_ref, kv_ref, out_ref):
+    out_ref[...] = kv_ref[offs_ref[lax.axis_index("inner")]]
+
+
+def pick(offsets, kv):
+    return pl.pallas_call(
+        pick_kernel,
+        out_shape=jax.ShapeDtypeStruct(kv.shape[1:], kv.dtype),
+        in_specs=[SMEM, VMEM],
+        out_specs=VMEM,
+        compiler_params=params(16),
+        cost_estimate=cost(10**3, 10**5),
+        name="pick_block",
+    )(offsets, kv)
 
 
 def block_terms(tail):
@@ -113,8 +143,19 @@
     return op(x.reshape(-1, 8, x.shape[1]), axis=0)
 
 
-def far_kernel(offs_ref, kv_ref, qg_ref, far_ref, part_ref, stat_ref, near_s, far_s, ed):
+def far_kernel(
+    offs_ref, kv_ref, qg_ref, far0, far1, far2, far3, part_ref, stat_ref, near_s, far_s, ed
+):
     offset = offs_ref[lax.axis_index("inner")]
+    place = lax.axis_index("outer")
+    place_x, place_y = place // RING, place % RING
+    fars = (far0, far1, far2, far3)
+
+    def far_rows(c):
+        per = CHUNK // BLOCK
+        a, b = divmod(c * per, RING)
+        return fars[a][b : b + per].reshape(CHUNK, 2 * HD)
+
     qg = qg_ref[offset, :BLOCK, :]
     terms = block_terms(qg_ref[offset, BLOCK:, :])
     weights = score_weights(qg)
@@ -124,7 +165,7 @@
         blocks = slice(c * CHUNK // BLOCK, (c + 1) * CHUNK // BLOCK)
         near = dot(kv_ref[blocks].reshape(CHUNK, 2 * HD), weights[:, :BLOCK])
         near_s[rows, :] = near
-        far = dot(far_ref[blocks].reshape(CHUNK, 2 * HD), weights)
+        far = dot(far_rows(c), weights)
         far_s[rows, :] = far
         top8 = jnp.maximum(top8, jnp.maximum(fold(near, jnp.max), fold(far[:, :BLOCK], jnp.max)))
     top = jnp.max(top8, axis=0, keepdims=True)
@@ -141,24 +182,27 @@
     query_grad = jnp.zeros((HD, BLOCK), F32)
     for c in range(SEG // CHUNK):
         rows = slice(c * CHUNK, (c + 1) * CHUNK)
-        blocks = slice(c * CHUNK // BLOCK, (c + 1) * CHUNK // BLOCK)
         both = ed[rows, :]
-        part_ref[blocks] = dot(both, second).astype(BF).reshape(-1, BLOCK, 2 * HD)
-        keys = far_ref[blocks].reshape(CHUNK, 2 * HD).T[:HD, :]
+        grads = dot(both, second).astype(BF)
+        for n in range(CHUNK // BLOCK):
+            a, b = divmod(c * CHUNK // BLOCK + n, RING)
+            owner = (place_x + a) % RING * RING + (place_y + b) % RING
+            part_ref[owner] = grads[n * BLOCK : (n + 1) * BLOCK, :]
+        keys = far_rows(c).T[:HD, :]
         query_grad += dot(keys, both[:, BLOCK:])
     stat_ref[0:1, :] = top
     stat_ref[1:2, :] = factor
     stat_ref[8:, :] = query_grad * factor * (HD**-0.5)
 
 
-def far_part(offsets, kv, qg, far):
+def far_part(offsets, kv, qg, fars):
     return pl.pallas_call(
         far_kernel,
         out_shape=(
             jax.ShapeDtypeStruct((NB, BLOCK, 2 * HD), BF),
             jax.ShapeDtypeStruct((8 + HD, BLOCK), F32),
         ),
-        in_specs=[SMEM, VMEM, VMEM, VMEM],
+        in_specs=[SMEM] + [VMEM] * 6,
         out_specs=(VMEM, VMEM),
         scratch_shapes=[
             pltpu.VMEM((SEG, BLOCK), F32),
@@ -168,11 +212,11 @@
         compiler_params=params(32),
         cost_estimate=cost(2 * 10**9, 2 * 10**6),
         name="far_part",
-    )(offsets, kv, qg, far)
+    )(offsets, kv, qg, *fars)
 
 
 def near_kernel(
-    offs_ref, kv_ref, qg_ref, stat_ref, out_ref, pick_ref, keys_t, s0, s1, e0, e1, acc, st0, st1
+    offs_ref, kv_ref, qg_ref, stat_ref, dq_ref, acc, keys_t, s0, s1, e0, e1, st0, st1
 ):
     offset = offs_ref[lax.axis_index("inner")]
     score_refs, grad_refs, stats = (s0, s1), (e0, e1), (st0, st1)
@@ -216,7 +260,7 @@
         if third:
             query_grad = query_grad * (factor * (HD**-0.5))
             query_grad += jnp.where(picked2, stat_ref[8:, :], 0.0)
-            out_ref[j - 2, BLOCK:, :] = query_grad.astype(BF)
+            dq_ref[j - 2] = query_grad.astype(BF)
         if first:
             top = jnp.max(top8, axis=0, keepdims=True)
             st_now[0:1, :] = jnp.where(j == offset, stat_ref[0:1, :], top)
@@ -235,17 +279,14 @@
     lax.fori_loop(1, NB // 2, pair, 0)
     step(NB, 0, False, True, True)
     step(NB + 1, 1, False, False, True)
-    for b in range(NB):
-        out_ref[b, :BLOCK, :] = acc[b * BLOCK : (b + 1) * BLOCK, :].astype(BF)
-    pick_ref[...] = acc[pl.ds(pl.multiple_of(offset * BLOCK, BLOCK), BLOCK), :]
 
 
 def near_part(offsets, kv, qg, stat):
     return pl.pallas_call(
         near_kernel,
         out_shape=(
-            jax.ShapeDtypeStruct((NB, OUT_ROWS, BLOCK), BF),
-            jax.ShapeDtypeStruct((BLOCK, 2 * HD), F32),
+            jax.ShapeDtypeStruct((NB, HD, BLOCK), BF),
+            jax.ShapeDtypeStruct((SEG, 2 * HD), F32),
         ),
         in_specs=[SMEM, VMEM, VMEM, VMEM],
         out_specs=(VMEM, VMEM),
@@ -255,7 +296,6 @@
             pltpu.VMEM((SEG, 2 * BLOCK), F32),
             pltpu.VMEM((SEG, 2 * BLOCK), BF),
             pltpu.VMEM((SEG, 2 * BLOCK), BF),
-            pltpu.VMEM((SEG, 2 * HD), F32),
             pltpu.VMEM((8, BLOCK), F32),
             pltpu.VMEM((8, BLOCK), F32),
         ],
@@ -265,32 +305,27 @@
     )(offsets, kv, qg, stat)
 
 
-def finish_kernel(offs_ref, pick_ref, parts_ref, whole_ref, out_ref):
-    del offs_ref, whole_ref
-    total = pick_ref[...]
+def finish_kernel(offs_ref, dq_ref, acc, parts_ref, out_ref):
+    offset = offs_ref[lax.axis_index("inner")]
+    for b in range(NB):
+        out_ref[b, :BLOCK, :] = acc[b * BLOCK : (b + 1) * BLOCK, :].astype(BF)
+        out_ref[b, BLOCK:, :] = dq_ref[b]
+    total = acc[pl.ds(pl.multiple_of(offset * BLOCK, BLOCK), BLOCK), :]
     for n in range(NB):
         total += parts_ref[n].astype(F32)
-    out_ref[0] = total.astype(BF)
-
-
-def finish(head_offset, pick, parts, whole):
+    out_ref[offset, :BLOCK, :] = total.astype(BF)
+
+
+def finish(offsets, dq, sums, parts):
     return pl.pallas_call(
         finish_kernel,
         out_shape=jax.ShapeDtypeStruct((NB, OUT_ROWS, BLOCK), BF),
-        grid_spec=pltpu.PrefetchScalarGridSpec(
-            num_scalar_prefetch=1,
-            grid=(1,),
-            in_specs=[
-                pl.BlockSpec((BLOCK, 2 * HD), lambda i, off: (0, 0)),
-                pl.BlockSpec((NB, BLOCK, 2 * HD), lambda i, off: (0, 0, 0)),
-                pl.BlockSpec(memory_space=pl.ANY),
-            ],
-            out_specs=pl.BlockSpec((1, BLOCK, 2 * HD), lambda i, off: (off[0], 0, 0)),
-        ),
-        input_output_aliases={3: 0},
+        in_specs=[SMEM, VMEM, VMEM, VMEM],
+        out_specs=VMEM,
+        compiler_params=params(32),
         cost_estimate=cost(10**6, 10**6),
         name="finish_picked",
-    )(head_offset, pick, parts, whole)
+    )(offsets, dq, sums, parts)
 
 
 def unpack_kernel(in_ref, q_ref, k_ref, v_ref):
@@ -322,17 +357,28 @@
     return lax.all_to_all(array, axis, split_axis=0, concat_axis=0, tiled=True)
 
 
+def spread(block):
+    def ring(step, along_x):
+        pairs = []
+        for x in range(RING):
+            for y in range(RING):
+                source = (x + step) % RING * RING + y if along_x else x * RING + (y + step) % RING
+                pairs.append((source, x * RING + y))
+        return pairs
+
+    row = jnp.stack([block] + [lax.ppermute(block, "outer", ring(n, False)) for n in (1, 2, 3)])
+    return [row] + [lax.ppermute(row, "outer", ring(n, True)) for n in (1, 2, 3)]
+
+
 def on_device(queries, keys, values, saved_out, out_grad, offsets):
-    head_offset = lax.dynamic_slice_in_dim(offsets, lax.axis_index("inner"), 1)
     kv, qg = pack(queries, keys, values, saved_out, out_grad)
     kv = exchange(kv, "inner")
-    picked = lax.dynamic_index_in_dim(kv, head_offset[0], 0, keepdims=True)
-    far = exchange(jnp.broadcast_to(picked, kv.shape), "outer")
+    fars = spread(pick(offsets, kv))
     qg = exchange(qg, "inner")
-    parts, stat = far_part(offsets, kv, qg, far)
+    parts, stat = far_part(offsets, kv, qg, fars)
     parts = exchange(parts, "outer")
-    whole, pick = near_part(offsets, kv, qg, stat)
-    whole = finish(head_offset, pick, parts, whole)
+    dq, sums = near_part(offsets, kv, qg, stat)
+    whole = finish(offsets, dq, sums, parts)
     return unpack(exchange(whole, "inner"))
 
 

time: 130 us -> 110 us (0.85)
  blocking collectives: 71.8 us -> 56.2 us
  starting transfers between devices: 7.05 us -> 20.3 us
  local copies, waits for them, and re-layouts: 8.42 us -> 0.01 us
  waiting for transfers between devices: 14.9 us -> 7.52 us
  between operations: 2.65 us -> 0.71 us
    all_to_all x3 -> x2, blocking collectives: 71.8 us -> 56.2 us  [exchange(): return lax.all_to_all(array, axis, split_axis=0, concat_axis=0, tiled=True)]
    ppermute x0 -> x6, starting transfers between devices: none -> 9.97 us  [the longest x3 5.08 us: spread(): lax.ppermute(block, 'outer', ring(n, False))]
    all_to_all x2, waiting for transfers between devices: 14.9 us -> 5.52 us  [exchange(): return lax.all_to_all(array, axis, split_axis=0, concat_axis=0, tiled=True)]
    unnamed x18 -> x2, local copies, waits for them, and re-layouts: 7.74 us -> 0.01 us
    all_to_all x2, starting transfers between devices: 7.05 us -> 10.4 us  [exchange(): return lax.all_to_all(array, axis, split_axis=0, concat_axis=0, tiled=True)]
    ppermute x0 -> x6, waiting for transfers between devices: none -> 2 us  [the longest x3 1.99 us: spread(): lax.ppermute(block, 'outer', ring(n, False))]
    pallas_call x1, Pallas kernels: 2.4 us -> 0.68 us  [finish(): pl.pallas_call(finish_kernel, out_shape=jax.ShapeDtypeStruct((NB, OUT_ROW...]
    pallas_call x1, Pallas kernels: 1.21 us -> 2.7 us  [pack(): pl.pallas_call(pack_kernel, out_shape=(jax.ShapeDtypeStruct((HEADS, BLOCK...]
  transfers between devices with their start and end apart: 2 -> 8, of which waited for: 1 -> 3; matrix products, arithmetic and copies ran while one was open for 0% -> 0% of each run, Pallas kernels for 13% -> 16%
where the time goes in v2:
time: 110 us
  blocking collectives  56.2 us (51%)
  Pallas kernels  24.7 us (22%)
  starting transfers between devices  20.3 us (18%)
  waiting for transfers between devices  7.52 us (7%)
    all_to_all x2, blocking collectives, exchange(): return lax.all_to_all(array, axis, split_axis=0, concat_axis=0, tiled=True)  56.2 us
    pallas_call x1, Pallas kernels, near_part(): pl.pallas_call(near_kernel, out_shape=(jax.ShapeDtypeStruct((NB, HD, BLOC...  16.5 us
    all_to_all x2, starting transfers between devices, exchange(): return lax.all_to_all(array, axis, split_axis=0, concat_axis=0, tiled=True)  10.4 us
    all_to_all x2, waiting for transfers between devices, exchange(): return lax.all_to_all(array, axis, split_axis=0, concat_axis=0, tiled=True)  5.52 us
    ppermute x3, starting transfers between devices, spread(): lax.ppermute(block, 'outer', ring(n, False))  5.08 us
    ppermute x3, starting transfers between devices, spread(): lax.ppermute(row, 'outer', ring(n, True))  4.89 us
    pallas_call x1, Pallas kernels, far_part(): pl.pallas_call(far_kernel, out_shape=(jax.ShapeDtypeStruct((NB, BLOCK, 2...  3.13 us
    pallas_call x1, Pallas kernels, pack(): pl.pallas_call(pack_kernel, out_shape=(jax.ShapeDtypeStruct((HEADS, BLOCK...  2.7 us
  transfers between devices with their start and end apart: 8, of which 3 were waited for; matrix products, arithmetic and copies ran while one was open for 0% of the time, Pallas kernels for 16%

profile of v2, /device:TPU:1, one launch (start us, length us, event | category | flops | bytes accessed | tf_op | source)
XLA Modules:
  0.0 109.5 jit_solution(8140364689955935210)
XLA Ops:
  0.6 2.7 %pack_heads.1 = (bf16[16,128,128]{2,1,0:T(8,128)(2,1)}, bf16[16,144,128]{2,1,0:T(8,128)(2,1)}) custom-call(bf16[128,1024]{1,0:T(8,128)(2,1)} %q_in.1, bf16[128,1024]{1,0:T(8,128)(2,1)} %k_in.1, bf16[128,1024]{1,0:T(8,128)(2,1)} %v_in.1, bf16[128,1024]{1,0:T(8,128)(2,1)} %o_in.1, bf16[128,1024]{1,0:T(8,128)(2,1)} %g_in.1), custom_call_target="tpu_custom_call" | custom-call | flops 10000000 | bytes 2000000 | tf_op jit(solution)/shard_map/pack_heads/pallas_call | solution.py:89
  3.3 27.3 %all_to_all.20.kv_ref = bf16[16,128,128]{2,1,0:T(8,128)(2,1)S(1)} all-to-all(bf16[16,128,128]{2,1,0:T(8,128)(2,1)} %get-tuple-element.9), channel_id=1, replica_groups=mesh['outer'=16,'inner'=16] {'inner'}, dimensions={0} | all-to-all | bytes 1048576 | tf_op jit(solution)/shard_map/all_to_all | solution.py:357
  30.6 0.0 copy-start
  30.6 3.6 %all-to-all-start.1 = ((bf16[16,144,128]{2,1,0:T(8,128)(2,1)}), bf16[16,144,128]{2,1,0:T(8,128)(2,1)S(1)}, u32[]{:S(2)}, u32[]{:S(2)}) async-start(bf16[16,144,128]{2,1,0:T(8,128)(2,1)} %get-tuple-element.10), calls=%async_computation.1 | async-start | bytes 1179648 | tf_op jit(solution)/shard_map/all_to_all | solution.py:357
  34.3 0.0 copy-done
  34.3 0.6 pick_block.1
  34.8 1.4 %collective-permute-start.2 = (bf16[128,128]{1,0:T(8,128)(2,1)S(1)}, bf16[128,128]{1,0:T(8,128)(2,1)S(1)}, u32[]{:S(2)}, u32[]{:S(2)}) collective-permute-start(bf16[128,128]{1,0:T(8,128)(2,1)S(1)} %pick_block.1), channel_id=1, source_target_pairs={{48,0},{0,16},{16,32},{32,48},{112,64},{64,80},{80,96},{96,112},{1... | collective-permute-start | bytes 98312 | tf_op jit(solution)/shard_map/ppermute | solution.py:369
  36.2 2.6 %collective-permute-start.1 = (bf16[128,128]{1,0:T(8,128)(2,1)S(1)}, bf16[128,128]{1,0:T(8,128)(2,1)S(1)}, u32[]{:S(2)}, u32[]{:S(2)}) collective-permute-start(bf16[128,128]{1,0:T(8,128)(2,1)S(1)} %pick_block.1), channel_id=1, source_target_pairs={{32,0},{48,16},{0,32},{16,48},{96,64},{112,80},{64,96},{80,112},{1... | collective-permute-start | bytes 98312 | tf_op jit(solution)/shard_map/ppermute | solution.py:369
  38.8 1.1 collective-permute-start
  39.9 0.0 collective-permute-done.2
  39.9 1.5 %collective-permute-done.1 = bf16[128,128]{1,0:T(8,128)(2,1)S(1)} collective-permute-done((bf16[128,128]{1,0:T(8,128)(2,1)S(1)}, bf16[128,128]{1,0:T(8,128)(2,1)S(1)}, u32[]{:S(2)}, u32[]{:S(2)}) %collective-permute-start.1) | collective-permute-done | bytes 32800 | tf_op jit(solution)/shard_map/ppermute | solution.py:369
  41.5 0.5 collective-permute-done
  41.9 1.3 %collective-permute-start.5 = (bf16[4,128,128]{2,1,0:T(8,128)(2,1)S(1)}, bf16[4,128,128]{2,1,0:T(8,128)(2,1)S(1)}, u32[]{:S(2)}, u32[]{:S(2)}) collective-permute-start(bf16[4,128,128]{2,1,0:T(8,128)(2,1)S(1)} %pad_maximum_fusion.far0), channel_id=1, source_target_pairs={{192,0},{208,16},{224,32},{240,48},{0,64},{16,80},{32,96},{48,112}... | collective-permute-start | bytes 393224 | tf_op jit(solution)/shard_map/ppermute | solution.py:370
  43.2 2.5 %collective-permute-start.4 = (bf16[4,128,128]{2,1,0:T(8,128)(2,1)S(1)}, bf16[4,128,128]{2,1,0:T(8,128)(2,1)S(1)}, u32[]{:S(2)}, u32[]{:S(2)}) collective-permute-start(bf16[4,128,128]{2,1,0:T(8,128)(2,1)S(1)} %pad_maximum_fusion.far0), channel_id=1, source_target_pairs={{128,0},{144,16},{160,32},{176,48},{192,64},{208,80},{224,96},{240... | collective-permute-start | bytes 393224 | tf_op jit(solution)/shard_map/ppermute | solution.py:370
  45.7 1.2 %collective-permute-start.3 = (bf16[4,128,128]{2,1,0:T(8,128)(2,1)S(1)}, bf16[4,128,128]{2,1,0:T(8,128)(2,1)S(1)}, u32[]{:S(2)}, u32[]{:S(2)}) collective-permute-start(bf16[4,128,128]{2,1,0:T(8,128)(2,1)S(1)} %pad_maximum_fusion.far0), channel_id=1, source_target_pairs={{64,0},{80,16},{96,32},{112,48},{128,64},{144,80},{160,96},{176,11... | collective-permute-start | bytes 393224 | tf_op jit(solution)/shard_map/ppermute | solution.py:370
  46.8 5.5 %all-to-all-done.1.qg_ref = bf16[16,144,128]{2,1,0:T(8,128)(2,1)S(1)} async-done(((bf16[16,144,128]{2,1,0:T(8,128)(2,1)}), bf16[16,144,128]{2,1,0:T(8,128)(2,1)S(1)}, u32[]{:S(2)}, u32[]{:S(2)}) %all-to-all-start.1) | async-done | bytes 589856 | tf_op jit(solution)/shard_map/all_to_all | solution.py:357
  52.3 0.0 collective-permute-done.5.far3
  52.3 0.0 collective-permute-done.4.far2
  52.3 0.0 collective-permute-done.3.far1
  52.4 3.1 %far_part.1 = (bf16[16,128,128]{2,1,0:T(8,128)(2,1)}, f32[72,128]{1,0:T(8,128)S(1)}) custom-call(s32[16]{0:T(128)S(1)} %copy-done, bf16[16,128,128]{2,1,0:T(8,128)(2,1)S(1)} %all_to_all.20.kv_ref, bf16[16,144,128]{2,1,0:T(8,128)(2,1)S(1)} %all-to-all-done.1.qg_ref, bf16[4,128,128]{2,1,0:T(8,128)(2,1)S(1)} %pad_maximum_fusion.far0, ...), custom_call_target="tpu_custom_call" | custom-call | flops 2000000000 | bytes 2000000 | tf_op jit(solution)/shard_map/far_part/pallas_call | solution.py:199
  55.5 6.8 %all-to-all-start.2 = ((bf16[16,128,128]{2,1,0:T(8,128)(2,1)}), bf16[16,128,128]{2,1,0:T(8,128)(2,1)S(1)}, u32[]{:S(2)}, u32[]{:S(2)}) async-start(bf16[16,128,128]{2,1,0:T(8,128)(2,1)} %get-tuple-element.14), calls=%async_computation.2 | async-start | bytes 1048576 | tf_op jit(solution)/shard_map/all_to_all | solution.py:357
  62.2 16.5 %near_part.1 = (bf16[16,64,128]{2,1,0:T(8,128)(2,1)S(1)}, f32[2048,128]{1,0:T(8,128)S(1)}) custom-call(s32[16]{0:T(128)S(1)} %copy-done, bf16[16,128,128]{2,1,0:T(8,128)(2,1)S(1)} %all_to_all.20.kv_ref, bf16[16,144,128]{2,1,0:T(8,128)(2,1)S(1)} %all-to-all-done.1.qg_ref, f32[72,128]{1,0:T(8,128)S(1)} %get-tuple-element.11.stat_ref), custom_call_target="tpu_custom_call" | custom-call | flops 15000000512 | bytes 4000000 | tf_op jit(solution)/shard_map/near_part/pallas_call | solution.py:285
  78.8 0.0 all-to-all-done.2.parts_ref
  78.8 0.7 finish_picked.1
  79.5 28.9 %all_to_all.21.in_ref = bf16[16,192,128]{2,1,0:T(8,128)(2,1)S(1)} all-to-all(bf16[16,192,128]{2,1,0:T(8,128)(2,1)S(1)} %finish_picked.1), channel_id=1, replica_groups=mesh['outer'=16,'inner'=16] {'inner'}, dimensions={0} | all-to-all | bytes 1572864 | tf_op jit(solution)/shard_map/all_to_all | solution.py:357
  108.4 1.1 %unpack_heads.1 = (bf16[128,1024]{1,0:T(8,128)(2,1)}, bf16[128,1024]{1,0:T(8,128)(2,1)}, bf16[128,1024]{1,0:T(8,128)(2,1)}) custom-call(bf16[16,192,128]{2,1,0:T(8,128)(2,1)S(1)} %all_to_all.21.in_ref), custom_call_target="tpu_custom_call" | custom-call | flops 1000000 | bytes 2000000 | tf_op jit(solution)/shard_map/unpack_heads/pallas_call | solution.py:345
  (1 shorter events, 0.0 us)
Async XLA Ops:
  30.6 3.6 %copy-start = (s32[16]{0:T(128)S(1)}, s32[16]{0:T(128)}, u32[]{:S(2)}) copy-start(s32[16]{0:T(128)} %offs_ref.7) | copy-start | bytes 196
  30.6 21.7 %all-to-all-start.1 = ((bf16[16,144,128]{2,1,0:T(8,128)(2,1)}), bf16[16,144,128]{2,1,0:T(8,128)(2,1)S(1)}, u32[]{:S(2)}, u32[]{:S(2)}) async-start(bf16[16,144,128]{2,1,0:T(8,128)(2,1)} %get-tuple-element.10), calls=%async_computation.1 | async-start | bytes 1179648 | tf_op jit(solution)/shard_map/all_to_all | solution.py:357
  34.8 5.1 %collective-permute-start.2 = (bf16[128,128]{1,0:T(8,128)(2,1)S(1)}, bf16[128,128]{1,0:T(8,128)(2,1)S(1)}, u32[]{:S(2)}, u32[]{:S(2)}) collective-permute-start(bf16[128,128]{1,0:T(8,128)(2,1)S(1)} %pick_block.1), channel_id=1, source_target_pairs={{48,0},{0,16},{16,32},{32,48},{112,64},{64,80},{80,96},{96,112},{1... | collective-permute-start | bytes 98312 | tf_op jit(solution)/shard_map/ppermute | solution.py:369
  36.2 5.2 %collective-permute-start.1 = (bf16[128,128]{1,0:T(8,128)(2,1)S(1)}, bf16[128,128]{1,0:T(8,128)(2,1)S(1)}, u32[]{:S(2)}, u32[]{:S(2)}) collective-permute-start(bf16[128,128]{1,0:T(8,128)(2,1)S(1)} %pick_block.1), channel_id=1, source_target_pairs={{32,0},{48,16},{0,32},{16,48},{96,64},{112,80},{64,96},{80,112},{1... | collective-permute-start | bytes 98312 | tf_op jit(solution)/shard_map/ppermute | solution.py:369
  38.8 3.1 %collective-permute-start = (bf16[128,128]{1,0:T(8,128)(2,1)S(1)}, bf16[128,128]{1,0:T(8,128)(2,1)S(1)}, u32[]{:S(2)}, u32[]{:S(2)}) collective-permute-start(bf16[128,128]{1,0:T(8,128)(2,1)S(1)} %pick_block.1), channel_id=1, source_target_pairs={{16,0},{32,16},{48,32},{0,48},{80,64},{96,80},{112,96},{64,112},{1... | collective-permute-start | bytes 98312 | tf_op jit(solution)/shard_map/ppermute | solution.py:369
  41.9 10.4 %collective-permute-start.5 = (bf16[4,128,128]{2,1,0:T(8,128)(2,1)S(1)}, bf16[4,128,128]{2,1,0:T(8,128)(2,1)S(1)}, u32[]{:S(2)}, u32[]{:S(2)}) collective-permute-start(bf16[4,128,128]{2,1,0:T(8,128)(2,1)S(1)} %pad_maximum_fusion.far0), channel_id=1, source_target_pairs={{192,0},{208,16},{224,32},{240,48},{0,64},{16,80},{32,96},{48,112}... | collective-permute-start | bytes 393224 | tf_op jit(solution)/shard_map/ppermute | solution.py:370
  43.2 9.1 %collective-permute-start.4 = (bf16[4,128,128]{2,1,0:T(8,128)(2,1)S(1)}, bf16[4,128,128]{2,1,0:T(8,128)(2,1)S(1)}, u32[]{:S(2)}, u32[]{:S(2)}) collective-permute-start(bf16[4,128,128]{2,1,0:T(8,128)(2,1)S(1)} %pad_maximum_fusion.far0), channel_id=1, source_target_pairs={{128,0},{144,16},{160,32},{176,48},{192,64},{208,80},{224,96},{240... | collective-permute-start | bytes 393224 | tf_op jit(solution)/shard_map/ppermute | solution.py:370
  45.7 6.7 %collective-permute-start.3 = (bf16[4,128,128]{2,1,0:T(8,128)(2,1)S(1)}, bf16[4,128,128]{2,1,0:T(8,128)(2,1)S(1)}, u32[]{:S(2)}, u32[]{:S(2)}) collective-permute-start(bf16[4,128,128]{2,1,0:T(8,128)(2,1)S(1)} %pad_maximum_fusion.far0), channel_id=1, source_target_pairs={{64,0},{80,16},{96,32},{112,48},{128,64},{144,80},{160,96},{176,11... | collective-permute-start | bytes 393224 | tf_op jit(solution)/shard_map/ppermute | solution.py:370
  55.5 23.3 %all-to-all-start.2 = ((bf16[16,128,128]{2,1,0:T(8,128)(2,1)}), bf16[16,128,128]{2,1,0:T(8,128)(2,1)S(1)}, u32[]{:S(2)}, u32[]{:S(2)}) async-start(bf16[16,128,128]{2,1,0:T(8,128)(2,1)} %get-tuple-element.14), calls=%async_computation.2 | async-start | bytes 1048576 | tf_op jit(solution)/shard_map/all_to_all | solution.py:357

commit v3 on v2

v3 whole, which is shorter than its diff:
```python
import jax
import jax.numpy as jnp
from jax import lax
from jax.experimental import pallas as pl
from jax.experimental.pallas import tpu as pltpu
from jax.sharding import PartitionSpec as P

HEADS = 16
HD = 64
BLOCK = 128
NB = 16
RING = 4
GROUP = 4
GROUPS = HEADS // GROUP
GROUP_COLS = GROUP * HD
SEG = NB * BLOCK
CHUNK = 256
BF = jnp.bfloat16
F32 = jnp.float32
VMEM = pl.BlockSpec(memory_space=pltpu.VMEM)
SMEM = pl.BlockSpec(memory_space=pltpu.SMEM)
QG_ROWS = BLOCK + 16
OUT_ROWS = BLOCK + HD


def params(mib):
    return pltpu.CompilerParams(vmem_limit_bytes=mib * 1024 * 1024)


def cost(flops, nbytes, exps=0):
    return pl.CostEstimate(flops=flops, bytes_accessed=nbytes, transcendentals=exps)


def dot(a, b):
    return jnp.dot(a, b, preferred_element_type=F32)


def dot_nt(a, b):
    return lax.dot_general(a, b, (((1,), (1,)), ((), ())), preferred_element_type=F32)


def split3(x):
    high = x.astype(BF)
    rest = x - high.astype(F32)
    mid = rest.astype(BF)
    low = (rest - mid.astype(F32)).astype(BF)
    return high, mid, low


ANY = pl.BlockSpec(memory_space=pl.ANY)


def fetch(pairs, sems):
    copies = [
        pltpu.make_async_copy(source, target, sems.at[n]) for n, (source, target) in enumerate(pairs)
    ]
    for copy in copies:
        copy.start()
    return copies


def half_of(ref, head):
    start = head * HD
    return ref[:, start : start + HD]


def pack_kv_kernel(k_in, v_in, kv_out, k_ref, v_ref, kv_ref, sems, out_sems):
    copies = []
    for n in range(GROUPS):
        cols = pl.ds(n * GROUP_COLS, GROUP_COLS)
        pairs = ((k_in.at[:, cols], k_ref.at[:, cols]), (v_in.at[:, cols], v_ref.at[:, cols]))
        copies.append(fetch(pairs, sems.at[n]))
    outs = []
    for n in range(GROUPS):
        for copy in copies[n]:
            copy.wait()
        for head in range(n * GROUP, (n + 1) * GROUP):
            kv_ref[head] = jnp.concatenate([half_of(k_ref, head), half_of(v_ref, head)], axis=1)
        heads = pl.ds(n * GROUP, GROUP)
        outs.append(pltpu.make_async_copy(kv_ref.at[heads], kv_out.at[heads], out_sems.at[n]))
        outs[n].start()
    for out in outs:
        out.wait()


def pack_kv(keys, values):
    return pl.pallas_call(
        pack_kv_kernel,
        out_shape=jax.ShapeDtypeStruct((HEADS, BLOCK, 2 * HD), BF),
        in_specs=[ANY] * 2,
        out_specs=ANY,
        scratch_shapes=[pltpu.VMEM((BLOCK, HEADS * HD), BF)] * 2
        + [
            pltpu.VMEM((HEADS, BLOCK, 2 * HD), BF),
            pltpu.SemaphoreType.DMA((GROUPS, 2)),
            pltpu.SemaphoreType.DMA((GROUPS,)),
        ],
        compiler_params=params(60),
        cost_estimate=cost(10**6, 10**6),
        name="pack_keys_values",
    )(keys, values)


def pack_qg_kernel(q_in, o_in, g_in, qg_ref, q_ref, o_ref, g_ref, sems):
    copies = fetch(((g_in, g_ref), (o_in, o_ref), (q_in, q_ref)), sems)
    copies[0].wait()
    copies[1].wait()
    head_of = lax.broadcasted_iota(jnp.int32, (HEADS, HEADS * HD), 1) // HD
    mine = head_of == lax.broadcasted_iota(jnp.int32, (HEADS, HEADS * HD), 0)
    ones = jnp.where(mine, 1.0, 0.0).astype(BF)
    product = g_ref[...].astype(F32) * o_ref[...].astype(F32)
    high = product.astype(BF)
    low = (product - high.astype(F32)).astype(BF)
    terms = dot_nt(ones, high) + dot_nt(ones, low)
    parts = [part.astype(F32) for part in split3(terms)]
    row = lax.broadcasted_iota(jnp.int32, (16, BLOCK), 0)
    copies[2].wait()
    for head in range(HEADS):
        q = (half_of(q_ref, head).astype(F32) * (HD**-0.5)).astype(BF)
        qg_ref[head, :BLOCK, :] = jnp.concatenate([q, half_of(g_ref, head)], axis=1)
        tail = jnp.zeros((16, BLOCK), F32)
        for n, part in enumerate(parts):
            tail = jnp.where(row == n, part[head : head + 1, :], tail)
        qg_ref[head, BLOCK:, :] = tail.astype(BF)


def pack_qg(queries, saved_out, out_grad):
    return pl.pallas_call(
        pack_qg_kernel,
        out_shape=jax.ShapeDtypeStruct((HEADS, QG_ROWS, 2 * HD), BF),
        in_specs=[ANY] * 3,
        out_specs=VMEM,
        scratch_shapes=[pltpu.VMEM((BLOCK, HEADS * HD), BF)] * 3 + [pltpu.SemaphoreType.DMA((3,))],
        compiler_params=params(60),
        cost_estimate=cost(10**7, 2 * 10**6),
        name="pack_queries_grads",
    )(queries, saved_out, out_grad)


def pick_kernel(offs_ref, kv_ref, out_ref):
    out_ref[...] = kv_ref[offs_ref[lax.axis_index("inner")]]


def pick(offsets, kv):
    return pl.pallas_call(
        pick_kernel,
        out_shape=jax.ShapeDtypeStruct(kv.shape[1:], kv.dtype),
        in_specs=[SMEM, VMEM],
        out_specs=VMEM,
        compiler_params=params(4),
        cost_estimate=cost(10**3, 10**5),
        name="pick_block",
    )(offsets, kv)


def block_terms(tail):
    tail = tail.astype(F32)
    return tail[0:1, :] + tail[1:2, :] + tail[2:3, :]


def score_weights(q_turned, g_turned):
    zero = jnp.zeros((HD, BLOCK), BF)
    none = zero if q_turned is None else q_turned
    grad = zero if g_turned is None else g_turned
    return jnp.concatenate(
        [jnp.concatenate([none, zero], axis=1), jnp.concatenate([zero, grad], axis=1)], axis=0
    )


def grad_weights(turned, factor):
    scaled = (turned.astype(F32) * factor).T.astype(BF)
    left = lax.broadcasted_iota(jnp.int32, scaled.shape, 1) < HD
    zero = jnp.zeros_like(scaled)
    return jnp.concatenate(
        [jnp.where(left, zero, scaled), jnp.where(left, scaled, zero)], axis=0
    )


def kv_rows(kv_ref, c):
    per = CHUNK // BLOCK
    return kv_ref[c * per : (c + 1) * per].reshape(CHUNK, 2 * HD)


def fold(x, op):
    return op(x.reshape(-1, 8, x.shape[1]), axis=0)


def prepare_kernel(offs_ref, kv_ref, qg_ref, stat_ref, near_s):
    offset = offs_ref[lax.axis_index("inner")]
    weights = qg_ref[offset, :BLOCK, :].T
    top_half = lax.broadcasted_iota(jnp.int32, weights.shape, 0) < HD
    weights = jnp.where(top_half, weights, jnp.zeros_like(weights))
    top8 = jnp.full((8, BLOCK), -jnp.inf, F32)
    for c in range(SEG // CHUNK):
        near = dot(kv_rows(kv_ref, c), weights)
        near_s[c * CHUNK : (c + 1) * CHUNK, :] = near
        top8 = jnp.maximum(top8, fold(near, jnp.max))
    top = jnp.max(top8, axis=0, keepdims=True)
    sum8 = jnp.zeros((8, BLOCK), F32)
    for c in range(SEG // CHUNK):
        sum8 += fold(jnp.exp(near_s[c * CHUNK : (c + 1) * CHUNK, :] - top), jnp.sum)
    stat_ref[0:1, :] = top
    stat_ref[1:2, :] = jnp.sum(sum8, axis=0, keepdims=True)


def prepare(offsets, kv, qg):
    return pl.pallas_call(
        prepare_kernel,
        out_shape=jax.ShapeDtypeStruct((8, BLOCK), F32),
        in_specs=[SMEM, VMEM, VMEM],
        out_specs=VMEM,
        scratch_shapes=[pltpu.VMEM((SEG, BLOCK), F32)],
        compiler_params=params(20),
        cost_estimate=cost(10**9, 2 * 10**6),
        name="prepare_near",
    )(offsets, kv, qg)


def far_kernel(
    offs_ref, qg_ref, near_ref, far0, far1, far2, far3, part_ref, stat_ref, far_s, ed
):
    offset = offs_ref[lax.axis_index("inner")]
    place = lax.axis_index("outer")
    place_x, place_y = place // RING, place % RING
    fars = (far0, far1, far2, far3)

    def far_rows(c):
        per = CHUNK // BLOCK
        a, b = divmod(c * per, RING)
        return fars[a][b : b + per].reshape(CHUNK, 2 * HD)

    terms = block_terms(qg_ref[offset, BLOCK:, :])
    turned = qg_ref[offset, :BLOCK, :].T
    weights = score_weights(turned[:HD, :], turned[HD:, :])
    near_top = near_ref[0:1, :]
    top8 = jnp.broadcast_to(near_top, (8, BLOCK))
    for c in range(SEG // CHUNK):
        rows = slice(c * CHUNK, (c + 1) * CHUNK)
        far = dot(far_rows(c), weights)
        far_s[rows, :] = far
        top8 = jnp.maximum(top8, fold(far[:, :BLOCK], jnp.max))
    top = jnp.max(top8, axis=0, keepdims=True)
    sum8 = jnp.zeros((8, BLOCK), F32)
    for c in range(SEG // CHUNK):
        rows = slice(c * CHUNK, (c + 1) * CHUNK)
        prob = jnp.exp(far_s[rows, :BLOCK] - top)
        sum8 += fold(prob, jnp.sum)
        ed[rows, :BLOCK] = prob.astype(BF)
        ed[rows, BLOCK:] = (prob * (far_s[rows, BLOCK:] - terms)).astype(BF)
    total = jnp.sum(sum8, axis=0, keepdims=True) + near_ref[1:2, :] * jnp.exp(near_top - top)
    factor = 1.0 / total
    second = grad_weights(turned, factor)
    query_grad = jnp.zeros((HD, BLOCK), F32)
    for c in range(SEG // CHUNK):
        rows = slice(c * CHUNK, (c + 1) * CHUNK)
        both = ed[rows, :]
        grads = dot(both, second).astype(BF)
        for n in range(CHUNK // BLOCK):
            a, b = divmod(c * CHUNK // BLOCK + n, RING)
            owner = (place_x + a) % RING * RING + (place_y + b) % RING
            part_ref[owner] = grads[n * BLOCK : (n + 1) * BLOCK, :]
        query_grad += dot(far_rows(c).T[:HD, :], both[:, BLOCK:])
    stat_ref[0:1, :] = top
    stat_ref[1:2, :] = factor
    stat_ref[8:, :] = query_grad * factor * (HD**-0.5)


def far_part(offsets, qg, near_stat, fars):
    return pl.pallas_call(
        far_kernel,
        out_shape=(
            jax.ShapeDtypeStruct((NB, BLOCK, 2 * HD), BF),
            jax.ShapeDtypeStruct((8 + HD, BLOCK), F32),
        ),
        in_specs=[SMEM] + [VMEM] * 6,
        out_specs=(VMEM, VMEM),
        scratch_shapes=[
            pltpu.VMEM((SEG, 2 * BLOCK), F32),
            pltpu.VMEM((SEG, 2 * BLOCK), BF),
        ],
        compiler_params=params(20),
        cost_estimate=cost(2 * 10**9, 2 * 10**6),
        name="far_part",
    )(offsets, qg, near_stat, *fars)


def near_kernel(
    offs_ref, kv_ref, qg_ref, stat_ref, dq_ref, acc, keys_t, turned_ref, s0, s1, e0, e1, st0, st1
):
    offset = offs_ref[lax.axis_index("inner")]
    score_refs, grad_refs, stats = (s0, s1), (e0, e1), (st0, st1)
    chunks = SEG // CHUNK
    for b in range(NB):
        keys_t[:, b * BLOCK : (b + 1) * BLOCK] = kv_ref[b].T[:HD, :]
        turned_ref[b] = qg_ref[b, :BLOCK, :].T

    def step(j, slot, first, second, third):
        s_now, s_old = score_refs[slot], score_refs[1 - slot]
        e_now, e_old = grad_refs[1 - slot], grad_refs[slot]
        st_now, st_old = stats[slot], stats[1 - slot]
        top8 = jnp.full((8, BLOCK), -jnp.inf, F32)
        sum8 = jnp.zeros((8, BLOCK), F32)
        query_grad = jnp.zeros((HD, BLOCK), F32)
        if first or second:
            weights = score_weights(
                turned_ref[j, :HD, :] if first else None,
                turned_ref[j - 1, HD:, :] if second else None,
            )
        if second:
            terms = block_terms(qg_ref[j - 1, BLOCK:, :])
            top = st_old[0:1, :]
        if third:
            factor = st_now[1:2, :]
            gweights = grad_weights(turned_ref[j - 2], factor)
        for c in range(chunks + 1):
            if c < chunks and (first or second):
                rows = slice(c * CHUNK, (c + 1) * CHUNK)
                score = dot(kv_rows(kv_ref, c), weights)
                if first:
                    s_now[rows, :] = score[:, :BLOCK]
                    top8 = jnp.maximum(top8, fold(score[:, :BLOCK], jnp.max))
                if second:
                    prob = jnp.exp(s_old[rows, :] - top)
                    sum8 += fold(prob, jnp.sum)
                    e_now[rows, :BLOCK] = prob.astype(BF)
                    e_now[rows, BLOCK:] = (prob * (score[:, BLOCK:] - terms)).astype(BF)
            if c > 0 and third:
                rows = slice((c - 1) * CHUNK, c * CHUNK)
                both = e_old[rows, :]
                acc[rows, :] += dot(both, gweights)
                query_grad += dot(keys_t[:, rows], both[:, BLOCK:])
        if third:
            query_grad = query_grad * (factor * (HD**-0.5))
            query_grad += jnp.where((j - 2) == offset, stat_ref[8:, :], 0.0)
            dq_ref[j - 2] = query_grad.astype(BF)
        if first:
            top = jnp.max(top8, axis=0, keepdims=True)
            st_now[0:1, :] = jnp.where(j == offset, stat_ref[0:1, :], top)
        if second:
            total = jnp.sum(sum8, axis=0, keepdims=True)
            st_old[1:2, :] = jnp.where((j - 1) == offset, stat_ref[1:2, :], 1.0 / total)

    step(0, 0, True, False, False)
    step(1, 1, True, True, False)
    acc[...] = jnp.zeros_like(acc)

    def pair(i, carry):
        step(2 * i, 0, True, True, True)
        step(2 * i + 1, 1, True, True, True)
        return carry

    lax.fori_loop(1, NB // 2, pair, 0)
    step(NB, 0, False, True, True)
    step(NB + 1, 1, False, False, True)


def near_part(offsets, kv, qg, stat):
    return pl.pallas_call(
        near_kernel,
        out_shape=(
            jax.ShapeDtypeStruct((NB, HD, BLOCK), BF),
            jax.ShapeDtypeStruct((SEG, 2 * HD), F32),
        ),
        in_specs=[SMEM] + [VMEM] * 3,
        out_specs=(VMEM, VMEM),
        scratch_shapes=[
            pltpu.VMEM((HD, SEG), BF),
            pltpu.VMEM((NB, 2 * HD, BLOCK), BF),
            pltpu.VMEM((SEG, BLOCK), F32),
            pltpu.VMEM((SEG, BLOCK), F32),
            pltpu.VMEM((SEG, 2 * BLOCK), BF),
            pltpu.VMEM((SEG, 2 * BLOCK), BF),
            pltpu.VMEM((8, BLOCK), F32),
            pltpu.VMEM((8, BLOCK), F32),
        ],
        compiler_params=params(28),
        cost_estimate=cost(15 * 10**9, 4 * 10**6, SEG * SEG),
        name="near_part",
    )(offsets, kv, qg, stat)


def finish_kernel(offs_ref, dq_ref, acc, parts_ref, out_ref):
    offset = offs_ref[lax.axis_index("inner")]
    for b in range(NB):
        out_ref[b, :BLOCK, :] = acc[b * BLOCK : (b + 1) * BLOCK, :].astype(BF)
        out_ref[b, BLOCK:, :] = dq_ref[b]
    total = acc[pl.ds(pl.multiple_of(offset * BLOCK, BLOCK), BLOCK), :]
    for n in range(NB):
        total += parts_ref[n].astype(F32)
    out_ref[offset, :BLOCK, :] = total.astype(BF)


def finish(offsets, dq, sums, parts):
    return pl.pallas_call(
        finish_kernel,
        out_shape=jax.ShapeDtypeStruct((NB, OUT_ROWS, BLOCK), BF),
        in_specs=[SMEM, VMEM, VMEM, VMEM],
        out_specs=VMEM,
        compiler_params=params(16),
        cost_estimate=cost(10**6, 10**6),
        name="finish_picked",
    )(offsets, dq, sums, parts)


def unpack_kernel(in_ref, q_out, k_out, v_out, q_ref, k_ref, v_ref, sems):
    outs = []
    for n in range(GROUPS):
        for pair in range(n * GROUP // 2, (n + 1) * GROUP // 2):
            cols = slice(pair * 2 * HD, (pair + 1) * 2 * HD)
            one, two = in_ref[2 * pair, :BLOCK, :], in_ref[2 * pair + 1, :BLOCK, :]
            k_ref[:, cols] = jnp.concatenate([one[:, :HD], two[:, :HD]], axis=1)
            v_ref[:, cols] = jnp.concatenate([one[:, HD:], two[:, HD:]], axis=1)
            turned = jnp.concatenate(
                [in_ref[2 * pair, BLOCK:, :], in_ref[2 * pair + 1, BLOCK:, :]], axis=0
            )
            q_ref[:, cols] = turned.T
        cols = pl.ds(n * GROUP_COLS, GROUP_COLS)
        pairs = [(ref.at[:, cols], out.at[:, cols]) for ref, out in ((q_ref, q_out), (k_ref, k_out), (v_ref, v_out))]
        outs += fetch(pairs, sems.at[n])
    for out in outs:
        out.wait()


def unpack(block):
    shape = jax.ShapeDtypeStruct((BLOCK, HEADS * HD), BF)
    return pl.pallas_call(
        unpack_kernel,
        out_shape=(shape, shape, shape),
        in_specs=[VMEM],
        out_specs=(ANY, ANY, ANY),
        scratch_shapes=[pltpu.VMEM((BLOCK, HEADS * HD), BF)] * 3
        + [pltpu.SemaphoreType.DMA((GROUPS, 3))],
        compiler_params=params(16),
        cost_estimate=cost(10**6, 2 * 10**6),
        name="unpack_heads",
    )(block)


def exchange(array, axis):
    return lax.all_to_all(array, axis, split_axis=0, concat_axis=0, tiled=True)


def spread(block):
    def ring(step, along_x):
        pairs = []
        for x in range(RING):
            for y in range(RING):
                source = (x + step) % RING * RING + y if along_x else x * RING + (y + step) % RING
                pairs.append((source, x * RING + y))
        return pairs

    row = jnp.stack([block] + [lax.ppermute(block, "outer", ring(n, False)) for n in (1, 2, 3)])
    return [row] + [lax.ppermute(row, "outer", ring(n, True)) for n in (1, 2, 3)]


def on_device(queries, keys, values, saved_out, out_grad, offsets):
    kv = exchange(pack_kv(keys, values), "inner")
    qg = pack_qg(queries, saved_out, out_grad)
    fars = spread(pick(offsets, kv))
    qg = exchange(qg, "inner")
    near_stat = prepare(offsets, kv, qg)
    parts, stat = far_part(offsets, qg, near_stat, fars)
    parts = exchange(parts, "outer")
    dq, sums = near_part(offsets, kv, qg, stat)
    whole = finish(offsets, dq, sums, parts)
    return unpack(exchange(whole, "inner"))


def solution(mesh):
    rows = P(("outer", "inner"), None)
    return jax.shard_map(
        on_device,
        mesh=mesh,
        in_specs=(rows, rows, rows, rows, rows, P()),
        out_specs=(rows, rows, rows),
        check_vma=False,
    )
```

time: 110 us -> 105 us (0.955)
  blocking collectives: 56.2 us -> 27.8 us
  waiting for transfers between devices: 7.52 us -> 22.5 us
  starting transfers between devices: 20.3 us -> 30.2 us
    all_to_all x2 -> x1, blocking collectives: 56.2 us -> 27.8 us  [exchange(): return lax.all_to_all(array, axis, split_axis=0, concat_axis=0, tiled=True)]
    all_to_all x2 -> x3, waiting for transfers between devices: 5.52 us -> 20.5 us  [exchange(): return lax.all_to_all(array, axis, split_axis=0, concat_axis=0, tiled=True)]
    all_to_all x2 -> x3, starting transfers between devices: 10.4 us -> 20.2 us  [exchange(): return lax.all_to_all(array, axis, split_axis=0, concat_axis=0, tiled=True)]
    pallas_call x1, Pallas kernels: 16.5 us -> 13 us  [near_part(): pl.pallas_call(near_kernel, out_shape=(jax.ShapeDtypeStruct((NB, HD, BLOC...]
    pallas_call x1 -> x3, Pallas kernels: 2.7 us -> 5.48 us  [the longest x1 2.36 us: pack_qg(): pl.pallas_call(pack_qg_kernel, out_shape=jax.ShapeDtypeStruct((HEADS, QG_...]
  transfers between devices with their start and end apart: 8 -> 9, of which waited for: 3 -> 4; matrix products, arithmetic and copies ran while one was open for 0% -> 0% of each run, Pallas kernels for 16% -> 16%
where the time goes in v3:
time: 105 us
  starting transfers between devices  30.2 us (29%)
  blocking collectives  27.8 us (26%)
  Pallas kernels  23.6 us (22%)
  waiting for transfers between devices  22.5 us (21%)
    all_to_all x1, blocking collectives, exchange(): return lax.all_to_all(array, axis, split_axis=0, concat_axis=0, tiled=True)  27.8 us
    all_to_all x3, waiting for transfers between devices, exchange(): return lax.all_to_all(array, axis, split_axis=0, concat_axis=0, tiled=True)  20.5 us
    all_to_all x3, starting transfers between devices, exchange(): return lax.all_to_all(array, axis, split_axis=0, concat_axis=0, tiled=True)  20.2 us
    pallas_call x1, Pallas kernels, near_part(): pl.pallas_call(near_kernel, out_shape=(jax.ShapeDtypeStruct((NB, HD, BLOC...  13 us
    ppermute x3, starting transfers between devices, spread(): lax.ppermute(block, 'outer', ring(n, False))  5.08 us
    ppermute x3, starting transfers between devices, spread(): lax.ppermute(row, 'outer', ring(n, True))  4.89 us
    pallas_call x1, Pallas kernels, far_part(): pl.pallas_call(far_kernel, out_shape=(jax.ShapeDtypeStruct((NB, BLOCK, 2...  2.86 us
    pallas_call x1, Pallas kernels, pack_qg(): pl.pallas_call(pack_qg_kernel, out_shape=jax.ShapeDtypeStruct((HEADS, QG_...  2.36 us
  transfers between devices with their start and end apart: 9, of which 4 were waited for; matrix products, arithmetic and copies ran while one was open for 0% of the time, Pallas kernels for 16%

profile of v3, /device:TPU:1, one launch (start us, length us, event | category | flops | bytes accessed | tf_op | source)
XLA Modules:
  0.0 104.9 jit_solution(10675664355871787525)
XLA Ops:
  0.6 2.1 %pack_keys_values.1 = bf16[16,128,128]{2,1,0:T(8,128)(2,1)} custom-call(bf16[128,1024]{1,0:T(8,128)(2,1)} %k_in.1, bf16[128,1024]{1,0:T(8,128)(2,1)} %v_in.1), custom_call_target="tpu_custom_call" | custom-call | flops 1000000 | bytes 1000000 | tf_op jit(solution)/shard_map/pack_keys_values/pallas_call | solution.py:87
  2.7 10.0 %all-to-all-start = ((bf16[16,128,128]{2,1,0:T(8,128)(2,1)}), bf16[16,128,128]{2,1,0:T(8,128)(2,1)S(1)}, u32[]{:S(2)}, u32[]{:S(2)}) async-start(bf16[16,128,128]{2,1,0:T(8,128)(2,1)} %pack_keys_values.1), calls=%async_computation | async-start | bytes 1048576 | tf_op jit(solution)/shard_map/all_to_all | solution.py:440
  12.7 2.4 %pack_queries_grads.1 = bf16[16,144,128]{2,1,0:T(8,128)(2,1)} custom-call(bf16[128,1024]{1,0:T(8,128)(2,1)} %q_in.1, bf16[128,1024]{1,0:T(8,128)(2,1)} %o_in.1, bf16[128,1024]{1,0:T(8,128)(2,1)} %g_in.1), custom_call_target="tpu_custom_call" | custom-call | flops 10000000 | bytes 2000000 | tf_op jit(solution)/shard_map/pack_queries_grads/pallas_call | solution.py:128
  15.1 0.0 copy-start
  15.1 14.9 %all-to-all-done.kv_ref = bf16[16,128,128]{2,1,0:T(8,128)(2,1)S(1)} async-done(((bf16[16,128,128]{2,1,0:T(8,128)(2,1)}), bf16[16,128,128]{2,1,0:T(8,128)(2,1)S(1)}, u32[]{:S(2)}, u32[]{:S(2)}) %all-to-all-start) | async-done | bytes 524320 | tf_op jit(solution)/shard_map/all_to_all | solution.py:440
  30.0 3.5 %all-to-all-start.1 = ((bf16[16,144,128]{2,1,0:T(8,128)(2,1)}), bf16[16,144,128]{2,1,0:T(8,128)(2,1)S(1)}, u32[]{:S(2)}, u32[]{:S(2)}) async-start(bf16[16,144,128]{2,1,0:T(8,128)(2,1)} %pack_queries_grads.1), calls=%async_computation.1 | async-start | bytes 1179648 | tf_op jit(solution)/shard_map/all_to_all | solution.py:440
  33.5 0.0 copy-done
  33.5 0.6 pick_block.1
  34.1 1.4 %collective-permute-start.2 = (bf16[128,128]{1,0:T(8,128)(2,1)S(1)}, bf16[128,128]{1,0:T(8,128)(2,1)S(1)}, u32[]{:S(2)}, u32[]{:S(2)}) collective-permute-start(bf16[128,128]{1,0:T(8,128)(2,1)S(1)} %pick_block.1), channel_id=1, source_target_pairs={{48,0},{0,16},{16,32},{32,48},{112,64},{64,80},{80,96},{96,112},{1... | collective-permute-start | bytes 98312 | tf_op jit(solution)/shard_map/ppermute | solution.py:452
  35.4 2.6 %collective-permute-start.1 = (bf16[128,128]{1,0:T(8,128)(2,1)S(1)}, bf16[128,128]{1,0:T(8,128)(2,1)S(1)}, u32[]{:S(2)}, u32[]{:S(2)}) collective-permute-start(bf16[128,128]{1,0:T(8,128)(2,1)S(1)} %pick_block.1), channel_id=1, source_target_pairs={{32,0},{48,16},{0,32},{16,48},{96,64},{112,80},{64,96},{80,112},{1... | collective-permute-start | bytes 98312 | tf_op jit(solution)/shard_map/ppermute | solution.py:452
  38.1 1.1 %collective-permute-start = (bf16[128,128]{1,0:T(8,128)(2,1)S(1)}, bf16[128,128]{1,0:T(8,128)(2,1)S(1)}, u32[]{:S(2)}, u32[]{:S(2)}) collective-permute-start(bf16[128,128]{1,0:T(8,128)(2,1)S(1)} %pick_block.1), channel_id=1, source_target_pairs={{16,0},{32,16},{48,32},{0,48},{80,64},{96,80},{112,96},{64,112},{1... | collective-permute-start | bytes 98312 | tf_op jit(solution)/shard_map/ppermute | solution.py:452
  39.2 0.0 collective-permute-done.2
  39.2 1.5 %collective-permute-done.1 = bf16[128,128]{1,0:T(8,128)(2,1)S(1)} collective-permute-done((bf16[128,128]{1,0:T(8,128)(2,1)S(1)}, bf16[128,128]{1,0:T(8,128)(2,1)S(1)}, u32[]{:S(2)}, u32[]{:S(2)}) %collective-permute-start.1) | collective-permute-done | bytes 32800 | tf_op jit(solution)/shard_map/ppermute | solution.py:452
  40.7 0.5 collective-permute-done
  41.2 1.3 %collective-permute-start.5 = (bf16[4,128,128]{2,1,0:T(8,128)(2,1)S(1)}, bf16[4,128,128]{2,1,0:T(8,128)(2,1)S(1)}, u32[]{:S(2)}, u32[]{:S(2)}) collective-permute-start(bf16[4,128,128]{2,1,0:T(8,128)(2,1)S(1)} %pad_maximum_fusion.far0), channel_id=1, source_target_pairs={{192,0},{208,16},{224,32},{240,48},{0,64},{16,80},{32,96},{48,112}... | collective-permute-start | bytes 393224 | tf_op jit(solution)/shard_map/ppermute | solution.py:453
  42.5 2.5 %collective-permute-start.4 = (bf16[4,128,128]{2,1,0:T(8,128)(2,1)S(1)}, bf16[4,128,128]{2,1,0:T(8,128)(2,1)S(1)}, u32[]{:S(2)}, u32[]{:S(2)}) collective-permute-start(bf16[4,128,128]{2,1,0:T(8,128)(2,1)S(1)} %pad_maximum_fusion.far0), channel_id=1, source_target_pairs={{128,0},{144,16},{160,32},{176,48},{192,64},{208,80},{224,96},{240... | collective-permute-start | bytes 393224 | tf_op jit(solution)/shard_map/ppermute | solution.py:453
  44.9 1.2 %collective-permute-start.3 = (bf16[4,128,128]{2,1,0:T(8,128)(2,1)S(1)}, bf16[4,128,128]{2,1,0:T(8,128)(2,1)S(1)}, u32[]{:S(2)}, u32[]{:S(2)}) collective-permute-start(bf16[4,128,128]{2,1,0:T(8,128)(2,1)S(1)} %pad_maximum_fusion.far0), channel_id=1, source_target_pairs={{64,0},{80,16},{96,32},{112,48},{128,64},{144,80},{160,96},{176,11... | collective-permute-start | bytes 393224 | tf_op jit(solution)/shard_map/ppermute | solution.py:453
  46.1 5.5 %all-to-all-done.1.qg_ref = bf16[16,144,128]{2,1,0:T(8,128)(2,1)S(1)} async-done(((bf16[16,144,128]{2,1,0:T(8,128)(2,1)}), bf16[16,144,128]{2,1,0:T(8,128)(2,1)S(1)}, u32[]{:S(2)}, u32[]{:S(2)}) %all-to-all-start.1) | async-done | bytes 589856 | tf_op jit(solution)/shard_map/all_to_all | solution.py:440
  51.6 1.1 %prepare_near.1.near_ref = f32[8,128]{1,0:T(8,128)S(1)} custom-call(s32[16]{0:T(128)S(1)} %copy-done, bf16[16,128,128]{2,1,0:T(8,128)(2,1)S(1)} %all-to-all-done.kv_ref, bf16[16,144,128]{2,1,0:T(8,128)(2,1)S(1)} %all-to-all-done.1.qg_ref), custom_call_target="tpu_custom_call" | custom-call | flops 1000000000 | bytes 2000000 | tf_op jit(solution)/shard_map/prepare_near/pallas_call | solution.py:207
  52.6 0.0 collective-permute-done.5.far3
  52.6 0.0 collective-permute-done.4.far2
  52.7 0.0 collective-permute-done.3.far1
  52.7 2.9 %far_part.1 = (bf16[16,128,128]{2,1,0:T(8,128)(2,1)}, f32[72,128]{1,0:T(8,128)S(1)}) custom-call(s32[16]{0:T(128)S(1)} %copy-done, bf16[16,144,128]{2,1,0:T(8,128)(2,1)S(1)} %all-to-all-done.1.qg_ref, f32[8,128]{1,0:T(8,128)S(1)} %prepare_near.1.near_ref, bf16[4,128,128]{2,1,0:T(8,128)(2,1)S(1)} %pad_maximum_fusion.far0, ...), custom_call_target="tpu_custom_call" | custom-call | flops 2000000000 | bytes 2000000 | tf_op jit(solution)/shard_map/far_part/pallas_call | solution.py:269
  55.5 6.8 %all-to-all-start.2 = ((bf16[16,128,128]{2,1,0:T(8,128)(2,1)}), bf16[16,128,128]{2,1,0:T(8,128)(2,1)S(1)}, u32[]{:S(2)}, u32[]{:S(2)}) async-start(bf16[16,128,128]{2,1,0:T(8,128)(2,1)} %get-tuple-element.10), calls=%async_computation.2 | async-start | bytes 1048576 | tf_op jit(solution)/shard_map/all_to_all | solution.py:440
  62.3 13.0 %near_part.1 = (bf16[16,64,128]{2,1,0:T(8,128)(2,1)S(1)}, f32[2048,128]{1,0:T(8,128)S(1)}) custom-call(s32[16]{0:T(128)S(1)} %copy-done, bf16[16,128,128]{2,1,0:T(8,128)(2,1)S(1)} %all-to-all-done.kv_ref, bf16[16,144,128]{2,1,0:T(8,128)(2,1)S(1)} %all-to-all-done.1.qg_ref, f32[72,128]{1,0:T(8,128)S(1)} %get-tuple-element.7.stat_ref), custom_call_target="tpu_custom_call" | custom-call | flops 15000000512 | bytes 4000000 | tf_op jit(solution)/shard_map/near_part/pallas_call | solution.py:358
  75.3 0.0 all-to-all-done.2.parts_ref
  75.3 0.7 finish_picked.1
  76.0 27.8 %all_to_all.20.in_ref = bf16[16,192,128]{2,1,0:T(8,128)(2,1)S(1)} all-to-all(bf16[16,192,128]{2,1,0:T(8,128)(2,1)S(1)} %finish_picked.1), channel_id=1, replica_groups=mesh['outer'=16,'inner'=16] {'inner'}, dimensions={0} | all-to-all | bytes 1572864 | tf_op jit(solution)/shard_map/all_to_all | solution.py:440
  103.8 1.1 %unpack_heads.1 = (bf16[128,1024]{1,0:T(8,128)(2,1)}, bf16[128,1024]{1,0:T(8,128)(2,1)}, bf16[128,1024]{1,0:T(8,128)(2,1)}) custom-call(bf16[16,192,128]{2,1,0:T(8,128)(2,1)S(1)} %all_to_all.20.in_ref), custom_call_target="tpu_custom_call" | custom-call | flops 1000000 | bytes 2000000 | tf_op jit(solution)/shard_map/unpack_heads/pallas_call | solution.py:426
  (1 shorter events, 0.0 us)
Async XLA Ops:
  2.7 27.3 %all-to-all-start = ((bf16[16,128,128]{2,1,0:T(8,128)(2,1)}), bf16[16,128,128]{2,1,0:T(8,128)(2,1)S(1)}, u32[]{:S(2)}, u32[]{:S(2)}) async-start(bf16[16,128,128]{2,1,0:T(8,128)(2,1)} %pack_keys_values.1), calls=%async_computation | async-start | bytes 1048576 | tf_op jit(solution)/shard_map/all_to_all | solution.py:440
  15.1 18.4 %copy-start = (s32[16]{0:T(128)S(1)}, s32[16]{0:T(128)}, u32[]{:S(2)}) copy-start(s32[16]{0:T(128)} %offs_ref.9) | copy-start | bytes 196
  30.0 21.6 %all-to-all-start.1 = ((bf16[16,144,128]{2,1,0:T(8,128)(2,1)}), bf16[16,144,128]{2,1,0:T(8,128)(2,1)S(1)}, u32[]{:S(2)}, u32[]{:S(2)}) async-start(bf16[16,144,128]{2,1,0:T(8,128)(2,1)} %pack_queries_grads.1), calls=%async_computation.1 | async-start | bytes 1179648 | tf_op jit(solution)/shard_map/all_to_all | solution.py:440
  34.1 5.1 %collective-permute-start.2 = (bf16[128,128]{1,0:T(8,128)(2,1)S(1)}, bf16[128,128]{1,0:T(8,128)(2,1)S(1)}, u32[]{:S(2)}, u32[]{:S(2)}) collective-permute-start(bf16[128,128]{1,0:T(8,128)(2,1)S(1)} %pick_block.1), channel_id=1, source_target_pairs={{48,0},{0,16},{16,32},{32,48},{112,64},{64,80},{80,96},{96,112},{1... | collective-permute-start | bytes 98312 | tf_op jit(solution)/shard_map/ppermute | solution.py:452
  35.4 5.2 %collective-permute-start.1 = (bf16[128,128]{1,0:T(8,128)(2,1)S(1)}, bf16[128,128]{1,0:T(8,128)(2,1)S(1)}, u32[]{:S(2)}, u32[]{:S(2)}) collective-permute-start(bf16[128,128]{1,0:T(8,128)(2,1)S(1)} %pick_block.1), channel_id=1, source_target_pairs={{32,0},{48,16},{0,32},{16,48},{96,64},{112,80},{64,96},{80,112},{1... | collective-permute-start | bytes 98312 | tf_op jit(solution)/shard_map/ppermute | solution.py:452
  38.1 3.1 %collective-permute-start = (bf16[128,128]{1,0:T(8,128)(2,1)S(1)}, bf16[128,128]{1,0:T(8,128)(2,1)S(1)}, u32[]{:S(2)}, u32[]{:S(2)}) collective-permute-start(bf16[128,128]{1,0:T(8,128)(2,1)S(1)} %pick_block.1), channel_id=1, source_target_pairs={{16,0},{32,16},{48,32},{0,48},{80,64},{96,80},{112,96},{64,112},{1... | collective-permute-start | bytes 98312 | tf_op jit(solution)/shard_map/ppermute | solution.py:452
  41.2 11.5 %collective-permute-start.5 = (bf16[4,128,128]{2,1,0:T(8,128)(2,1)S(1)}, bf16[4,128,128]{2,1,0:T(8,128)(2,1)S(1)}, u32[]{:S(2)}, u32[]{:S(2)}) collective-permute-start(bf16[4,128,128]{2,1,0:T(8,128)(2,1)S(1)} %pad_maximum_fusion.far0), channel_id=1, source_target_pairs={{192,0},{208,16},{224,32},{240,48},{0,64},{16,80},{32,96},{48,112}... | collective-permute-start | bytes 393224 | tf_op jit(solution)/shard_map/ppermute | solution.py:453
  42.5 10.2 %collective-permute-start.4 = (bf16[4,128,128]{2,1,0:T(8,128)(2,1)S(1)}, bf16[4,128,128]{2,1,0:T(8,128)(2,1)S(1)}, u32[]{:S(2)}, u32[]{:S(2)}) collective-permute-start(bf16[4,128,128]{2,1,0:T(8,128)(2,1)S(1)} %pad_maximum_fusion.far0), channel_id=1, source_target_pairs={{128,0},{144,16},{160,32},{176,48},{192,64},{208,80},{224,96},{240... | collective-permute-start | bytes 393224 | tf_op jit(solution)/shard_map/ppermute | solution.py:453
  44.9 7.8 %collective-permute-start.3 = (bf16[4,128,128]{2,1,0:T(8,128)(2,1)S(1)}, bf16[4,128,128]{2,1,0:T(8,128)(2,1)S(1)}, u32[]{:S(2)}, u32[]{:S(2)}) collective-permute-start(bf16[4,128,128]{2,1,0:T(8,128)(2,1)S(1)} %pad_maximum_fusion.far0), channel_id=1, source_target_pairs={{64,0},{80,16},{96,32},{112,48},{128,64},{144,80},{160,96},{176,11... | collective-permute-start | bytes 393224 | tf_op jit(solution)/shard_map/ppermute | solution.py:453
  55.5 19.7 %all-to-all-start.2 = ((bf16[16,128,128]{2,1,0:T(8,128)(2,1)}), bf16[16,128,128]{2,1,0:T(8,128)(2,1)S(1)}, u32[]{:S(2)}, u32[]{:S(2)}) async-start(bf16[16,128,128]{2,1,0:T(8,128)(2,1)} %get-tuple-element.10), calls=%async_computation.2 | async-start | bytes 1048576 | tf_op jit(solution)/shard_map/all_to_all | solution.py:440

commit v4 on v3

--- a/solution.py
+++ b/solution.py
@@ -10,13 +10,16 @@
 BLOCK = 128
 NB = 16
 RING = 4
-GROUP = 4
+GROUP = 8
 GROUPS = HEADS // GROUP
 GROUP_COLS = GROUP * HD
 SEG = NB * BLOCK
 CHUNK = 256
 BF = jnp.bfloat16
 F32 = jnp.float32
+KV_ORDER = (1, 0)
+QG_ORDER = (1, 0)
+OUT_ORDER = (-1, 15)
 VMEM = pl.BlockSpec(memory_space=pltpu.VMEM)
 SMEM = pl.BlockSpec(memory_space=pltpu.SMEM)
 QG_ROWS = BLOCK + 16
@@ -29,6 +32,11 @@
 
 def cost(flops, nbytes, exps=0):
     return pl.CostEstimate(flops=flops, bytes_accessed=nbytes, transcendentals=exps)
+
+
+def entry(order, i):
+    sign, first = order
+    return (sign * (i - first) + 2 * HEADS) % HEADS
 
 
 def dot(a, b):
@@ -72,11 +80,14 @@
         copies.append(fetch(pairs, sems.at[n]))
     outs = []
     for n in range(GROUPS):
+        group = range(n * GROUP, (n + 1) * GROUP)
         for copy in copies[n]:
             copy.wait()
-        for head in range(n * GROUP, (n + 1) * GROUP):
-            kv_ref[head] = jnp.concatenate([half_of(k_ref, head), half_of(v_ref, head)], axis=1)
-        heads = pl.ds(n * GROUP, GROUP)
+        for head in group:
+            kv_ref[entry(KV_ORDER, head)] = jnp.concatenate(
+                [half_of(k_ref, head), half_of(v_ref, head)], axis=1
+            )
+        heads = pl.ds(min(entry(KV_ORDER, head) for head in group), GROUP)
         outs.append(pltpu.make_async_copy(kv_ref.at[heads], kv_out.at[heads], out_sems.at[n]))
         outs[n].start()
     for out in outs:
@@ -117,11 +128,12 @@
     copies[2].wait()
     for head in range(HEADS):
         q = (half_of(q_ref, head).astype(F32) * (HD**-0.5)).astype(BF)
-        qg_ref[head, :BLOCK, :] = jnp.concatenate([q, half_of(g_ref, head)], axis=1)
+        place = entry(QG_ORDER, head)
+        qg_ref[place, :BLOCK, :] = jnp.concatenate([q, half_of(g_ref, head)], axis=1)
         tail = jnp.zeros((16, BLOCK), F32)
         for n, part in enumerate(parts):
             tail = jnp.where(row == n, part[head : head + 1, :], tail)
-        qg_ref[head, BLOCK:, :] = tail.astype(BF)
+        qg_ref[place, BLOCK:, :] = tail.astype(BF)
 
 
 def pack_qg(queries, saved_out, out_grad):
@@ -138,7 +150,7 @@
 
 
 def pick_kernel(offs_ref, kv_ref, out_ref):
-    out_ref[...] = kv_ref[offs_ref[lax.axis_index("inner")]]
+    out_ref[...] = kv_ref[entry(KV_ORDER, offs_ref[lax.axis_index("inner")])]
 
 
 def pick(offsets, kv):
@@ -185,43 +197,13 @@
     return op(x.reshape(-1, 8, x.shape[1]), axis=0)
 
 
-def prepare_kernel(offs_ref, kv_ref, qg_ref, stat_ref, near_s):
-    offset = offs_ref[lax.axis_index("inner")]
-    weights = qg_ref[offset, :BLOCK, :].T
-    top_half = lax.broadcasted_iota(jnp.int32, weights.shape, 0) < HD
-    weights = jnp.where(top_half, weights, jnp.zeros_like(weights))
-    top8 = jnp.full((8, BLOCK), -jnp.inf, F32)
-    for c in range(SEG // CHUNK):
-        near = dot(kv_rows(kv_ref, c), weights)
-        near_s[c * CHUNK : (c + 1) * CHUNK, :] = near
-        top8 = jnp.maximum(top8, fold(near, jnp.max))
-    top = jnp.max(top8, axis=0, keepdims=True)
-    sum8 = jnp.zeros((8, BLOCK), F32)
-    for c in range(SEG // CHUNK):
-        sum8 += fold(jnp.exp(near_s[c * CHUNK : (c + 1) * CHUNK, :] - top), jnp.sum)
-    stat_ref[0:1, :] = top
-    stat_ref[1:2, :] = jnp.sum(sum8, axis=0, keepdims=True)
-
-
-def prepare(offsets, kv, qg):
-    return pl.pallas_call(
-        prepare_kernel,
-        out_shape=jax.ShapeDtypeStruct((8, BLOCK), F32),
-        in_specs=[SMEM, VMEM, VMEM],
-        out_specs=VMEM,
-        scratch_shapes=[pltpu.VMEM((SEG, BLOCK), F32)],
-        compiler_params=params(20),
-        cost_estimate=cost(10**9, 2 * 10**6),
-        name="prepare_near",
-    )(offsets, kv, qg)
-
-
 def far_kernel(
-    offs_ref, qg_ref, near_ref, far0, far1, far2, far3, part_ref, stat_ref, far_s, ed
+    offs_ref, kv_ref, qg_ref, far0, far1, far2, far3, part_ref, stat_ref, near_s, far_s, ed, keys_t
 ):
-    offset = offs_ref[lax.axis_index("inner")]
+    offset = entry(QG_ORDER, offs_ref[lax.axis_index("inner")])
     place = lax.axis_index("outer")
     place_x, place_y = place // RING, place % RING
+    odd = lax.axis_index("inner") % 2
     fars = (far0, far1, far2, far3)
 
     def far_rows(c):
@@ -232,23 +214,24 @@
     terms = block_terms(qg_ref[offset, BLOCK:, :])
     turned = qg_ref[offset, :BLOCK, :].T
     weights = score_weights(turned[:HD, :], turned[HD:, :])
-    near_top = near_ref[0:1, :]
-    top8 = jnp.broadcast_to(near_top, (8, BLOCK))
+    top8 = jnp.full((8, BLOCK), -jnp.inf, F32)
     for c in range(SEG // CHUNK):
         rows = slice(c * CHUNK, (c + 1) * CHUNK)
+        near = dot(kv_rows(kv_ref, c), weights[:, :BLOCK])
+        near_s[rows, :] = near
         far = dot(far_rows(c), weights)
         far_s[rows, :] = far
-        top8 = jnp.maximum(top8, fold(far[:, :BLOCK], jnp.max))
+        keys_t[:, rows] = far_rows(c).T[:HD, :]
+        top8 = jnp.maximum(top8, jnp.maximum(fold(near, jnp.max), fold(far[:, :BLOCK], jnp.max)))
     top = jnp.max(top8, axis=0, keepdims=True)
     sum8 = jnp.zeros((8, BLOCK), F32)
     for c in range(SEG // CHUNK):
         rows = slice(c * CHUNK, (c + 1) * CHUNK)
         prob = jnp.exp(far_s[rows, :BLOCK] - top)
-        sum8 += fold(prob, jnp.sum)
+        sum8 += fold(prob, jnp.sum) + fold(jnp.exp(near_s[rows, :] - top), jnp.sum)
         ed[rows, :BLOCK] = prob.astype(BF)
         ed[rows, BLOCK:] = (prob * (far_s[rows, BLOCK:] - terms)).astype(BF)
-    total = jnp.sum(sum8, axis=0, keepdims=True) + near_ref[1:2, :] * jnp.exp(near_top - top)
-    factor = 1.0 / total
+    factor = 1.0 / jnp.sum(sum8, axis=0, keepdims=True)
     second = grad_weights(turned, factor)
     query_grad = jnp.zeros((HD, BLOCK), F32)
     for c in range(SEG // CHUNK):
@@ -257,15 +240,16 @@
         grads = dot(both, second).astype(BF)
         for n in range(CHUNK // BLOCK):
             a, b = divmod(c * CHUNK // BLOCK + n, RING)
-            owner = (place_x + a) % RING * RING + (place_y + b) % RING
+            step_x = b + odd * (a - b)
+            owner = (place_x + step_x) % RING * RING + (place_y + a + b - step_x) % RING
             part_ref[owner] = grads[n * BLOCK : (n + 1) * BLOCK, :]
-        query_grad += dot(far_rows(c).T[:HD, :], both[:, BLOCK:])
+        query_grad += dot(keys_t[:, rows], both[:, BLOCK:])
     stat_ref[0:1, :] = top
     stat_ref[1:2, :] = factor
     stat_ref[8:, :] = query_grad * factor * (HD**-0.5)
 
 
-def far_part(offsets, qg, near_stat, fars):
+def far_part(offsets, kv, qg, fars):
     return pl.pallas_call(
         far_kernel,
         out_shape=(
@@ -275,24 +259,31 @@
         in_specs=[SMEM] + [VMEM] * 6,
         out_specs=(VMEM, VMEM),
         scratch_shapes=[
+            pltpu.VMEM((SEG, BLOCK), F32),
             pltpu.VMEM((SEG, 2 * BLOCK), F32),
             pltpu.VMEM((SEG, 2 * BLOCK), BF),
+            pltpu.VMEM((HD, SEG), BF),
         ],
         compiler_params=params(20),
         cost_estimate=cost(2 * 10**9, 2 * 10**6),
         name="far_part",
-    )(offsets, qg, near_stat, *fars)
+    )(offsets, kv, qg, *fars)
 
 
 def near_kernel(
     offs_ref, kv_ref, qg_ref, stat_ref, dq_ref, acc, keys_t, turned_ref, s0, s1, e0, e1, st0, st1
 ):
-    offset = offs_ref[lax.axis_index("inner")]
+    offset = entry(QG_ORDER, offs_ref[lax.axis_index("inner")])
     score_refs, grad_refs, stats = (s0, s1), (e0, e1), (st0, st1)
     chunks = SEG // CHUNK
-    for b in range(NB):
-        keys_t[:, b * BLOCK : (b + 1) * BLOCK] = kv_ref[b].T[:HD, :]
-        turned_ref[b] = qg_ref[b, :BLOCK, :].T
+    turned_ref[0] = qg_ref[0, :BLOCK, :].T
+
+    def prepare(c):
+        rows = slice(c * CHUNK, (c + 1) * CHUNK)
+        keys_t[:, rows] = kv_rows(kv_ref, c).T[:HD, :]
+        acc[rows, :] = jnp.zeros((CHUNK, 2 * HD), F32)
+        for b in range(max(1, c * NB // chunks), (c + 1) * NB // chunks):
+            turned_ref[b] = qg_ref[b, :BLOCK, :].T
 
     def step(j, slot, first, second, third):
         s_now, s_old = score_refs[slot], score_refs[1 - slot]
@@ -313,6 +304,8 @@
             factor = st_now[1:2, :]
             gweights = grad_weights(turned_ref[j - 2], factor)
         for c in range(chunks + 1):
+            if c < chunks and not second and not third:
+                prepare(c)
             if c < chunks and (first or second):
                 rows = slice(c * CHUNK, (c + 1) * CHUNK)
                 score = dot(kv_rows(kv_ref, c), weights)
@@ -342,7 +335,6 @@
 
     step(0, 0, True, False, False)
     step(1, 1, True, True, False)
-    acc[...] = jnp.zeros_like(acc)
 
     def pair(i, carry):
         step(2 * i, 0, True, True, True)
@@ -382,12 +374,15 @@
 def finish_kernel(offs_ref, dq_ref, acc, parts_ref, out_ref):
     offset = offs_ref[lax.axis_index("inner")]
     for b in range(NB):
-        out_ref[b, :BLOCK, :] = acc[b * BLOCK : (b + 1) * BLOCK, :].astype(BF)
-        out_ref[b, BLOCK:, :] = dq_ref[b]
-    total = acc[pl.ds(pl.multiple_of(offset * BLOCK, BLOCK), BLOCK), :]
+        start = entry(KV_ORDER, b) * BLOCK
+        place = entry(OUT_ORDER, b)
+        out_ref[place, :BLOCK, :] = acc[start : start + BLOCK, :].astype(BF)
+        out_ref[place, BLOCK:, :] = dq_ref[entry(QG_ORDER, b)]
+    start = pl.multiple_of(entry(KV_ORDER, offset) * BLOCK, BLOCK)
+    total = acc[pl.ds(start, BLOCK), :]
     for n in range(NB):
         total += parts_ref[n].astype(F32)
-    out_ref[offset, :BLOCK, :] = total.astype(BF)
+    out_ref[entry(OUT_ORDER, offset), :BLOCK, :] = total.astype(BF)
 
 
 def finish(offsets, dq, sums, parts):
@@ -407,12 +402,11 @@
     for n in range(GROUPS):
         for pair in range(n * GROUP // 2, (n + 1) * GROUP // 2):
             cols = slice(pair * 2 * HD, (pair + 1) * 2 * HD)
-            one, two = in_ref[2 * pair, :BLOCK, :], in_ref[2 * pair + 1, :BLOCK, :]
+            first, second = (in_ref.at[entry(OUT_ORDER, 2 * pair + n)] for n in range(2))
+            one, two = first[:BLOCK, :], second[:BLOCK, :]
             k_ref[:, cols] = jnp.concatenate([one[:, :HD], two[:, :HD]], axis=1)
             v_ref[:, cols] = jnp.concatenate([one[:, HD:], two[:, HD:]], axis=1)
-            turned = jnp.concatenate(
-                [in_ref[2 * pair, BLOCK:, :], in_ref[2 * pair + 1, BLOCK:, :]], axis=0
-            )
+            turned = jnp.concatenate([first[BLOCK:, :], second[BLOCK:, :]], axis=0)
             q_ref[:, cols] = turned.T
         cols = pl.ds(n * GROUP_COLS, GROUP_COLS)
         pairs = [(ref.at[:, cols], out.at[:, cols]) for ref, out in ((q_ref, q_out), (k_ref, k_out), (v_ref, v_out))]
@@ -436,34 +430,47 @@
     )(block)
 
 
-def exchange(array, axis):
-    return lax.all_to_all(array, axis, split_axis=0, concat_axis=0, tiled=True)
+def exchange(array, axis, order=None):
+    groups = None
+    if order is not None:
+        sign, first = order
+        groups = [[(first + sign * n) % HEADS for n in range(HEADS)]]
+    return lax.all_to_all(
+        array, axis, split_axis=0, concat_axis=0, tiled=True, axis_index_groups=groups
+    )
 
 
 def spread(block):
-    def ring(step, along_x):
+    inner_count = lax.axis_size("inner")
+
+    def ring(step, first):
         pairs = []
-        for x in range(RING):
-            for y in range(RING):
-                source = (x + step) % RING * RING + y if along_x else x * RING + (y + step) % RING
-                pairs.append((source, x * RING + y))
+        for place in range(RING * RING):
+            x, y = place // RING, place % RING
+            along_y = x * RING + (y + step) % RING
+            along_x = (x + step) % RING * RING + y
+            for inner in range(inner_count):
+                source = along_y if (inner % 2 == 1) == first else along_x
+                pairs.append((source * inner_count + inner, place * inner_count + inner))
         return pairs
 
-    row = jnp.stack([block] + [lax.ppermute(block, "outer", ring(n, False)) for n in (1, 2, 3)])
-    return [row] + [lax.ppermute(row, "outer", ring(n, True)) for n in (1, 2, 3)]
+    def send(array, step, first):
+        return lax.ppermute(array, ("outer", "inner"), ring(step, first))
+
+    row = jnp.stack([block] + [send(block, n, True) for n in (1, 2, 3)])
+    return [row] + [send(row, n, False) for n in (1, 2, 3)]
 
 
 def on_device(queries, keys, values, saved_out, out_grad, offsets):
-    kv = exchange(pack_kv(keys, values), "inner")
+    kv = exchange(pack_kv(keys, values), "inner", KV_ORDER)
     qg = pack_qg(queries, saved_out, out_grad)
     fars = spread(pick(offsets, kv))
-    qg = exchange(qg, "inner")
-    near_stat = prepare(offsets, kv, qg)
-    parts, stat = far_part(offsets, qg, near_stat, fars)
+    qg = exchange(qg, "inner", QG_ORDER)
+    parts, stat = far_part(offsets, kv, qg, fars)
     parts = exchange(parts, "outer")
     dq, sums = near_part(offsets, kv, qg, stat)
     whole = finish(offsets, dq, sums, parts)
-    return unpack(exchange(whole, "inner"))
+    return unpack(exchange(whole, "inner", OUT_ORDER))
 
 
 def solution(mesh):

time: 105 us -> 102 us (0.971)
  blocking collectives: 27.8 us -> 25.4 us
    all_to_all x1, blocking collectives: 27.8 us -> 25.4 us  [exchange(): lax.all_to_all(array, axis, split_axis=0, concat_axis=0, tiled=True, axis...]
    pallas_call x1 -> x0, Pallas kernels: 1.06 us -> none  [prepare(): pl.pallas_call(prepare_kernel, out_shape=jax.ShapeDtypeStruct((8, BLOCK),...]
where the time goes in v4:
time: 102 us
  starting transfers between devices  30.2 us (30%)
  blocking collectives  25.4 us (25%)
  Pallas kernels  22.7 us (22%)
  waiting for transfers between devices  22.5 us (22%)
    all_to_all x1, blocking collectives, exchange(): lax.all_to_all(array, axis, split_axis=0, concat_axis=0, tiled=True, axis...  25.4 us
    all_to_all x3, waiting for transfers between devices, exchange(): lax.all_to_all(array, axis, split_axis=0, concat_axis=0, tiled=True, axis...  20.5 us
    all_to_all x3, starting transfers between devices, exchange(): lax.all_to_all(array, axis, split_axis=0, concat_axis=0, tiled=True, axis...  20.2 us
    pallas_call x1, Pallas kernels, near_part(): pl.pallas_call(near_kernel, out_shape=(jax.ShapeDtypeStruct((NB, HD, BLOC...  12.9 us
    ppermute x6, starting transfers between devices, send(): return lax.ppermute(array, ('outer', 'inner'), ring(step, first))  9.95 us
    pallas_call x1, Pallas kernels, far_part(): pl.pallas_call(far_kernel, out_shape=(jax.ShapeDtypeStruct((NB, BLOCK, 2...  3.12 us
    pallas_call x1, Pallas kernels, pack_qg(): pl.pallas_call(pack_qg_kernel, out_shape=jax.ShapeDtypeStruct((HEADS, QG_...  2.36 us
  transfers between devices with their start and end apart: 9, of which 4 were waited for; matrix products, arithmetic and copies ran while one was open for 0% of the time, Pallas kernels for 16%

profile of v4, /device:TPU:1, one launch (start us, length us, event | category | flops | bytes accessed | tf_op | source)
XLA Modules:
  0.0 101.5 jit_solution(9582219446027207118)
XLA Ops:
  0.6 2.0 %pack_keys_values.1 = bf16[16,128,128]{2,1,0:T(8,128)(2,1)} custom-call(bf16[128,1024]{1,0:T(8,128)(2,1)} %k_in.1, bf16[128,1024]{1,0:T(8,128)(2,1)} %v_in.1), custom_call_target="tpu_custom_call" | custom-call | flops 1000000 | bytes 1000000 | tf_op jit(solution)/shard_map/pack_keys_values/pallas_call | solution.py:98
  2.6 10.0 %all-to-all-start = ((bf16[16,128,128]{2,1,0:T(8,128)(2,1)}), bf16[16,128,128]{2,1,0:T(8,128)(2,1)S(1)}, u32[]{:S(2)}, u32[]{:S(2)}) async-start(bf16[16,128,128]{2,1,0:T(8,128)(2,1)} %pack_keys_values.1), calls=%async_computation | async-start | bytes 1048576 | tf_op jit(solution)/shard_map/all_to_all | solution.py:438
  12.6 2.4 %pack_queries_grads.1 = bf16[16,144,128]{2,1,0:T(8,128)(2,1)} custom-call(bf16[128,1024]{1,0:T(8,128)(2,1)} %q_in.1, bf16[128,1024]{1,0:T(8,128)(2,1)} %o_in.1, bf16[128,1024]{1,0:T(8,128)(2,1)} %g_in.1), custom_call_target="tpu_custom_call" | custom-call | flops 10000000 | bytes 2000000 | tf_op jit(solution)/shard_map/pack_queries_grads/pallas_call | solution.py:140
  15.0 0.0 copy-start
  15.0 14.9 %all-to-all-done.kv_ref = bf16[16,128,128]{2,1,0:T(8,128)(2,1)S(1)} async-done(((bf16[16,128,128]{2,1,0:T(8,128)(2,1)}), bf16[16,128,128]{2,1,0:T(8,128)(2,1)S(1)}, u32[]{:S(2)}, u32[]{:S(2)}) %all-to-all-start) | async-done | bytes 524320 | tf_op jit(solution)/shard_map/all_to_all | solution.py:438
  30.0 3.5 %all-to-all-start.1 = ((bf16[16,144,128]{2,1,0:T(8,128)(2,1)}), bf16[16,144,128]{2,1,0:T(8,128)(2,1)S(1)}, u32[]{:S(2)}, u32[]{:S(2)}) async-start(bf16[16,144,128]{2,1,0:T(8,128)(2,1)} %pack_queries_grads.1), calls=%async_computation.1 | async-start | bytes 1179648 | tf_op jit(solution)/shard_map/all_to_all | solution.py:438
  33.4 0.0 copy-done
  33.5 0.6 pick_block.1
  34.0 1.4 %collective-permute-start.2 = (bf16[128,128]{1,0:T(8,128)(2,1)S(1)}, bf16[128,128]{1,0:T(8,128)(2,1)S(1)}, u32[]{:S(2)}, u32[]{:S(2)}) collective-permute-start(bf16[128,128]{1,0:T(8,128)(2,1)S(1)} %pick_block.1), channel_id=1, source_target_pairs={{192,0},{49,1},{194,2},{51,3},{196,4},{53,5},{198,6},{55,7},{200,8... | collective-permute-start | bytes 98312 | tf_op jit(solution)/shard_map/ppermute | solution.py:458
  35.4 2.6 %collective-permute-start.1 = (bf16[128,128]{1,0:T(8,128)(2,1)S(1)}, bf16[128,128]{1,0:T(8,128)(2,1)S(1)}, u32[]{:S(2)}, u32[]{:S(2)}) collective-permute-start(bf16[128,128]{1,0:T(8,128)(2,1)S(1)} %pick_block.1), channel_id=1, source_target_pairs={{128,0},{33,1},{130,2},{35,3},{132,4},{37,5},{134,6},{39,7},{136,8... | collective-permute-start | bytes 98312 | tf_op jit(solution)/shard_map/ppermute | solution.py:458
  38.0 1.1 %collective-permute-start = (bf16[128,128]{1,0:T(8,128)(2,1)S(1)}, bf16[128,128]{1,0:T(8,128)(2,1)S(1)}, u32[]{:S(2)}, u32[]{:S(2)}) collective-permute-start(bf16[128,128]{1,0:T(8,128)(2,1)S(1)} %pick_block.1), channel_id=1, source_target_pairs={{64,0},{17,1},{66,2},{19,3},{68,4},{21,5},{70,6},{23,7},{72,8},{25... | collective-permute-start | bytes 98312 | tf_op jit(solution)/shard_map/ppermute | solution.py:458
  39.1 0.0 collective-permute-done.2
  39.1 0.9 collective-permute-done.1
  40.0 1.1 %collective-permute-done = bf16[128,128]{1,0:T(8,128)(2,1)S(1)} collective-permute-done((bf16[128,128]{1,0:T(8,128)(2,1)S(1)}, bf16[128,128]{1,0:T(8,128)(2,1)S(1)}, u32[]{:S(2)}, u32[]{:S(2)}) %collective-permute-start) | collective-permute-done | bytes 32800 | tf_op jit(solution)/shard_map/ppermute | solution.py:458
  41.1 1.3 %collective-permute-start.5 = (bf16[4,128,128]{2,1,0:T(8,128)(2,1)S(1)}, bf16[4,128,128]{2,1,0:T(8,128)(2,1)S(1)}, u32[]{:S(2)}, u32[]{:S(2)}) collective-permute-start(bf16[4,128,128]{2,1,0:T(8,128)(2,1)S(1)} %pad_maximum_fusion.far0), channel_id=1, source_target_pairs={{48,0},{193,1},{50,2},{195,3},{52,4},{197,5},{54,6},{199,7},{56,8}... | collective-permute-start | bytes 393224 | tf_op jit(solution)/shard_map/ppermute | solution.py:458
  42.4 2.5 %collective-permute-start.4 = (bf16[4,128,128]{2,1,0:T(8,128)(2,1)S(1)}, bf16[4,128,128]{2,1,0:T(8,128)(2,1)S(1)}, u32[]{:S(2)}, u32[]{:S(2)}) collective-permute-start(bf16[4,128,128]{2,1,0:T(8,128)(2,1)S(1)} %pad_maximum_fusion.far0), channel_id=1, source_target_pairs={{32,0},{129,1},{34,2},{131,3},{36,4},{133,5},{38,6},{135,7},{40,8}... | collective-permute-start | bytes 393224 | tf_op jit(solution)/shard_map/ppermute | solution.py:458
  44.8 1.2 %collective-permute-start.3 = (bf16[4,128,128]{2,1,0:T(8,128)(2,1)S(1)}, bf16[4,128,128]{2,1,0:T(8,128)(2,1)S(1)}, u32[]{:S(2)}, u32[]{:S(2)}) collective-permute-start(bf16[4,128,128]{2,1,0:T(8,128)(2,1)S(1)} %pad_maximum_fusion.far0), channel_id=1, source_target_pairs={{16,0},{65,1},{18,2},{67,3},{20,4},{69,5},{22,6},{71,7},{24,8},{73... | collective-permute-start | bytes 393224 | tf_op jit(solution)/shard_map/ppermute | solution.py:458
  46.0 5.5 %all-to-all-done.1.qg_ref = bf16[16,144,128]{2,1,0:T(8,128)(2,1)S(1)} async-done(((bf16[16,144,128]{2,1,0:T(8,128)(2,1)}), bf16[16,144,128]{2,1,0:T(8,128)(2,1)S(1)}, u32[]{:S(2)}, u32[]{:S(2)}) %all-to-all-start.1) | async-done | bytes 589856 | tf_op jit(solution)/shard_map/all_to_all | solution.py:438
  51.5 0.0 collective-permute-done.5.far3
  51.5 0.0 collective-permute-done.4.far2
  51.5 0.0 collective-permute-done.3.far1
  51.5 3.1 %far_part.1 = (bf16[16,128,128]{2,1,0:T(8,128)(2,1)}, f32[72,128]{1,0:T(8,128)S(1)}) custom-call(s32[16]{0:T(128)S(1)} %copy-done, bf16[16,128,128]{2,1,0:T(8,128)(2,1)S(1)} %all-to-all-done.kv_ref, bf16[16,144,128]{2,1,0:T(8,128)(2,1)S(1)} %all-to-all-done.1.qg_ref, bf16[4,128,128]{2,1,0:T(8,128)(2,1)S(1)} %pad_maximum_fusion.far0, ...), custom_call_target="tpu_custom_call" | custom-call | flops 2000000000 | bytes 2000000 | tf_op jit(solution)/shard_map/far_part/pallas_call | solution.py:253
  54.7 6.8 %all-to-all-start.2 = ((bf16[16,128,128]{2,1,0:T(8,128)(2,1)}), bf16[16,128,128]{2,1,0:T(8,128)(2,1)S(1)}, u32[]{:S(2)}, u32[]{:S(2)}) async-start(bf16[16,128,128]{2,1,0:T(8,128)(2,1)} %get-tuple-element.10), calls=%async_computation.2 | async-start | bytes 1048576 | tf_op jit(solution)/shard_map/all_to_all | solution.py:438
  61.4 12.9 %near_part.1 = (bf16[16,64,128]{2,1,0:T(8,128)(2,1)S(1)}, f32[2048,128]{1,0:T(8,128)S(1)}) custom-call(s32[16]{0:T(128)S(1)} %copy-done, bf16[16,128,128]{2,1,0:T(8,128)(2,1)S(1)} %all-to-all-done.kv_ref, bf16[16,144,128]{2,1,0:T(8,128)(2,1)S(1)} %all-to-all-done.1.qg_ref, f32[72,128]{1,0:T(8,128)S(1)} %get-tuple-element.7.stat_ref), custom_call_target="tpu_custom_call" | custom-call | flops 15000000512 | bytes 4000000 | tf_op jit(solution)/shard_map/near_part/pallas_call | solution.py:350
  74.3 0.0 all-to-all-done.2.parts_ref
  74.3 0.7 finish_picked.1
  75.0 25.4 %all_to_all.20.in_ref = bf16[16,192,128]{2,1,0:T(8,128)(2,1)S(1)} all-to-all(bf16[16,192,128]{2,1,0:T(8,128)(2,1)S(1)} %finish_picked.1), channel_id=1, replica_groups={{15,14,13,12,11,10,9,8,7,6,5,4,3,2,1,0},{31,30,29,28,27,26,25,24,23,22,..., dimensions={0} | all-to-all | bytes 1572864 | tf_op jit(solution)/shard_map/all_to_all | solution.py:438
  100.4 1.1 %unpack_heads.1 = (bf16[128,1024]{1,0:T(8,128)(2,1)}, bf16[128,1024]{1,0:T(8,128)(2,1)}, bf16[128,1024]{1,0:T(8,128)(2,1)}) custom-call(bf16[16,192,128]{2,1,0:T(8,128)(2,1)S(1)} %all_to_all.20.in_ref), custom_call_target="tpu_custom_call" | custom-call | flops 1000000 | bytes 2000000 | tf_op jit(solution)/shard_map/unpack_heads/pallas_call | solution.py:420
  (1 shorter events, 0.0 us)
Async XLA Ops:
  2.6 27.3 %all-to-all-start = ((bf16[16,128,128]{2,1,0:T(8,128)(2,1)}), bf16[16,128,128]{2,1,0:T(8,128)(2,1)S(1)}, u32[]{:S(2)}, u32[]{:S(2)}) async-start(bf16[16,128,128]{2,1,0:T(8,128)(2,1)} %pack_keys_values.1), calls=%async_computation | async-start | bytes 1048576 | tf_op jit(solution)/shard_map/all_to_all | solution.py:438
  15.0 18.4 %copy-start = (s32[16]{0:T(128)S(1)}, s32[16]{0:T(128)}, u32[]{:S(2)}) copy-start(s32[16]{0:T(128)} %offs_ref.7) | copy-start | bytes 196
  30.0 21.6 %all-to-all-start.1 = ((bf16[16,144,128]{2,1,0:T(8,128)(2,1)}), bf16[16,144,128]{2,1,0:T(8,128)(2,1)S(1)}, u32[]{:S(2)}, u32[]{:S(2)}) async-start(bf16[16,144,128]{2,1,0:T(8,128)(2,1)} %pack_queries_grads.1), calls=%async_computation.1 | async-start | bytes 1179648 | tf_op jit(solution)/shard_map/all_to_all | solution.py:438
  34.0 5.1 %collective-permute-start.2 = (bf16[128,128]{1,0:T(8,128)(2,1)S(1)}, bf16[128,128]{1,0:T(8,128)(2,1)S(1)}, u32[]{:S(2)}, u32[]{:S(2)}) collective-permute-start(bf16[128,128]{1,0:T(8,128)(2,1)S(1)} %pick_block.1), channel_id=1, source_target_pairs={{192,0},{49,1},{194,2},{51,3},{196,4},{53,5},{198,6},{55,7},{200,8... | collective-permute-start | bytes 98312 | tf_op jit(solution)/shard_map/ppermute | solution.py:458
  35.4 4.6 %collective-permute-start.1 = (bf16[128,128]{1,0:T(8,128)(2,1)S(1)}, bf16[128,128]{1,0:T(8,128)(2,1)S(1)}, u32[]{:S(2)}, u32[]{:S(2)}) collective-permute-start(bf16[128,128]{1,0:T(8,128)(2,1)S(1)} %pick_block.1), channel_id=1, source_target_pairs={{128,0},{33,1},{130,2},{35,3},{132,4},{37,5},{134,6},{39,7},{136,8... | collective-permute-start | bytes 98312 | tf_op jit(solution)/shard_map/ppermute | solution.py:458
  38.0 3.1 %collective-permute-start = (bf16[128,128]{1,0:T(8,128)(2,1)S(1)}, bf16[128,128]{1,0:T(8,128)(2,1)S(1)}, u32[]{:S(2)}, u32[]{:S(2)}) collective-permute-start(bf16[128,128]{1,0:T(8,128)(2,1)S(1)} %pick_block.1), channel_id=1, source_target_pairs={{64,0},{17,1},{66,2},{19,3},{68,4},{21,5},{70,6},{23,7},{72,8},{25... | collective-permute-start | bytes 98312 | tf_op jit(solution)/shard_map/ppermute | solution.py:458
  41.1 10.4 %collective-permute-start.5 = (bf16[4,128,128]{2,1,0:T(8,128)(2,1)S(1)}, bf16[4,128,128]{2,1,0:T(8,128)(2,1)S(1)}, u32[]{:S(2)}, u32[]{:S(2)}) collective-permute-start(bf16[4,128,128]{2,1,0:T(8,128)(2,1)S(1)} %pad_maximum_fusion.far0), channel_id=1, source_target_pairs={{48,0},{193,1},{50,2},{195,3},{52,4},{197,5},{54,6},{199,7},{56,8}... | collective-permute-start | bytes 393224 | tf_op jit(solution)/shard_map/ppermute | solution.py:458
  42.4 9.1 %collective-permute-start.4 = (bf16[4,128,128]{2,1,0:T(8,128)(2,1)S(1)}, bf16[4,128,128]{2,1,0:T(8,128)(2,1)S(1)}, u32[]{:S(2)}, u32[]{:S(2)}) collective-permute-start(bf16[4,128,128]{2,1,0:T(8,128)(2,1)S(1)} %pad_maximum_fusion.far0), channel_id=1, source_target_pairs={{32,0},{129,1},{34,2},{131,3},{36,4},{133,5},{38,6},{135,7},{40,8}... | collective-permute-start | bytes 393224 | tf_op jit(solution)/shard_map/ppermute | solution.py:458
  44.8 6.7 %collective-permute-start.3 = (bf16[4,128,128]{2,1,0:T(8,128)(2,1)S(1)}, bf16[4,128,128]{2,1,0:T(8,128)(2,1)S(1)}, u32[]{:S(2)}, u32[]{:S(2)}) collective-permute-start(bf16[4,128,128]{2,1,0:T(8,128)(2,1)S(1)} %pad_maximum_fusion.far0), channel_id=1, source_target_pairs={{16,0},{65,1},{18,2},{67,3},{20,4},{69,5},{22,6},{71,7},{24,8},{73... | collective-permute-start | bytes 393224 | tf_op jit(solution)/shard_map/ppermute | solution.py:458
  54.7 19.7 %all-to-all-start.2 = ((bf16[16,128,128]{2,1,0:T(8,128)(2,1)}), bf16[16,128,128]{2,1,0:T(8,128)(2,1)S(1)}, u32[]{:S(2)}, u32[]{:S(2)}) async-start(bf16[16,128,128]{2,1,0:T(8,128)(2,1)} %get-tuple-element.10), calls=%async_computation.2 | async-start | bytes 1048576 | tf_op jit(solution)/shard_map/all_to_all | solution.py:438

commit v5 on v4

--- a/solution.py
+++ b/solution.py
@@ -17,8 +17,8 @@
 CHUNK = 256
 BF = jnp.bfloat16
 F32 = jnp.float32
-KV_ORDER = (1, 0)
-QG_ORDER = (1, 0)
+KV_ORDER = (1, 8)
+QG_ORDER = (1, 8)
 OUT_ORDER = (-1, 15)
 VMEM = pl.BlockSpec(memory_space=pltpu.VMEM)
 SMEM = pl.BlockSpec(memory_space=pltpu.SMEM)

time: 102 us -> 101 us (level)
  waiting for transfers between devices: 22.5 us -> 15.2 us
  starting transfers between devices: 30.2 us -> 35 us
  blocking collectives: 25.4 us -> 26.7 us
    all_to_all x3, waiting for transfers between devices: 20.5 us -> 12.4 us  [exchange(): lax.all_to_all(array, axis, split_axis=0, concat_axis=0, tiled=True, axis...]
    all_to_all x3, starting transfers between devices: 20.2 us -> 25.1 us  [exchange(): lax.all_to_all(array, axis, split_axis=0, concat_axis=0, tiled=True, axis...]
    all_to_all x1, blocking collectives: 25.4 us -> 26.7 us  [exchange(): lax.all_to_all(array, axis, split_axis=0, concat_axis=0, tiled=True, axis...]
  transfers between devices with their start and end apart: 9 -> 9, of which waited for: 4 -> 6; matrix products, arithmetic and copies ran while one was open for 0% -> 0% of each run, Pallas kernels for 16% -> 16%
where the time goes in v5:
time: 101 us; the launch traced here: 100 us
  starting transfers between devices  35 us (35%)
  blocking collectives  26.7 us (26%)
  Pallas kernels  22.7 us (22%)
  waiting for transfers between devices  15.2 us (15%)
    all_to_all x1, blocking collectives, exchange(): lax.all_to_all(array, axis, split_axis=0, concat_axis=0, tiled=True, axis...  26.7 us
    all_to_all x3, starting transfers between devices, exchange(): lax.all_to_all(array, axis, split_axis=0, concat_axis=0, tiled=True, axis...  25.1 us
    pallas_call x1, Pallas kernels, near_part(): pl.pallas_call(near_kernel, out_shape=(jax.ShapeDtypeStruct((NB, HD, BLOC...  12.9 us
    all_to_all x3, waiting for transfers between devices, exchange(): lax.all_to_all(array, axis, split_axis=0, concat_axis=0, tiled=True, axis...  12.4 us
    ppermute x6, starting transfers between devices, send(): return lax.ppermute(array, ('outer', 'inner'), ring(step, first))  9.95 us
    pallas_call x1, Pallas kernels, far_part(): pl.pallas_call(far_kernel, out_shape=(jax.ShapeDtypeStruct((NB, BLOCK, 2...  3.12 us
    ppermute x6, waiting for transfers between devices, send(): return lax.ppermute(array, ('outer', 'inner'), ring(step, first))  2.78 us
    pallas_call x1, Pallas kernels, pack_qg(): pl.pallas_call(pack_qg_kernel, out_shape=jax.ShapeDtypeStruct((HEADS, QG_...  2.36 us
  transfers between devices with their start and end apart: 9, of which 6 were waited for; matrix products, arithmetic and copies ran while one was open for 0% of the time, Pallas kernels for 16%

profile of v5, /device:TPU:1, one launch (start us, length us, event | category | flops | bytes accessed | tf_op | source)
XLA Modules:
  0.0 100.4 jit_solution(5935024347327223618)
XLA Ops:
  0.6 2.0 %pack_keys_values.1 = bf16[16,128,128]{2,1,0:T(8,128)(2,1)} custom-call(bf16[128,1024]{1,0:T(8,128)(2,1)} %k_in.1, bf16[128,1024]{1,0:T(8,128)(2,1)} %v_in.1), custom_call_target="tpu_custom_call" | custom-call | flops 1000000 | bytes 1000000 | tf_op jit(solution)/shard_map/pack_keys_values/pallas_call | solution.py:98
  2.6 11.8 %all-to-all-start = ((bf16[16,128,128]{2,1,0:T(8,128)(2,1)}), bf16[16,128,128]{2,1,0:T(8,128)(2,1)S(1)}, u32[]{:S(2)}, u32[]{:S(2)}) async-start(bf16[16,128,128]{2,1,0:T(8,128)(2,1)} %pack_keys_values.1), calls=%async_computation | async-start | bytes 1048576 | tf_op jit(solution)/shard_map/all_to_all | solution.py:438
  14.4 2.4 %pack_queries_grads.1 = bf16[16,144,128]{2,1,0:T(8,128)(2,1)} custom-call(bf16[128,1024]{1,0:T(8,128)(2,1)} %q_in.1, bf16[128,1024]{1,0:T(8,128)(2,1)} %o_in.1, bf16[128,1024]{1,0:T(8,128)(2,1)} %g_in.1), custom_call_target="tpu_custom_call" | custom-call | flops 10000000 | bytes 2000000 | tf_op jit(solution)/shard_map/pack_queries_grads/pallas_call | solution.py:140
  16.8 0.0 copy-start
  16.8 10.6 %all-to-all-done.kv_ref = bf16[16,128,128]{2,1,0:T(8,128)(2,1)S(1)} async-done(((bf16[16,128,128]{2,1,0:T(8,128)(2,1)}), bf16[16,128,128]{2,1,0:T(8,128)(2,1)S(1)}, u32[]{:S(2)}, u32[]{:S(2)}) %all-to-all-start) | async-done | bytes 524320 | tf_op jit(solution)/shard_map/all_to_all | solution.py:438
  27.3 7.3 %all-to-all-start.1 = ((bf16[16,144,128]{2,1,0:T(8,128)(2,1)}), bf16[16,144,128]{2,1,0:T(8,128)(2,1)S(1)}, u32[]{:S(2)}, u32[]{:S(2)}) async-start(bf16[16,144,128]{2,1,0:T(8,128)(2,1)} %pack_queries_grads.1), calls=%async_computation.1 | async-start | bytes 1179648 | tf_op jit(solution)/shard_map/all_to_all | solution.py:438
  34.6 0.0 copy-done
  34.6 0.6 pick_block.1
  35.2 1.4 %collective-permute-start.2 = (bf16[128,128]{1,0:T(8,128)(2,1)S(1)}, bf16[128,128]{1,0:T(8,128)(2,1)S(1)}, u32[]{:S(2)}, u32[]{:S(2)}) collective-permute-start(bf16[128,128]{1,0:T(8,128)(2,1)S(1)} %pick_block.1), channel_id=1, source_target_pairs={{192,0},{49,1},{194,2},{51,3},{196,4},{53,5},{198,6},{55,7},{200,8... | collective-permute-start | bytes 98312 | tf_op jit(solution)/shard_map/ppermute | solution.py:458
  36.6 2.6 %collective-permute-start.1 = (bf16[128,128]{1,0:T(8,128)(2,1)S(1)}, bf16[128,128]{1,0:T(8,128)(2,1)S(1)}, u32[]{:S(2)}, u32[]{:S(2)}) collective-permute-start(bf16[128,128]{1,0:T(8,128)(2,1)S(1)} %pick_block.1), channel_id=1, source_target_pairs={{128,0},{33,1},{130,2},{35,3},{132,4},{37,5},{134,6},{39,7},{136,8... | collective-permute-start | bytes 98312 | tf_op jit(solution)/shard_map/ppermute | solution.py:458
  39.2 1.1 %collective-permute-start = (bf16[128,128]{1,0:T(8,128)(2,1)S(1)}, bf16[128,128]{1,0:T(8,128)(2,1)S(1)}, u32[]{:S(2)}, u32[]{:S(2)}) collective-permute-start(bf16[128,128]{1,0:T(8,128)(2,1)S(1)} %pick_block.1), channel_id=1, source_target_pairs={{64,0},{17,1},{66,2},{19,3},{68,4},{21,5},{70,6},{23,7},{72,8},{25... | collective-permute-start | bytes 98312 | tf_op jit(solution)/shard_map/ppermute | solution.py:458
  40.2 0.0 collective-permute-done.2
  40.3 0.6 collective-permute-done.1
  40.8 1.4 %collective-permute-done = bf16[128,128]{1,0:T(8,128)(2,1)S(1)} collective-permute-done((bf16[128,128]{1,0:T(8,128)(2,1)S(1)}, bf16[128,128]{1,0:T(8,128)(2,1)S(1)}, u32[]{:S(2)}, u32[]{:S(2)}) %collective-permute-start) | collective-permute-done | bytes 32800 | tf_op jit(solution)/shard_map/ppermute | solution.py:458
  42.3 1.3 %collective-permute-start.5 = (bf16[4,128,128]{2,1,0:T(8,128)(2,1)S(1)}, bf16[4,128,128]{2,1,0:T(8,128)(2,1)S(1)}, u32[]{:S(2)}, u32[]{:S(2)}) collective-permute-start(bf16[4,128,128]{2,1,0:T(8,128)(2,1)S(1)} %pad_maximum_fusion.far0), channel_id=1, source_target_pairs={{48,0},{193,1},{50,2},{195,3},{52,4},{197,5},{54,6},{199,7},{56,8}... | collective-permute-start | bytes 393224 | tf_op jit(solution)/shard_map/ppermute | solution.py:458
  43.6 2.5 %collective-permute-start.4 = (bf16[4,128,128]{2,1,0:T(8,128)(2,1)S(1)}, bf16[4,128,128]{2,1,0:T(8,128)(2,1)S(1)}, u32[]{:S(2)}, u32[]{:S(2)}) collective-permute-start(bf16[4,128,128]{2,1,0:T(8,128)(2,1)S(1)} %pad_maximum_fusion.far0), channel_id=1, source_target_pairs={{32,0},{129,1},{34,2},{131,3},{36,4},{133,5},{38,6},{135,7},{40,8}... | collective-permute-start | bytes 393224 | tf_op jit(solution)/shard_map/ppermute | solution.py:458
  46.0 1.2 %collective-permute-start.3 = (bf16[4,128,128]{2,1,0:T(8,128)(2,1)S(1)}, bf16[4,128,128]{2,1,0:T(8,128)(2,1)S(1)}, u32[]{:S(2)}, u32[]{:S(2)}) collective-permute-start(bf16[4,128,128]{2,1,0:T(8,128)(2,1)S(1)} %pad_maximum_fusion.far0), channel_id=1, source_target_pairs={{16,0},{65,1},{18,2},{67,3},{20,4},{69,5},{22,6},{71,7},{24,8},{73... | collective-permute-start | bytes 393224 | tf_op jit(solution)/shard_map/ppermute | solution.py:458
  47.2 1.9 %all-to-all-done.1.qg_ref = bf16[16,144,128]{2,1,0:T(8,128)(2,1)S(1)} async-done(((bf16[16,144,128]{2,1,0:T(8,128)(2,1)}), bf16[16,144,128]{2,1,0:T(8,128)(2,1)S(1)}, u32[]{:S(2)}, u32[]{:S(2)}) %all-to-all-start.1) | async-done | bytes 589856 | tf_op jit(solution)/shard_map/all_to_all | solution.py:438
  49.0 0.0 collective-permute-done.5.far3
  49.0 0.7 collective-permute-done.4.far2
  49.8 0.1 collective-permute-done.3.far1
  49.8 3.1 %far_part.1 = (bf16[16,128,128]{2,1,0:T(8,128)(2,1)}, f32[72,128]{1,0:T(8,128)S(1)}) custom-call(s32[16]{0:T(128)S(1)} %copy-done, bf16[16,128,128]{2,1,0:T(8,128)(2,1)S(1)} %all-to-all-done.kv_ref, bf16[16,144,128]{2,1,0:T(8,128)(2,1)S(1)} %all-to-all-done.1.qg_ref, bf16[4,128,128]{2,1,0:T(8,128)(2,1)S(1)} %pad_maximum_fusion.far0, ...), custom_call_target="tpu_custom_call" | custom-call | flops 2000000000 | bytes 2000000 | tf_op jit(solution)/shard_map/far_part/pallas_call | solution.py:253
  52.9 6.0 %all-to-all-start.2 = ((bf16[16,128,128]{2,1,0:T(8,128)(2,1)}), bf16[16,128,128]{2,1,0:T(8,128)(2,1)S(1)}, u32[]{:S(2)}, u32[]{:S(2)}) async-start(bf16[16,128,128]{2,1,0:T(8,128)(2,1)} %get-tuple-element.10), calls=%async_computation.2 | async-start | bytes 1048576 | tf_op jit(solution)/shard_map/all_to_all | solution.py:438
  59.0 12.9 %near_part.1 = (bf16[16,64,128]{2,1,0:T(8,128)(2,1)S(1)}, f32[2048,128]{1,0:T(8,128)S(1)}) custom-call(s32[16]{0:T(128)S(1)} %copy-done, bf16[16,128,128]{2,1,0:T(8,128)(2,1)S(1)} %all-to-all-done.kv_ref, bf16[16,144,128]{2,1,0:T(8,128)(2,1)S(1)} %all-to-all-done.1.qg_ref, f32[72,128]{1,0:T(8,128)S(1)} %get-tuple-element.7.stat_ref), custom_call_target="tpu_custom_call" | custom-call | flops 15000000512 | bytes 4000000 | tf_op jit(solution)/shard_map/near_part/pallas_call | solution.py:350
  71.9 0.0 all-to-all-done.2.parts_ref
  71.9 0.7 finish_picked.1
  72.6 26.7 %all_to_all.20.in_ref = bf16[16,192,128]{2,1,0:T(8,128)(2,1)S(1)} all-to-all(bf16[16,192,128]{2,1,0:T(8,128)(2,1)S(1)} %finish_picked.1), channel_id=1, replica_groups={{15,14,13,12,11,10,9,8,7,6,5,4,3,2,1,0},{31,30,29,28,27,26,25,24,23,22,..., dimensions={0} | all-to-all | bytes 1572864 | tf_op jit(solution)/shard_map/all_to_all | solution.py:438
  99.3 1.1 %unpack_heads.1 = (bf16[128,1024]{1,0:T(8,128)(2,1)}, bf16[128,1024]{1,0:T(8,128)(2,1)}, bf16[128,1024]{1,0:T(8,128)(2,1)}) custom-call(bf16[16,192,128]{2,1,0:T(8,128)(2,1)S(1)} %all_to_all.20.in_ref), custom_call_target="tpu_custom_call" | custom-call | flops 1000000 | bytes 2000000 | tf_op jit(solution)/shard_map/unpack_heads/pallas_call | solution.py:420
  (1 shorter events, 0.0 us)
Async XLA Ops:
  2.6 24.7 %all-to-all-start = ((bf16[16,128,128]{2,1,0:T(8,128)(2,1)}), bf16[16,128,128]{2,1,0:T(8,128)(2,1)S(1)}, u32[]{:S(2)}, u32[]{:S(2)}) async-start(bf16[16,128,128]{2,1,0:T(8,128)(2,1)} %pack_keys_values.1), calls=%async_computation | async-start | bytes 1048576 | tf_op jit(solution)/shard_map/all_to_all | solution.py:438
  16.8 17.9 %copy-start = (s32[16]{0:T(128)S(1)}, s32[16]{0:T(128)}, u32[]{:S(2)}) copy-start(s32[16]{0:T(128)} %offs_ref.7) | copy-start | bytes 196
  27.3 21.7 %all-to-all-start.1 = ((bf16[16,144,128]{2,1,0:T(8,128)(2,1)}), bf16[16,144,128]{2,1,0:T(8,128)(2,1)S(1)}, u32[]{:S(2)}, u32[]{:S(2)}) async-start(bf16[16,144,128]{2,1,0:T(8,128)(2,1)} %pack_queries_grads.1), calls=%async_computation.1 | async-start | bytes 1179648 | tf_op jit(solution)/shard_map/all_to_all | solution.py:438
  35.2 5.1 %collective-permute-start.2 = (bf16[128,128]{1,0:T(8,128)(2,1)S(1)}, bf16[128,128]{1,0:T(8,128)(2,1)S(1)}, u32[]{:S(2)}, u32[]{:S(2)}) collective-permute-start(bf16[128,128]{1,0:T(8,128)(2,1)S(1)} %pick_block.1), channel_id=1, source_target_pairs={{192,0},{49,1},{194,2},{51,3},{196,4},{53,5},{198,6},{55,7},{200,8... | collective-permute-start | bytes 98312 | tf_op jit(solution)/shard_map/ppermute | solution.py:458
  36.6 4.3 %collective-permute-start.1 = (bf16[128,128]{1,0:T(8,128)(2,1)S(1)}, bf16[128,128]{1,0:T(8,128)(2,1)S(1)}, u32[]{:S(2)}, u32[]{:S(2)}) collective-permute-start(bf16[128,128]{1,0:T(8,128)(2,1)S(1)} %pick_block.1), channel_id=1, source_target_pairs={{128,0},{33,1},{130,2},{35,3},{132,4},{37,5},{134,6},{39,7},{136,8... | collective-permute-start | bytes 98312 | tf_op jit(solution)/shard_map/ppermute | solution.py:458
  39.2 3.1 %collective-permute-start = (bf16[128,128]{1,0:T(8,128)(2,1)S(1)}, bf16[128,128]{1,0:T(8,128)(2,1)S(1)}, u32[]{:S(2)}, u32[]{:S(2)}) collective-permute-start(bf16[128,128]{1,0:T(8,128)(2,1)S(1)} %pick_block.1), channel_id=1, source_target_pairs={{64,0},{17,1},{66,2},{19,3},{68,4},{21,5},{70,6},{23,7},{72,8},{25... | collective-permute-start | bytes 98312 | tf_op jit(solution)/shard_map/ppermute | solution.py:458
  42.3 6.8 %collective-permute-start.5 = (bf16[4,128,128]{2,1,0:T(8,128)(2,1)S(1)}, bf16[4,128,128]{2,1,0:T(8,128)(2,1)S(1)}, u32[]{:S(2)}, u32[]{:S(2)}) collective-permute-start(bf16[4,128,128]{2,1,0:T(8,128)(2,1)S(1)} %pad_maximum_fusion.far0), channel_id=1, source_target_pairs={{48,0},{193,1},{50,2},{195,3},{52,4},{197,5},{54,6},{199,7},{56,8}... | collective-permute-start | bytes 393224 | tf_op jit(solution)/shard_map/ppermute | solution.py:458
  43.6 6.2 %collective-permute-start.4 = (bf16[4,128,128]{2,1,0:T(8,128)(2,1)S(1)}, bf16[4,128,128]{2,1,0:T(8,128)(2,1)S(1)}, u32[]{:S(2)}, u32[]{:S(2)}) collective-permute-start(bf16[4,128,128]{2,1,0:T(8,128)(2,1)S(1)} %pad_maximum_fusion.far0), channel_id=1, source_target_pairs={{32,0},{129,1},{34,2},{131,3},{36,4},{133,5},{38,6},{135,7},{40,8}... | collective-permute-start | bytes 393224 | tf_op jit(solution)/shard_map/ppermute | solution.py:458
  46.0 3.8 %collective-permute-start.3 = (bf16[4,128,128]{2,1,0:T(8,128)(2,1)S(1)}, bf16[4,128,128]{2,1,0:T(8,128)(2,1)S(1)}, u32[]{:S(2)}, u32[]{:S(2)}) collective-permute-start(bf16[4,128,128]{2,1,0:T(8,128)(2,1)S(1)} %pad_maximum_fusion.far0), channel_id=1, source_target_pairs={{16,0},{65,1},{18,2},{67,3},{20,4},{69,5},{22,6},{71,7},{24,8},{73... | collective-permute-start | bytes 393224 | tf_op jit(solution)/shard_map/ppermute | solution.py:458
  52.9 19.0 %all-to-all-start.2 = ((bf16[16,128,128]{2,1,0:T(8,128)(2,1)}), bf16[16,128,128]{2,1,0:T(8,128)(2,1)S(1)}, u32[]{:S(2)}, u32[]{:S(2)}) async-start(bf16[16,128,128]{2,1,0:T(8,128)(2,1)} %get-tuple-element.10), calls=%async_computation.2 | async-start | bytes 1048576 | tf_op jit(solution)/shard_map/all_to_all | solution.py:438

commit v6 on v5

--- a/solution.py
+++ b/solution.py
@@ -197,8 +197,39 @@
     return op(x.reshape(-1, 8, x.shape[1]), axis=0)
 
 
+def prepare_kernel(offs_ref, kv_ref, qg_ref, stat_ref, near_s):
+    offset = entry(QG_ORDER, offs_ref[lax.axis_index("inner")])
+    weights = qg_ref[offset, :BLOCK, :].T
+    top_half = lax.broadcasted_iota(jnp.int32, weights.shape, 0) < HD
+    weights = jnp.where(top_half, weights, jnp.zeros_like(weights))
+    top8 = jnp.full((8, BLOCK), -jnp.inf, F32)
+    for c in range(SEG // CHUNK):
+        near = dot(kv_rows(kv_ref, c), weights)
+        near_s[c * CHUNK : (c + 1) * CHUNK, :] = near
+        top8 = jnp.maximum(top8, fold(near, jnp.max))
+    top = jnp.max(top8, axis=0, keepdims=True)
+    sum8 = jnp.zeros((8, BLOCK), F32)
+    for c in range(SEG // CHUNK):
+        sum8 += fold(jnp.exp(near_s[c * CHUNK : (c + 1) * CHUNK, :] - top), jnp.sum)
+    stat_ref[0:1, :] = top
+    stat_ref[1:2, :] = jnp.sum(sum8, axis=0, keepdims=True)
+
+
+def prepare(offsets, kv, qg):
+    return pl.pallas_call(
+        prepare_kernel,
+        out_shape=jax.ShapeDtypeStruct((8, BLOCK), F32),
+        in_specs=[SMEM, VMEM, VMEM],
+        out_specs=VMEM,
+        scratch_shapes=[pltpu.VMEM((SEG, BLOCK), F32)],
+        compiler_params=params(20),
+        cost_estimate=cost(10**9, 2 * 10**6),
+        name="prepare_near",
+    )(offsets, kv, qg)
+
+
 def far_kernel(
-    offs_ref, kv_ref, qg_ref, far0, far1, far2, far3, part_ref, stat_ref, near_s, far_s, ed, keys_t
+    offs_ref, qg_ref, near_ref, far0, far1, far2, far3, part_ref, stat_ref, far_s, ed
 ):
     offset = entry(QG_ORDER, offs_ref[lax.axis_index("inner")])
     place = lax.axis_index("outer")
@@ -214,24 +245,23 @@
     terms = block_terms(qg_ref[offset, BLOCK:, :])
     turned = qg_ref[offset, :BLOCK, :].T
     weights = score_weights(turned[:HD, :], turned[HD:, :])
-    top8 = jnp.full((8, BLOCK), -jnp.inf, F32)
+    near_top = near_ref[0:1, :]
+    top8 = jnp.broadcast_to(near_top, (8, BLOCK))
     for c in range(SEG // CHUNK):
         rows = slice(c * CHUNK, (c + 1) * CHUNK)
-        near = dot(kv_rows(kv_ref, c), weights[:, :BLOCK])
-        near_s[rows, :] = near
         far = dot(far_rows(c), weights)
         far_s[rows, :] = far
-        keys_t[:, rows] = far_rows(c).T[:HD, :]
-        top8 = jnp.maximum(top8, jnp.maximum(fold(near, jnp.max), fold(far[:, :BLOCK], jnp.max)))
+        top8 = jnp.maximum(top8, fold(far[:, :BLOCK], jnp.max))
     top = jnp.max(top8, axis=0, keepdims=True)
     sum8 = jnp.zeros((8, BLOCK), F32)
     for c in range(SEG // CHUNK):
         rows = slice(c * CHUNK, (c + 1) * CHUNK)
         prob = jnp.exp(far_s[rows, :BLOCK] - top)
-        sum8 += fold(prob, jnp.sum) + fold(jnp.exp(near_s[rows, :] - top), jnp.sum)
+        sum8 += fold(prob, jnp.sum)
         ed[rows, :BLOCK] = prob.astype(BF)
         ed[rows, BLOCK:] = (prob * (far_s[rows, BLOCK:] - terms)).astype(BF)
-    factor = 1.0 / jnp.sum(sum8, axis=0, keepdims=True)
+    total = jnp.sum(sum8, axis=0, keepdims=True) + near_ref[1:2, :] * jnp.exp(near_top - top)
+    factor = 1.0 / total
     second = grad_weights(turned, factor)
     query_grad = jnp.zeros((HD, BLOCK), F32)
     for c in range(SEG // CHUNK):
@@ -243,13 +273,13 @@
             step_x = b + odd * (a - b)
             owner = (place_x + step_x) % RING * RING + (place_y + a + b - step_x) % RING
             part_ref[owner] = grads[n * BLOCK : (n + 1) * BLOCK, :]
-        query_grad += dot(keys_t[:, rows], both[:, BLOCK:])
+        query_grad += dot(far_rows(c).T[:HD, :], both[:, BLOCK:])
     stat_ref[0:1, :] = top
     stat_ref[1:2, :] = factor
     stat_ref[8:, :] = query_grad * factor * (HD**-0.5)
 
 
-def far_part(offsets, kv, qg, fars):
+def far_part(offsets, qg, near_stat, fars):
     return pl.pallas_call(
         far_kernel,
         out_shape=(
@@ -259,15 +289,13 @@
         in_specs=[SMEM] + [VMEM] * 6,
         out_specs=(VMEM, VMEM),
         scratch_shapes=[
-            pltpu.VMEM((SEG, BLOCK), F32),
             pltpu.VMEM((SEG, 2 * BLOCK), F32),
             pltpu.VMEM((SEG, 2 * BLOCK), BF),
-            pltpu.VMEM((HD, SEG), BF),
         ],
         compiler_params=params(20),
         cost_estimate=cost(2 * 10**9, 2 * 10**6),
         name="far_part",
-    )(offsets, kv, qg, *fars)
+    )(offsets, qg, near_stat, *fars)
 
 
 def near_kernel(
@@ -466,7 +494,8 @@
     qg = pack_qg(queries, saved_out, out_grad)
     fars = spread(pick(offsets, kv))
     qg = exchange(qg, "inner", QG_ORDER)
-    parts, stat = far_part(offsets, kv, qg, fars)
+    near_stat = prepare(offsets, kv, qg)
+    parts, stat = far_part(offsets, qg, near_stat, fars)
     parts = exchange(parts, "outer")
     dq, sums = near_part(offsets, kv, qg, stat)
     whole = finish(offsets, dq, sums, parts)

time: 101 us -> 101 us (level)
    pallas_call x0 -> x1, Pallas kernels: none -> 1.06 us  [prepare(): pl.pallas_call(prepare_kernel, out_shape=jax.ShapeDtypeStruct((8, BLOCK),...]
    all_to_all x1, blocking collectives: 26.7 us -> 25.7 us  [exchange(): lax.all_to_all(array, axis, split_axis=0, concat_axis=0, tiled=True, axis...]
  transfers between devices with their start and end apart: 9 -> 9, of which waited for: 6 -> 4; matrix products, arithmetic and copies ran while one was open for 0% -> 0% of each run, Pallas kernels for 16% -> 17%
where the time goes in v6:
time: 101 us; the launch traced here: 100 us
  starting transfers between devices  35.8 us (35%)
  blocking collectives  25.7 us (25%)
  Pallas kernels  23.5 us (23%)
  waiting for transfers between devices  14.4 us (14%)
    all_to_all x3, starting transfers between devices, exchange(): lax.all_to_all(array, axis, split_axis=0, concat_axis=0, tiled=True, axis...  25.8 us
    all_to_all x1, blocking collectives, exchange(): lax.all_to_all(array, axis, split_axis=0, concat_axis=0, tiled=True, axis...  25.7 us
    pallas_call x1, Pallas kernels, near_part(): pl.pallas_call(near_kernel, out_shape=(jax.ShapeDtypeStruct((NB, HD, BLOC...  12.9 us
    all_to_all x3, waiting for transfers between devices, exchange(): lax.all_to_all(array, axis, split_axis=0, concat_axis=0, tiled=True, axis...  12.4 us
    ppermute x6, starting transfers between devices, send(): return lax.ppermute(array, ('outer', 'inner'), ring(step, first))  9.95 us
    pallas_call x1, Pallas kernels, far_part(): pl.pallas_call(far_kernel, out_shape=(jax.ShapeDtypeStruct((NB, BLOCK, 2...  2.86 us
    pallas_call x1, Pallas kernels, pack_qg(): pl.pallas_call(pack_qg_kernel, out_shape=jax.ShapeDtypeStruct((HEADS, QG_...  2.36 us
  transfers between devices with their start and end apart: 9, of which 4 were waited for; matrix products, arithmetic and copies ran while one was open for 0% of the time, Pallas kernels for 17%

profile of v6, /device:TPU:1, one launch (start us, length us, event | category | flops | bytes accessed | tf_op | source)
XLA Modules:
  0.0 100.1 jit_solution(13897486676029462684)
XLA Ops:
  0.6 2.0 %pack_keys_values.1 = bf16[16,128,128]{2,1,0:T(8,128)(2,1)} custom-call(bf16[128,1024]{1,0:T(8,128)(2,1)} %k_in.1, bf16[128,1024]{1,0:T(8,128)(2,1)} %v_in.1), custom_call_target="tpu_custom_call" | custom-call | flops 1000000 | bytes 1000000 | tf_op jit(solution)/shard_map/pack_keys_values/pallas_call | solution.py:98
  2.6 11.8 %all-to-all-start = ((bf16[16,128,128]{2,1,0:T(8,128)(2,1)}), bf16[16,128,128]{2,1,0:T(8,128)(2,1)S(1)}, u32[]{:S(2)}, u32[]{:S(2)}) async-start(bf16[16,128,128]{2,1,0:T(8,128)(2,1)} %pack_keys_values.1), calls=%async_computation | async-start | bytes 1048576 | tf_op jit(solution)/shard_map/all_to_all | solution.py:466
  14.4 2.4 %pack_queries_grads.1 = bf16[16,144,128]{2,1,0:T(8,128)(2,1)} custom-call(bf16[128,1024]{1,0:T(8,128)(2,1)} %q_in.1, bf16[128,1024]{1,0:T(8,128)(2,1)} %o_in.1, bf16[128,1024]{1,0:T(8,128)(2,1)} %g_in.1), custom_call_target="tpu_custom_call" | custom-call | flops 10000000 | bytes 2000000 | tf_op jit(solution)/shard_map/pack_queries_grads/pallas_call | solution.py:140
  16.8 0.0 copy-start
  16.8 10.6 %all-to-all-done.kv_ref = bf16[16,128,128]{2,1,0:T(8,128)(2,1)S(1)} async-done(((bf16[16,128,128]{2,1,0:T(8,128)(2,1)}), bf16[16,128,128]{2,1,0:T(8,128)(2,1)S(1)}, u32[]{:S(2)}, u32[]{:S(2)}) %all-to-all-start) | async-done | bytes 524320 | tf_op jit(solution)/shard_map/all_to_all | solution.py:466
  27.3 7.3 %all-to-all-start.1 = ((bf16[16,144,128]{2,1,0:T(8,128)(2,1)}), bf16[16,144,128]{2,1,0:T(8,128)(2,1)S(1)}, u32[]{:S(2)}, u32[]{:S(2)}) async-start(bf16[16,144,128]{2,1,0:T(8,128)(2,1)} %pack_queries_grads.1), calls=%async_computation.1 | async-start | bytes 1179648 | tf_op jit(solution)/shard_map/all_to_all | solution.py:466
  34.6 0.0 copy-done
  34.6 0.6 pick_block.1
  35.2 1.4 %collective-permute-start.2 = (bf16[128,128]{1,0:T(8,128)(2,1)S(1)}, bf16[128,128]{1,0:T(8,128)(2,1)S(1)}, u32[]{:S(2)}, u32[]{:S(2)}) collective-permute-start(bf16[128,128]{1,0:T(8,128)(2,1)S(1)} %pick_block.1), channel_id=1, source_target_pairs={{192,0},{49,1},{194,2},{51,3},{196,4},{53,5},{198,6},{55,7},{200,8... | collective-permute-start | bytes 98312 | tf_op jit(solution)/shard_map/ppermute | solution.py:486
  36.6 2.6 %collective-permute-start.1 = (bf16[128,128]{1,0:T(8,128)(2,1)S(1)}, bf16[128,128]{1,0:T(8,128)(2,1)S(1)}, u32[]{:S(2)}, u32[]{:S(2)}) collective-permute-start(bf16[128,128]{1,0:T(8,128)(2,1)S(1)} %pick_block.1), channel_id=1, source_target_pairs={{128,0},{33,1},{130,2},{35,3},{132,4},{37,5},{134,6},{39,7},{136,8... | collective-permute-start | bytes 98312 | tf_op jit(solution)/shard_map/ppermute | solution.py:486
  39.2 1.1 %collective-permute-start = (bf16[128,128]{1,0:T(8,128)(2,1)S(1)}, bf16[128,128]{1,0:T(8,128)(2,1)S(1)}, u32[]{:S(2)}, u32[]{:S(2)}) collective-permute-start(bf16[128,128]{1,0:T(8,128)(2,1)S(1)} %pick_block.1), channel_id=1, source_target_pairs={{64,0},{17,1},{66,2},{19,3},{68,4},{21,5},{70,6},{23,7},{72,8},{25... | collective-permute-start | bytes 98312 | tf_op jit(solution)/shard_map/ppermute | solution.py:486
  40.2 0.0 collective-permute-done.2
  40.3 0.6 collective-permute-done.1
  40.8 1.4 %collective-permute-done = bf16[128,128]{1,0:T(8,128)(2,1)S(1)} collective-permute-done((bf16[128,128]{1,0:T(8,128)(2,1)S(1)}, bf16[128,128]{1,0:T(8,128)(2,1)S(1)}, u32[]{:S(2)}, u32[]{:S(2)}) %collective-permute-start) | collective-permute-done | bytes 32800 | tf_op jit(solution)/shard_map/ppermute | solution.py:486
  42.3 1.3 %collective-permute-start.5 = (bf16[4,128,128]{2,1,0:T(8,128)(2,1)S(1)}, bf16[4,128,128]{2,1,0:T(8,128)(2,1)S(1)}, u32[]{:S(2)}, u32[]{:S(2)}) collective-permute-start(bf16[4,128,128]{2,1,0:T(8,128)(2,1)S(1)} %pad_maximum_fusion.far0), channel_id=1, source_target_pairs={{48,0},{193,1},{50,2},{195,3},{52,4},{197,5},{54,6},{199,7},{56,8}... | collective-permute-start | bytes 393224 | tf_op jit(solution)/shard_map/ppermute | solution.py:486
  43.6 2.5 %collective-permute-start.4 = (bf16[4,128,128]{2,1,0:T(8,128)(2,1)S(1)}, bf16[4,128,128]{2,1,0:T(8,128)(2,1)S(1)}, u32[]{:S(2)}, u32[]{:S(2)}) collective-permute-start(bf16[4,128,128]{2,1,0:T(8,128)(2,1)S(1)} %pad_maximum_fusion.far0), channel_id=1, source_target_pairs={{32,0},{129,1},{34,2},{131,3},{36,4},{133,5},{38,6},{135,7},{40,8}... | collective-permute-start | bytes 393224 | tf_op jit(solution)/shard_map/ppermute | solution.py:486
  46.0 1.2 %collective-permute-start.3 = (bf16[4,128,128]{2,1,0:T(8,128)(2,1)S(1)}, bf16[4,128,128]{2,1,0:T(8,128)(2,1)S(1)}, u32[]{:S(2)}, u32[]{:S(2)}) collective-permute-start(bf16[4,128,128]{2,1,0:T(8,128)(2,1)S(1)} %pad_maximum_fusion.far0), channel_id=1, source_target_pairs={{16,0},{65,1},{18,2},{67,3},{20,4},{69,5},{22,6},{71,7},{24,8},{73... | collective-permute-start | bytes 393224 | tf_op jit(solution)/shard_map/ppermute | solution.py:486
  47.2 1.9 %all-to-all-done.1.qg_ref = bf16[16,144,128]{2,1,0:T(8,128)(2,1)S(1)} async-done(((bf16[16,144,128]{2,1,0:T(8,128)(2,1)}), bf16[16,144,128]{2,1,0:T(8,128)(2,1)S(1)}, u32[]{:S(2)}, u32[]{:S(2)}) %all-to-all-start.1) | async-done | bytes 589856 | tf_op jit(solution)/shard_map/all_to_all | solution.py:466
  49.0 1.1 %prepare_near.1.near_ref = f32[8,128]{1,0:T(8,128)S(1)} custom-call(s32[16]{0:T(128)S(1)} %copy-done, bf16[16,128,128]{2,1,0:T(8,128)(2,1)S(1)} %all-to-all-done.kv_ref, bf16[16,144,128]{2,1,0:T(8,128)(2,1)S(1)} %all-to-all-done.1.qg_ref), custom_call_target="tpu_custom_call" | custom-call | flops 1000000000 | bytes 2000000 | tf_op jit(solution)/shard_map/prepare_near/pallas_call | solution.py:219
  50.1 0.0 collective-permute-done.5.far3
  50.1 0.0 collective-permute-done.4.far2
  50.1 0.0 collective-permute-done.3.far1
  50.1 2.9 %far_part.1 = (bf16[16,128,128]{2,1,0:T(8,128)(2,1)}, f32[72,128]{1,0:T(8,128)S(1)}) custom-call(s32[16]{0:T(128)S(1)} %copy-done, bf16[16,144,128]{2,1,0:T(8,128)(2,1)S(1)} %all-to-all-done.1.qg_ref, f32[8,128]{1,0:T(8,128)S(1)} %prepare_near.1.near_ref, bf16[4,128,128]{2,1,0:T(8,128)(2,1)S(1)} %pad_maximum_fusion.far0, ...), custom_call_target="tpu_custom_call" | custom-call | flops 2000000000 | bytes 2000000 | tf_op jit(solution)/shard_map/far_part/pallas_call | solution.py:283
  53.0 6.8 %all-to-all-start.2 = ((bf16[16,128,128]{2,1,0:T(8,128)(2,1)}), bf16[16,128,128]{2,1,0:T(8,128)(2,1)S(1)}, u32[]{:S(2)}, u32[]{:S(2)}) async-start(bf16[16,128,128]{2,1,0:T(8,128)(2,1)} %get-tuple-element.10), calls=%async_computation.2 | async-start | bytes 1048576 | tf_op jit(solution)/shard_map/all_to_all | solution.py:466
  59.8 12.9 %near_part.1 = (bf16[16,64,128]{2,1,0:T(8,128)(2,1)S(1)}, f32[2048,128]{1,0:T(8,128)S(1)}) custom-call(s32[16]{0:T(128)S(1)} %copy-done, bf16[16,128,128]{2,1,0:T(8,128)(2,1)S(1)} %all-to-all-done.kv_ref, bf16[16,144,128]{2,1,0:T(8,128)(2,1)S(1)} %all-to-all-done.1.qg_ref, f32[72,128]{1,0:T(8,128)S(1)} %get-tuple-element.7.stat_ref), custom_call_target="tpu_custom_call" | custom-call | flops 15000000512 | bytes 4000000 | tf_op jit(solution)/shard_map/near_part/pallas_call | solution.py:378
  72.7 0.0 all-to-all-done.2.parts_ref
  72.7 0.7 finish_picked.1
  73.4 25.7 %all_to_all.20.in_ref = bf16[16,192,128]{2,1,0:T(8,128)(2,1)S(1)} all-to-all(bf16[16,192,128]{2,1,0:T(8,128)(2,1)S(1)} %finish_picked.1), channel_id=1, replica_groups={{15,14,13,12,11,10,9,8,7,6,5,4,3,2,1,0},{31,30,29,28,27,26,25,24,23,22,..., dimensions={0} | all-to-all | bytes 1572864 | tf_op jit(solution)/shard_map/all_to_all | solution.py:466
  99.0 1.1 %unpack_heads.1 = (bf16[128,1024]{1,0:T(8,128)(2,1)}, bf16[128,1024]{1,0:T(8,128)(2,1)}, bf16[128,1024]{1,0:T(8,128)(2,1)}) custom-call(bf16[16,192,128]{2,1,0:T(8,128)(2,1)S(1)} %all_to_all.20.in_ref), custom_call_target="tpu_custom_call" | custom-call | flops 1000000 | bytes 2000000 | tf_op jit(solution)/shard_map/unpack_heads/pallas_call | solution.py:448
  (1 shorter events, 0.0 us)
Async XLA Ops:
  2.6 24.7 %all-to-all-start = ((bf16[16,128,128]{2,1,0:T(8,128)(2,1)}), bf16[16,128,128]{2,1,0:T(8,128)(2,1)S(1)}, u32[]{:S(2)}, u32[]{:S(2)}) async-start(bf16[16,128,128]{2,1,0:T(8,128)(2,1)} %pack_keys_values.1), calls=%async_computation | async-start | bytes 1048576 | tf_op jit(solution)/shard_map/all_to_all | solution.py:466
  16.8 17.9 %copy-start = (s32[16]{0:T(128)S(1)}, s32[16]{0:T(128)}, u32[]{:S(2)}) copy-start(s32[16]{0:T(128)} %offs_ref.9) | copy-start | bytes 196
  27.3 21.7 %all-to-all-start.1 = ((bf16[16,144,128]{2,1,0:T(8,128)(2,1)}), bf16[16,144,128]{2,1,0:T(8,128)(2,1)S(1)}, u32[]{:S(2)}, u32[]{:S(2)}) async-start(bf16[16,144,128]{2,1,0:T(8,128)(2,1)} %pack_queries_grads.1), calls=%async_computation.1 | async-start | bytes 1179648 | tf_op jit(solution)/shard_map/all_to_all | solution.py:466
  35.2 5.1 %collective-permute-start.2 = (bf16[128,128]{1,0:T(8,128)(2,1)S(1)}, bf16[128,128]{1,0:T(8,128)(2,1)S(1)}, u32[]{:S(2)}, u32[]{:S(2)}) collective-permute-start(bf16[128,128]{1,0:T(8,128)(2,1)S(1)} %pick_block.1), channel_id=1, source_target_pairs={{192,0},{49,1},{194,2},{51,3},{196,4},{53,5},{198,6},{55,7},{200,8... | collective-permute-start | bytes 98312 | tf_op jit(solution)/shard_map/ppermute | solution.py:486
  36.6 4.3 %collective-permute-start.1 = (bf16[128,128]{1,0:T(8,128)(2,1)S(1)}, bf16[128,128]{1,0:T(8,128)(2,1)S(1)}, u32[]{:S(2)}, u32[]{:S(2)}) collective-permute-start(bf16[128,128]{1,0:T(8,128)(2,1)S(1)} %pick_block.1), channel_id=1, source_target_pairs={{128,0},{33,1},{130,2},{35,3},{132,4},{37,5},{134,6},{39,7},{136,8... | collective-permute-start | bytes 98312 | tf_op jit(solution)/shard_map/ppermute | solution.py:486
  39.2 3.1 %collective-permute-start = (bf16[128,128]{1,0:T(8,128)(2,1)S(1)}, bf16[128,128]{1,0:T(8,128)(2,1)S(1)}, u32[]{:S(2)}, u32[]{:S(2)}) collective-permute-start(bf16[128,128]{1,0:T(8,128)(2,1)S(1)} %pick_block.1), channel_id=1, source_target_pairs={{64,0},{17,1},{66,2},{19,3},{68,4},{21,5},{70,6},{23,7},{72,8},{25... | collective-permute-start | bytes 98312 | tf_op jit(solution)/shard_map/ppermute | solution.py:486
  42.3 7.8 %collective-permute-start.5 = (bf16[4,128,128]{2,1,0:T(8,128)(2,1)S(1)}, bf16[4,128,128]{2,1,0:T(8,128)(2,1)S(1)}, u32[]{:S(2)}, u32[]{:S(2)}) collective-permute-start(bf16[4,128,128]{2,1,0:T(8,128)(2,1)S(1)} %pad_maximum_fusion.far0), channel_id=1, source_target_pairs={{48,0},{193,1},{50,2},{195,3},{52,4},{197,5},{54,6},{199,7},{56,8}... | collective-permute-start | bytes 393224 | tf_op jit(solution)/shard_map/ppermute | solution.py:486
  43.6 6.6 %collective-permute-start.4 = (bf16[4,128,128]{2,1,0:T(8,128)(2,1)S(1)}, bf16[4,128,128]{2,1,0:T(8,128)(2,1)S(1)}, u32[]{:S(2)}, u32[]{:S(2)}) collective-permute-start(bf16[4,128,128]{2,1,0:T(8,128)(2,1)S(1)} %pad_maximum_fusion.far0), channel_id=1, source_target_pairs={{32,0},{129,1},{34,2},{131,3},{36,4},{133,5},{38,6},{135,7},{40,8}... | collective-permute-start | bytes 393224 | tf_op jit(solution)/shard_map/ppermute | solution.py:486
  46.0 4.1 %collective-permute-start.3 = (bf16[4,128,128]{2,1,0:T(8,128)(2,1)S(1)}, bf16[4,128,128]{2,1,0:T(8,128)(2,1)S(1)}, u32[]{:S(2)}, u32[]{:S(2)}) collective-permute-start(bf16[4,128,128]{2,1,0:T(8,128)(2,1)S(1)} %pad_maximum_fusion.far0), channel_id=1, source_target_pairs={{16,0},{65,1},{18,2},{67,3},{20,4},{69,5},{22,6},{71,7},{24,8},{73... | collective-permute-start | bytes 393224 | tf_op jit(solution)/shard_map/ppermute | solution.py:486
  53.0 19.7 %all-to-all-start.2 = ((bf16[16,128,128]{2,1,0:T(8,128)(2,1)}), bf16[16,128,128]{2,1,0:T(8,128)(2,1)S(1)}, u32[]{:S(2)}, u32[]{:S(2)}) async-start(bf16[16,128,128]{2,1,0:T(8,128)(2,1)} %get-tuple-element.10), calls=%async_computation.2 | async-start | bytes 1048576 | tf_op jit(solution)/shard_map/all_to_all | solution.py:466
